TPU v7x, 256 devices: a whole 4x4x8 slice. The times are simulated.
256 devices in a mesh: cond: 16 (over x_lo, y, core), slab: 16 (over x_hi, z).
Axes of the slice: x: 4 (x_hi: 2, x_lo: 2; x = x_hi * 2 + x_lo), y: 4, z: 8, core: 2. Of those that a mesh axis runs over, the one named last changes fastest.
Arguments:
- features: bfloat16 [16, 32, 16, 64, 128], P('cond', 'slab'), as said below
- latent: float32 [4, 32, 1024], P(None, 'slab', 'cond'), may hold values from -6 to 6
- cond_codes: int32 [16, 8], P('cond'), may hold values from 0 to 15
- guide_codes: int32 [16], replicated, may hold values from 1 to 8
- timestep: int32 [1], replicated, may hold values from 50 to 800
- code_table: float32 [8, 16, 256], replicated, may hold values from -2.5 to 2.5
- time_weight: float32 [256, 256], replicated, may hold values from -0.375 to 0.375
- film_weight: float32 [256, 256], replicated, may hold values from -0.375 to 0.375
- conv_one: bfloat16 [3, 3, 3, 128, 128], replicated, may hold values from -0.109375 to 0.109375
- conv_two: bfloat16 [3, 3, 3, 128, 128], replicated, may hold values from -0.109375 to 0.109375
- head_weight: float32 [128, 4], replicated, may hold values from -0.5 to 0.5
Outputs:
- guided: float32 [4, 32, 1024], P(None, 'slab', 'cond')
- stepped: float32 [4, 32, 1024], P(None, 'slab', 'cond')
Inputs may be any that keep to these rules, and one draw needn't show every extreme that they name: `features`: finite values, up to about 60 in magnitude.
All inputs are finite; a program needn't handle non-finite values.
Results may differ from a plain program's by a relative error of at most 0.0026.
Values may be sent and summed in bfloat16 or wider, within the bound.
No kernel may reach another device: no remote copies, remote signals or barrier semaphores. Data moves between devices by JAX's collectives and lax.ppermute only.
A program may use at most 64 MiB of HBM per device.

v0:
```python
import math

import jax
import jax.numpy as jnp
from jax import lax
from jax.sharding import PartitionSpec as P

C = 128
GROUPS = 32
EMB = 256
LAT = 4
CODES = 16
STRIDE = 20
DEP_DEV = 2
H = 16
W = 64


def with_halo(block, sides, width):
    for axis, dim in sides:
        count = lax.axis_size(axis)
        forward = [(i, i + 1) for i in range(count - 1)]
        backward = [(target, source) for source, target in forward]
        low = lax.ppermute(
            lax.slice_in_dim(block, block.shape[dim] - width, None, axis=dim), axis, forward
        )
        high = lax.ppermute(lax.slice_in_dim(block, 0, width, axis=dim), axis, backward)
        block = jnp.concatenate([low, block, high], axis=dim)
    return block


def embed_terms(code_row, time_value, code_table, time_weight, film_weight):
    one_hot = (code_row[:, None] == jnp.arange(CODES, dtype=jnp.int32)[None, :]).astype(jnp.float32)
    code_part = jnp.einsum("jc,jce->e", one_hot, code_table, precision=lax.Precision.HIGHEST)
    half_width = EMB // 2
    frequency = jnp.exp(-math.log(10000.0) * jnp.arange(half_width, dtype=jnp.float32) / half_width)
    angles = time_value * frequency
    sinus = jnp.concatenate([jnp.cos(angles), jnp.sin(angles)])
    embedding = jax.nn.silu(
        jnp.dot(sinus, time_weight, precision=lax.Precision.HIGHEST) + code_part
    )
    return jnp.dot(embedding, film_weight, precision=lax.Precision.HIGHEST)


def group_sums(values):
    per_group = C // GROUPS
    return jnp.sum(values, axis=(0, 1, 2)).reshape(GROUPS, per_group).sum(axis=1)


def group_stats(values, members):
    per_group = C // GROUPS
    average = lax.psum(group_sums(values), "slab") / members
    centred = values - jnp.repeat(average, per_group)
    spread = lax.psum(group_sums(centred * centred), "slab") / members
    return (average, spread)


def normalize(values, average, spread):
    per_group = C // GROUPS
    return (values - jnp.repeat(average, per_group)) / jnp.sqrt(
        jnp.repeat(spread, per_group) + 1e-05
    )


def convolve(planes, weight):
    depth_out = planes.shape[0] - 2
    padded = jnp.pad(planes, ((0, 0), (1, 1), (1, 1), (0, 0)))
    summed = jnp.zeros((depth_out * H * W, C), jnp.float32)
    for depth_tap in range(3):
        for row_tap in range(3):
            columns = jnp.concatenate(
                [
                    padded[
                        depth_tap : depth_tap + depth_out,
                        row_tap : row_tap + H,
                        col_tap : col_tap + W,
                    ]
                    for col_tap in range(3)
                ],
                axis=-1,
            )
            summed = summed + jnp.dot(
                columns.reshape(-1, 3 * C),
                weight[depth_tap, row_tap].reshape(3 * C, C),
                preferred_element_type=jnp.float32,
            )
    return summed.reshape(depth_out, H, W, C)


def plane_rims(values):
    return with_halo(values, (("slab", 0),), 1)


def plan(step_value):
    frac = (step_value / 1000.0 + 0.008) / 1.008
    return jnp.cos(frac * math.pi / 2.0) ** 2


def per_device(
    features,
    latent,
    cond_codes,
    guide_codes,
    timestep,
    code_table,
    time_weight,
    film_weight,
    conv_one,
    conv_two,
    head_weight,
):
    slab_count = lax.axis_size("slab")
    depth_all = DEP_DEV * slab_count
    members = float(depth_all * H * W * (C // GROUPS))
    time_value = timestep[0].astype(jnp.float32)
    modulation = embed_terms(cond_codes[0], time_value, code_table, time_weight, film_weight)
    stretch = modulation[:C]
    offset = modulation[C:]
    base = features[0].astype(jnp.float32)
    average, spread = group_stats(base, members)
    first_act = jax.nn.silu(normalize(base, average, spread)).astype(jnp.bfloat16)
    first_conv = convolve(plane_rims(first_act), conv_one)
    average_two, spread_two = group_stats(first_conv, members)
    second_act = jax.nn.silu(
        normalize(first_conv, average_two, spread_two) * (1.0 + stretch) + offset
    ).astype(jnp.bfloat16)
    second_conv = convolve(plane_rims(second_act), conv_two)
    output = base + second_conv
    noise_pred = jnp.einsum(
        "dhwc,cl->ldhw", output, head_weight, precision=lax.Precision.HIGHEST
    ).reshape(LAT, DEP_DEV, H * W)
    term_count = lax.axis_size("cond")
    term_index = lax.axis_index("cond")
    term_weights = guide_codes.astype(jnp.float32) / 16.0
    others = jnp.sum(term_weights[1:])
    term_weights = term_weights.at[0].set(1.0 - others)
    own_weight = jnp.sum(
        jnp.where(jnp.arange(term_count, dtype=jnp.int32) == term_index, term_weights, 0.0)
    )
    weighted = own_weight * noise_pred
    share_width = H * W // term_count
    summed = lax.psum(weighted, "cond")
    guided = lax.dynamic_slice_in_dim(summed, term_index * share_width, share_width, 2)
    now_bar = plan(time_value)
    next_bar = plan(time_value - STRIDE)
    clean = (latent - jnp.sqrt(1.0 - now_bar) * guided) / jnp.sqrt(now_bar)
    stepped = jnp.sqrt(next_bar) * clean + jnp.sqrt(1.0 - next_bar) * guided
    return (guided, stepped)


def solution(mesh):
    placed = (
        P("cond", "slab", None, None, None),
        P(None, "slab", "cond"),
        P("cond", None),
        P(),
        P(),
        P(),
        P(),
        P(),
        P(),
        P(),
        P(),
    )
    return jax.shard_map(
        per_device,
        mesh=mesh,
        in_specs=placed,
        out_specs=(P(None, "slab", "cond"), P(None, "slab", "cond")),
        check_vma=False,
    )
```

profile of v0, /device:TPU:6, one launch (start us, length us, event | category | flops | bytes accessed | tf_op | source)
XLA Modules:
  0.0 273.5 jit_solution(15786523032038556497)
XLA Ops:
  0.7 1.4 convert_reduce_fusion
  2.3 43.3 %psum.35 = f32[32]{0:T(128)S(1)} all-reduce(f32[32]{0:T(128)S(1)} %reduce_sum.93), channel_id=1, replica_groups=mesh['cond'=16,'slab'=16] {'slab'}, use_global_device_ids=true, to_apply=%region_4.5 | all-reduce | flops 32 | bytes 256 | tf_op jit(solution)/shard_map/psum | solution.py:52
  45.8 1.3 fusion.24
  47.3 36.8 %psum.36 = f32[32]{0:T(128)S(1)} all-reduce(f32[32]{0:T(128)S(1)} %reduce_sum.95), channel_id=1, replica_groups=mesh['cond'=16,'slab'=16] {'slab'}, use_global_device_ids=true, to_apply=%region_7.8 | all-reduce | flops 32 | bytes 256 | tf_op jit(solution)/shard_map/psum | solution.py:54
  84.3 1.4 multiply_convert_fusion.1
  85.7 3.9 %collective-permute-start = (bf16[1,16,64,128]{3,2,1,0:T(8,128)(2,1)S(1)}, bf16[1,16,64,128]{3,2,1,0:T(8,128)(2,1)S(1)}, u32[]{:S(2)}, u32[]{:S(2)}) collective-permute-start(bf16[1,16,64,128]{3,2,1,0:T(8,128)(2,1)S(1)} %get-tuple-element.90), channel_id=1, source_target_pairs={{0,1},{1,2},{2,3},{3,4},{4,5},{5,6},{6,7},{7,8},{8,9},{9,10},{10,1... | collective-permute-start | bytes 786440 | tf_op jit(solution)/shard_map/ppermute | solution.py:24
  89.6 5.5 %collective-permute-start.1 = (bf16[1,16,64,128]{3,2,1,0:T(8,128)(2,1)S(1)}, bf16[1,16,64,128]{3,2,1,0:T(8,128)(2,1)S(1)}, u32[]{:S(2)}, u32[]{:S(2)}) collective-permute-start(bf16[1,16,64,128]{3,2,1,0:T(8,128)(2,1)S(1)} %get-tuple-element.91), channel_id=1, source_target_pairs={{1,0},{2,1},{3,2},{4,3},{5,4},{6,5},{7,6},{8,7},{9,8},{10,9},{11,1... | collective-permute-start | bytes 786440 | tf_op jit(solution)/shard_map/ppermute | solution.py:27
  96.7 0.7 slice_reduce_fusion
  98.2 0.9 collective-permute-done.1
  99.6 2.8 %fusion.35 = (bf16[2,16,64,128]{3,2,1,0:T(8,128)(2,1)S(1)}, bf16[2,16,64,128]{3,2,1,0:T(8,128)(2,1)S(1)}, bf16[2,16,64,128]{3,2,1,0:T(8,128)(2,1)S(1)}, bf16[2,1...) fusion(bf16[4,18,66,128]{3,2,1,0:T(8,128)(2,1)S(1)} %fusion.18), kind=kLoop, calls=%fused_computation.95 | loop fusion | bytes 19922944 | tf_op jit(solution)/shard_map/slice | solution.py:73
  104.0 0.7 fusion.8
  104.8 0.6 convolution_add_fusion.15
  105.9 0.6 convolution_add_fusion.14
  106.5 0.6 convolution_add_fusion.13
  109.3 0.6 convolution_add_fusion.9
  109.9 0.7 fusion.41
  110.8 42.7 %psum.37 = f32[32]{0:T(128)S(1)} all-reduce(f32[32]{0:T(128)S(1)} %reduce_sum.97), channel_id=1, replica_groups=mesh['cond'=16,'slab'=16] {'slab'}, use_global_device_ids=true, to_apply=%region_10.11 | all-reduce | flops 32 | bytes 256 | tf_op jit(solution)/shard_map/psum | solution.py:52
  154.2 36.8 %psum.38 = f32[32]{0:T(128)S(1)} all-reduce(f32[32]{0:T(128)S(1)} %reduce_sum.99), channel_id=1, replica_groups=mesh['cond'=16,'slab'=16] {'slab'}, use_global_device_ids=true, to_apply=%region_13.14 | all-reduce | flops 32 | bytes 256 | tf_op jit(solution)/shard_map/psum | solution.py:54
  191.6 4.1 %collective-permute-start.2 = (bf16[1,16,64,128]{3,2,1,0:T(8,128)(2,1)S(1)}, bf16[1,16,64,128]{3,2,1,0:T(8,128)(2,1)S(1)}, u32[]{:S(2)}, u32[]{:S(2)}) collective-permute-start(bf16[1,16,64,128]{3,2,1,0:T(8,128)(2,1)S(1)} %get-tuple-element.85), channel_id=1, source_target_pairs={{0,1},{1,2},{2,3},{3,4},{4,5},{5,6},{6,7},{7,8},{8,9},{9,10},{10,1... | collective-permute-start | bytes 786440 | tf_op jit(solution)/shard_map/ppermute | solution.py:24
  195.7 5.5 %collective-permute-start.3 = (bf16[1,16,64,128]{3,2,1,0:T(8,128)(2,1)S(1)}, bf16[1,16,64,128]{3,2,1,0:T(8,128)(2,1)S(1)}, u32[]{:S(2)}, u32[]{:S(2)}) collective-permute-start(bf16[1,16,64,128]{3,2,1,0:T(8,128)(2,1)S(1)} %get-tuple-element.86), channel_id=1, source_target_pairs={{1,0},{2,1},{3,2},{4,3},{5,4},{6,5},{7,6},{8,7},{9,8},{10,9},{11,1... | collective-permute-start | bytes 786440 | tf_op jit(solution)/shard_map/ppermute | solution.py:27
  201.2 0.6 fusion.30
  202.3 1.2 collective-permute-done.2
  203.5 1.5 collective-permute-done.3
  205.4 2.5 fusion.33
  210.6 0.8 fusion.4
  211.4 0.6 convolution_add_fusion.7
  212.0 0.6 convolution_add_fusion.6
  212.6 0.6 convolution_add_fusion.5
  213.2 0.6 convolution_add_fusion.4
  216.6 3.2 %fusion.23 = f32[4,2,16,64]{3,0,2,1:T(4,128)S(1)} fusion(f32[2,16,64,128]{3,2,1,0:T(8,128)S(1)} %bitcast.132, bf16[1,2,16,64,128]{4,3,2,1,0:T(8,128)(2,1)S(1)} %copy-done.2, f32[]{:T(128)} %fusion.30, f32[128,4]{0,1:T(4,128)S(1)} %copy-done.8), kind=kOutput, calls=%fused_computation.66 | convolution fusion | flops 13115392 | bytes 1607684 | tf_op jit(solution)/shard_map/dhwc,cl->ldhw/dot_general | solution.py:129
  219.9 52.9 %psum.39 = f32[4,2,1024]{2,1,0:T(2,128)S(1)} all-reduce(f32[4,2,1024]{2,1,0:T(2,128)S(1)} %mul.81), channel_id=1, replica_groups=mesh['cond'=16,'slab'=16] {'cond'}, use_global_device_ids=true, to_apply=%region_14.15 | all-reduce | flops 8192 | bytes 65536 | tf_op jit(solution)/shard_map/psum | solution.py:142
  272.8 0.7 multiply_add_fusion
  (83 shorter events, 14.0 us)
Async XLA Ops:
  0.6 95.4 %copy-start = (f32[256,256]{1,0:T(8,128)S(1)}, f32[256,256]{1,0:T(8,128)}, u32[]{:S(2)}) copy-start(f32[256,256]{1,0:T(8,128)} %param.19) | copy-start | bytes 786436
  0.6 95.3 %copy-start.9 = (s32[1,8]{1,0:T(1,128)S(1)}, s32[1,8]{1,0:T(1,128)}, u32[]{:S(2)}) copy-start(s32[1,8]{1,0:T(1,128)} %param.15) | copy-start | bytes 100
  2.0 94.2 %copy-start.6 = (f32[8,16,256]{2,1,0:T(8,128)S(1)}, f32[8,16,256]{2,1,0:T(8,128)}, u32[]{:S(2)}) copy-start(f32[8,16,256]{2,1,0:T(8,128)} %param.18) | copy-start | bytes 393220
  45.7 50.8 %copy-start.5 = (f32[256,256]{1,0:T(8,128)S(1)}, f32[256,256]{1,0:T(8,128)}, u32[]{:S(2)}) copy-start(f32[256,256]{1,0:T(8,128)} %param.20) | copy-start | bytes 786436
  45.8 50.9 %copy-start.10 = (s32[16]{0:T(128)S(1)}, s32[16]{0:T(128)}, u32[]{:S(2)}) copy-start(s32[16]{0:T(128)} %param.16) | copy-start | bytes 196
  47.1 51.0 %copy-start.3 = (bf16[3,3,3,128,128]{4,3,2,1,0:T(8,128)(2,1)S(1)}, bf16[3,3,3,128,128]{4,3,2,1,0:T(8,128)(2,1)}, u32[]{:S(2)}) copy-start(bf16[3,3,3,128,128]{4,3,2,1,0:T(8,128)(2,1)} %param.21) | copy-start | bytes 2654212
  85.7 12.4 %collective-permute-start = (bf16[1,16,64,128]{3,2,1,0:T(8,128)(2,1)S(1)}, bf16[1,16,64,128]{3,2,1,0:T(8,128)(2,1)S(1)}, u32[]{:S(2)}, u32[]{:S(2)}) collective-permute-start(bf16[1,16,64,128]{3,2,1,0:T(8,128)(2,1)S(1)} %get-tuple-element.90), channel_id=1, source_target_pairs={{0,1},{1,2},{2,3},{3,4},{4,5},{5,6},{6,7},{7,8},{8,9},{9,10},{10,1... | collective-permute-start | bytes 786440 | tf_op jit(solution)/shard_map/ppermute | solution.py:24
  89.6 9.4 %collective-permute-start.1 = (bf16[1,16,64,128]{3,2,1,0:T(8,128)(2,1)S(1)}, bf16[1,16,64,128]{3,2,1,0:T(8,128)(2,1)S(1)}, u32[]{:S(2)}, u32[]{:S(2)}) collective-permute-start(bf16[1,16,64,128]{3,2,1,0:T(8,128)(2,1)S(1)} %get-tuple-element.91), channel_id=1, source_target_pairs={{1,0},{2,1},{3,2},{4,3},{5,4},{6,5},{7,6},{8,7},{9,8},{10,9},{11,1... | collective-permute-start | bytes 786440 | tf_op jit(solution)/shard_map/ppermute | solution.py:27
  154.0 48.2 %copy-start.4 = (bf16[3,3,3,128,128]{4,3,2,1,0:T(8,128)(2,1)S(1)}, bf16[3,3,3,128,128]{4,3,2,1,0:T(8,128)(2,1)}, u32[]{:S(2)}) copy-start(bf16[3,3,3,128,128]{4,3,2,1,0:T(8,128)(2,1)} %param.22) | copy-start | bytes 2654212
  191.6 11.9 %collective-permute-start.2 = (bf16[1,16,64,128]{3,2,1,0:T(8,128)(2,1)S(1)}, bf16[1,16,64,128]{3,2,1,0:T(8,128)(2,1)S(1)}, u32[]{:S(2)}, u32[]{:S(2)}) collective-permute-start(bf16[1,16,64,128]{3,2,1,0:T(8,128)(2,1)S(1)} %get-tuple-element.85), channel_id=1, source_target_pairs={{0,1},{1,2},{2,3},{3,4},{4,5},{5,6},{6,7},{7,8},{8,9},{9,10},{10,1... | collective-permute-start | bytes 786440 | tf_op jit(solution)/shard_map/ppermute | solution.py:24
  195.7 9.2 %collective-permute-start.3 = (bf16[1,16,64,128]{3,2,1,0:T(8,128)(2,1)S(1)}, bf16[1,16,64,128]{3,2,1,0:T(8,128)(2,1)S(1)}, u32[]{:S(2)}, u32[]{:S(2)}) collective-permute-start(bf16[1,16,64,128]{3,2,1,0:T(8,128)(2,1)S(1)} %get-tuple-element.86), channel_id=1, source_target_pairs={{1,0},{2,1},{3,2},{4,3},{5,4},{6,5},{7,6},{8,7},{9,8},{10,9},{11,1... | collective-permute-start | bytes 786440 | tf_op jit(solution)/shard_map/ppermute | solution.py:27
  215.5 1.0 copy-start.2
  215.5 1.0 copy-start.8
  215.5 57.9 %copy-start.1 = (f32[256,256]{1,0:T(8,128)S(1)}, f32[256,256]{1,0:T(8,128)}, u32[]{:S(2)}) copy-start(f32[256,256]{1,0:T(8,128)} %param.19) | copy-start | bytes 786436
  216.1 56.7 %copy-start.7 = (f32[4,2,64]{2,1,0:T(2,128)S(1)}, f32[4,2,64]{2,1,0:T(2,128)}, u32[]{:S(2)}) copy-start(f32[4,2,64]{2,1,0:T(2,128)} %param.14) | copy-start | bytes 6148
where the time goes:
time: 274 us; the launch traced here: 273 us
  blocking collectives  213 us (78%)
  starting transfers between devices  19.1 us (7%)
  matrix products  14.3 us (5%)
  other arithmetic  12.7 us (5%)
  local copies, waits for them, and re-layouts  8.4 us (3%)
  waiting for transfers between devices  3.58 us (1%)
  between operations  2.82 us (1%)
    psum x2, blocking collectives, group_stats(): average = lax.psum(group_sums(values), 'slab') / members  86 us
    psum x2, blocking collectives, group_stats(): spread = lax.psum(group_sums(centred * centred), 'slab') / members  73.6 us
    psum x1, blocking collectives, per_device(): summed = lax.psum(weighted, 'cond')  52.9 us
    ppermute x2, starting transfers between devices, with_halo(): lax.ppermute(lax.slice_in_dim(block, 0, width, axis=dim), axis, backward)  11 us
    dot_general x18, matrix products, convolve(): jnp.dot(columns.reshape(-1, 3 * C), weight[depth_tap, row_tap].reshape(3...  10.5 us
    ppermute x2, starting transfers between devices, with_halo(): lax.ppermute(lax.slice_in_dim(block, block.shape[dim] - width, None, axis...  8.05 us
    slice x4, local copies, waits for them, and re-layouts, convolve(): padded[depth_tap:depth_tap + depth_out, row_tap:row_tap + H, col_tap:col_...  6.51 us
  transfers between devices with their start and end apart: 4, of which 3 were waited for; matrix products, arithmetic and copies ran while one was open for 1% of the time, Pallas kernels for 0%

commit v1 on v0

--- a/solution.py
+++ b/solution.py
@@ -42,16 +42,26 @@
     return jnp.dot(embedding, film_weight, precision=lax.Precision.HIGHEST)
 
 
-def group_sums(values):
-    per_group = C // GROUPS
-    return jnp.sum(values, axis=(0, 1, 2)).reshape(GROUPS, per_group).sum(axis=1)
+def spread_out(values):
+    return lax.all_to_all(
+        jnp.broadcast_to(values[None], (lax.axis_size("slab"),) + values.shape), "slab", 0, 0
+    )
+
+
+def fold(values):
+    return values.reshape(values.shape[:-1] + (GROUPS, C // GROUPS)).sum(axis=-1)
 
 
 def group_stats(values, members):
     per_group = C // GROUPS
-    average = lax.psum(group_sums(values), "slab") / members
-    centred = values - jnp.repeat(average, per_group)
-    spread = lax.psum(group_sums(centred * centred), "slab") / members
+    cells = float(values.shape[0] * values.shape[1] * values.shape[2])
+    own_sum = jnp.sum(values, axis=(0, 1, 2))
+    centred = values - own_sum / cells
+    own_square = jnp.sum(centred * centred, axis=(0, 1, 2))
+    every = spread_out(jnp.stack([own_sum, own_square]))
+    average = fold(every[:, 0].sum(axis=0)) / members
+    apart = every[:, 0] / cells - jnp.repeat(average, per_group)
+    spread = fold((every[:, 1] + cells * apart * apart).sum(axis=0)) / members
     return (average, spread)
 
 
@@ -118,8 +128,13 @@
     offset = modulation[C:]
     base = features[0].astype(jnp.float32)
     average, spread = group_stats(base, members)
-    first_act = jax.nn.silu(normalize(base, average, spread)).astype(jnp.bfloat16)
-    first_conv = convolve(plane_rims(first_act), conv_one)
+    rims = plane_rims(features[0])
+    slab_index = lax.axis_index("slab")
+    depth_at = slab_index * DEP_DEV - 1 + jnp.arange(DEP_DEV + 2)
+    inside = ((depth_at >= 0) & (depth_at < depth_all))[:, None, None, None]
+    first_act = jax.nn.silu(normalize(rims.astype(jnp.float32), average, spread))
+    first_act = jnp.where(inside, first_act, 0.0).astype(jnp.bfloat16)
+    first_conv = convolve(first_act, conv_one)
     average_two, spread_two = group_stats(first_conv, members)
     second_act = jax.nn.silu(
         normalize(first_conv, average_two, spread_two) * (1.0 + stretch) + offset
@@ -139,8 +154,8 @@
     )
     weighted = own_weight * noise_pred
     share_width = H * W // term_count
-    summed = lax.psum(weighted, "cond")
-    guided = lax.dynamic_slice_in_dim(summed, term_index * share_width, share_width, 2)
+    pieces = weighted.reshape(LAT, DEP_DEV, term_count, share_width).transpose(2, 0, 1, 3)
+    guided = lax.all_to_all(pieces, "cond", 0, 0).sum(axis=0)
     now_bar = plan(time_value)
     next_bar = plan(time_value - STRIDE)
     clean = (latent - jnp.sqrt(1.0 - now_bar) * guided) / jnp.sqrt(now_bar)

time: 274 us -> 107 us (0.39)
  the two profiles are of different devices: /device:TPU:6 before, /device:TPU:1 now
where the time goes in v1:
time: 107 us; the launch traced here: 106 us
  starting transfers between devices  39.1 us (37%)
  waiting for transfers between devices  22.6 us (21%)
  local copies, waits for them, and re-layouts  15.3 us (14%)
  matrix products  14.4 us (13%)
  other arithmetic  11.8 us (11%)
  between operations  2.92 us (3%)
    all_to_all x2, starting transfers between devices, spread_out(): lax.all_to_all(jnp.broadcast_to(values[None], (lax.axis_size('slab'),) +...  20.9 us
    dot_general x18, matrix products, convolve(): jnp.dot(columns.reshape(-1, 3 * C), weight[depth_tap, row_tap].reshape(3...  10.6 us
    all_to_all x1, starting transfers between devices, per_device(): guided = lax.all_to_all(pieces, 'cond', 0, 0).sum(axis=0)  9.8 us
    slice x4, local copies, waits for them, and re-layouts, convolve(): padded[depth_tap:depth_tap + depth_out, row_tap:row_tap + H, col_tap:col_...  8.16 us
    all_to_all x2, waiting for transfers between devices, spread_out(): lax.all_to_all(jnp.broadcast_to(values[None], (lax.axis_size('slab'),) +...  8.05 us
    ppermute x2, waiting for transfers between devices, with_halo(): lax.ppermute(lax.slice_in_dim(block, 0, width, axis=dim), axis, backward)  7.57 us
    ppermute x2, starting transfers between devices, with_halo(): lax.ppermute(lax.slice_in_dim(block, block.shape[dim] - width, None, axis...  5.82 us
    all_to_all x1, waiting for transfers between devices, per_device(): guided = lax.all_to_all(pieces, 'cond', 0, 0).sum(axis=0)  5.47 us
  transfers between devices with their start and end apart: 7, of which 7 were waited for; matrix products, arithmetic and copies ran while one was open for 5% of the time, Pallas kernels for 0%

profile of v1, /device:TPU:1, one launch (start us, length us, event | category | flops | bytes accessed | tf_op | source)
XLA Modules:
  0.0 106.1 jit_solution(3308591265087213950)
XLA Ops:
  0.7 1.4 %convert_reduce_fusion = f32[128]{0:T(128)S(1)} fusion(bf16[1,2,16,64,128]{4,3,2,1,0:T(8,128)(2,1)} %param.13), kind=kLoop, calls=%fused_computation.48 | loop fusion | flops 524160 | bytes 524800 | tf_op jit(solution)/shard_map/reduce_sum | solution.py:58
  2.1 1.3 %fusion.12 = f32[128]{0:T(128)S(1)} fusion(f32[128]{0:T(128)S(1)} %broadcast_multiply_fusion.3, bf16[1,2,16,64,128]{4,3,2,1,0:T(8,128)(2,1)} %param.13), kind=kLoop, calls=%fused_computation.57 | loop fusion | flops 1048448 | bytes 525312 | tf_op jit(solution)/shard_map/reduce_sum | solution.py:60
  3.4 0.6 broadcast_in_dim.29
  4.0 11.7 %all-to-all-start = ((f32[16,2,128]{2,1,0:T(2,128)}), f32[16,2,128]{2,1,0:T(2,128)S(1)}, u32[]{:S(2)}, u32[]{:S(2)}) async-start(f32[16,2,128]{2,1,0:T(2,128)} %broadcast_in_dim.29), calls=%async_computation | async-start | bytes 32768 | tf_op jit(solution)/shard_map/all_to_all | solution.py:46
  15.8 1.9 %slice_bitcast_fusion.1 = (bf16[1,16,64,128]{3,2,1,0:T(8,128)(2,1)}, bf16[1,16,64,128]{3,2,1,0:T(8,128)(2,1)}) fusion(bf16[1,2,16,64,128]{4,3,2,1,0:T(8,128)(2,1)} %param.13), kind=kLoop, calls=%fused_computation.85 | loop fusion | bytes 1048576 | tf_op jit(solution)/shard_map/slice | solution.py:25
  17.7 3.4 %collective-permute-start = (bf16[1,16,64,128]{3,2,1,0:T(8,128)(2,1)}, bf16[1,16,64,128]{3,2,1,0:T(8,128)(2,1)S(1)}, u32[]{:S(2)}, u32[]{:S(2)}) collective-permute-start(bf16[1,16,64,128]{3,2,1,0:T(8,128)(2,1)} %get-tuple-element.92), channel_id=1, source_target_pairs={{0,1},{1,2},{2,3},{3,4},{4,5},{5,6},{6,7},{7,8},{8,9},{9,10},{10,1... | collective-permute-start | bytes 786440 | tf_op jit(solution)/shard_map/ppermute | solution.py:24
  21.1 1.3 %collective-permute-start.1 = (bf16[1,16,64,128]{3,2,1,0:T(8,128)(2,1)}, bf16[1,16,64,128]{3,2,1,0:T(8,128)(2,1)S(1)}, u32[]{:S(2)}, u32[]{:S(2)}) collective-permute-start(bf16[1,16,64,128]{3,2,1,0:T(8,128)(2,1)} %get-tuple-element.93), channel_id=1, source_target_pairs={{1,0},{2,1},{3,2},{4,3},{5,4},{6,5},{7,6},{8,7},{9,8},{10,9},{11,1... | collective-permute-start | bytes 786440 | tf_op jit(solution)/shard_map/ppermute | solution.py:27
  25.7 3.7 %collective-permute-done.1 = bf16[1,16,64,128]{3,2,1,0:T(8,128)(2,1)S(1)} collective-permute-done((bf16[1,16,64,128]{3,2,1,0:T(8,128)(2,1)}, bf16[1,16,64,128]{3,2,1,0:T(8,128)(2,1)S(1)}, u32[]{:S(2)}, u32[]{:S(2)}) %collective-permute-start.1) | collective-permute-done | bytes 262176 | tf_op jit(solution)/shard_map/ppermute | solution.py:27
  29.5 0.7 select_convert_fusion
  30.2 3.8 %pad_slice_fusion.2 = (bf16[2,16,64,128]{3,2,1,0:T(8,128)(2,1)S(1)}, bf16[2,16,64,128]{3,2,1,0:T(8,128)(2,1)S(1)}, bf16[2,16,64,128]{3,2,1,0:T(8,128)(2,1)S(1)},...) fusion(bf16[4,16,64,128]{3,2,1,0:T(8,128)(2,1)S(1)} %select_con, ...), kind=kLoop, calls=%fused_computation.62 | loop fusion | bytes 11010048 | tf_op jit(solution)/shard_map/slice | solution.py:83
  34.0 1.0 pad_slice_fusion.1
  36.1 0.6 convolution_add_fusion.15
  42.0 0.7 fusion.33
  43.0 0.6 broadcast_in_dim.56
  43.6 9.2 %all-to-all-start.1 = ((f32[16,2,128]{2,1,0:T(2,128)}), f32[16,2,128]{2,1,0:T(2,128)S(1)}, u32[]{:S(2)}, u32[]{:S(2)}) async-start(f32[16,2,128]{2,1,0:T(2,128)} %broadcast_in_dim.56), calls=%async_computation.1 | async-start | bytes 32768 | tf_op jit(solution)/shard_map/all_to_all | solution.py:46
  52.8 0.7 slice_reduce_fusion
  54.2 7.5 %all-to-all-done.1 = f32[16,2,128]{2,1,0:T(2,128)S(1)} async-done(((f32[16,2,128]{2,1,0:T(2,128)}), f32[16,2,128]{2,1,0:T(2,128)S(1)}, u32[]{:S(2)}, u32[]{:S(2)}) %all-to-all-start.1) | async-done | bytes 16416 | tf_op jit(solution)/shard_map/all_to_all | solution.py:46
  63.0 2.4 %collective-permute-start.2 = (bf16[1,16,64,128]{3,2,1,0:T(8,128)(2,1)S(1)}, bf16[1,16,64,128]{3,2,1,0:T(8,128)(2,1)S(1)}, u32[]{:S(2)}, u32[]{:S(2)}) collective-permute-start(bf16[1,16,64,128]{3,2,1,0:T(8,128)(2,1)S(1)} %get-tuple-element.90), channel_id=1, source_target_pairs={{0,1},{1,2},{2,3},{3,4},{4,5},{5,6},{6,7},{7,8},{8,9},{9,10},{10,1... | collective-permute-start | bytes 786440 | tf_op jit(solution)/shard_map/ppermute | solution.py:24
  65.4 1.3 %collective-permute-start.3 = (bf16[1,16,64,128]{3,2,1,0:T(8,128)(2,1)S(1)}, bf16[1,16,64,128]{3,2,1,0:T(8,128)(2,1)S(1)}, u32[]{:S(2)}, u32[]{:S(2)}) collective-permute-start(bf16[1,16,64,128]{3,2,1,0:T(8,128)(2,1)S(1)} %get-tuple-element.91), channel_id=1, source_target_pairs={{1,0},{2,1},{3,2},{4,3},{5,4},{6,5},{7,6},{8,7},{9,8},{10,9},{11,1... | collective-permute-start | bytes 786440 | tf_op jit(solution)/shard_map/ppermute | solution.py:27
  66.7 0.6 fusion.22
  67.4 1.3 %collective-permute-done.2 = bf16[1,16,64,128]{3,2,1,0:T(8,128)(2,1)S(1)} collective-permute-done((bf16[1,16,64,128]{3,2,1,0:T(8,128)(2,1)S(1)}, bf16[1,16,64,128]{3,2,1,0:T(8,128)(2,1)S(1)}, u32[]{:S(2)}, u32[]{:S(2)}) %collective-permute-start.2) | collective-permute-done | bytes 262176 | tf_op jit(solution)/shard_map/ppermute | solution.py:24
  68.7 3.8 %collective-permute-done.3 = bf16[1,16,64,128]{3,2,1,0:T(8,128)(2,1)S(1)} collective-permute-done((bf16[1,16,64,128]{3,2,1,0:T(8,128)(2,1)S(1)}, bf16[1,16,64,128]{3,2,1,0:T(8,128)(2,1)S(1)}, u32[]{:S(2)}, u32[]{:S(2)}) %collective-permute-start.3) | collective-permute-done | bytes 262176 | tf_op jit(solution)/shard_map/ppermute | solution.py:27
  73.0 2.8 %fusion.26 = (bf16[2,16,64,128]{3,2,1,0:T(8,128)(2,1)S(1)}, bf16[2,16,64,128]{3,2,1,0:T(8,128)(2,1)S(1)}, bf16[2,16,64,128]{3,2,1,0:T(8,128)(2,1)S(1)}, bf16[2,1...) fusion(bf16[4,18,66,128]{3,2,1,0:T(8,128)(2,1)S(1)} %select_max, ...), kind=kLoop, calls=%fused_computation.123 | loop fusion | bytes 19922944 | tf_op jit(solution)/shard_map/slice | solution.py:83
  78.4 0.8 fusion.4
  80.3 0.6 convolution_add_fusion.5
  84.0 3.2 %fusion.10 = f32[16,4,2,64]{3,1,0,2:T(4,128)S(1)} fusion(f32[2,16,64,128]{3,2,1,0:T(8,128)S(1)} %bitcast.150, f32[]{:T(128)} %fusion.22, f32[128,4]{0,1:T(4,128)S(1)} %copy-done.8, bf16[1,2,16,64,128]{4,3,2,1,0:T(8,128)(2,1)S(1)} %copy-done.2), kind=kOutput, calls=%fused_computation.55 | convolution fusion | flops 13115392 | bytes 1607684 | tf_op jit(solution)/shard_map/dhwc,cl->ldhw/dot_general | solution.py:144
  87.2 0.7 reshape.184
  87.9 9.8 %all-to-all-start.2 = ((f32[16,1,512]{2,1,0:T(1,128)}), f32[16,1,512]{2,1,0:T(1,128)S(1)}, u32[]{:S(2)}, u32[]{:S(2)}) async-start(f32[16,1,512]{2,1,0:T(1,128)} %reshape.184), calls=%async_computation.2 | async-start | bytes 65536 | tf_op jit(solution)/shard_map/all_to_all | solution.py:158
  98.0 5.5 %all-to-all-done.2 = f32[16,1,512]{2,1,0:T(1,128)S(1)} async-done(((f32[16,1,512]{2,1,0:T(1,128)}), f32[16,1,512]{2,1,0:T(1,128)S(1)}, u32[]{:S(2)}, u32[]{:S(2)}) %all-to-all-start.2) | async-done | bytes 32800 | tf_op jit(solution)/shard_map/all_to_all | solution.py:158
  104.0 0.7 reduce.6
  104.8 0.6 copy.27
  105.5 0.6 copy.28
  (103 shorter events, 18.3 us)
Async XLA Ops:
  0.6 22.7 %copy-start = (f32[256,256]{1,0:T(8,128)S(1)}, f32[256,256]{1,0:T(8,128)}, u32[]{:S(2)}) copy-start(f32[256,256]{1,0:T(8,128)} %param.19) | copy-start | bytes 786436
  0.6 21.7 %copy-start.3 = (bf16[3,3,3,128,128]{4,3,2,1,0:T(8,128)(2,1)S(1)}, bf16[3,3,3,128,128]{4,3,2,1,0:T(8,128)(2,1)}, u32[]{:S(2)}) copy-start(bf16[3,3,3,128,128]{4,3,2,1,0:T(8,128)(2,1)} %param.21) | copy-start | bytes 2654212
  3.4 19.8 %copy-start.9 = (s32[1,8]{1,0:T(1,128)S(1)}, s32[1,8]{1,0:T(1,128)}, u32[]{:S(2)}) copy-start(s32[1,8]{1,0:T(1,128)} %param.15) | copy-start | bytes 100
  4.0 19.5 %copy-start.6 = (f32[8,16,256]{2,1,0:T(8,128)S(1)}, f32[8,16,256]{2,1,0:T(8,128)}, u32[]{:S(2)}) copy-start(f32[8,16,256]{2,1,0:T(8,128)} %param.18) | copy-start | bytes 393220
  4.0 20.6 %all-to-all-start = ((f32[16,2,128]{2,1,0:T(2,128)}), f32[16,2,128]{2,1,0:T(2,128)S(1)}, u32[]{:S(2)}, u32[]{:S(2)}) async-start(f32[16,2,128]{2,1,0:T(2,128)} %broadcast_in_dim.29), calls=%async_computation | async-start | bytes 32768 | tf_op jit(solution)/shard_map/all_to_all | solution.py:46
  15.8 8.0 %copy-start.5 = (f32[256,256]{1,0:T(8,128)S(1)}, f32[256,256]{1,0:T(8,128)}, u32[]{:S(2)}) copy-start(f32[256,256]{1,0:T(8,128)} %param.20) | copy-start | bytes 786436
  15.8 8.2 %copy-start.10 = (s32[16]{0:T(128)S(1)}, s32[16]{0:T(128)}, u32[]{:S(2)}) copy-start(s32[16]{0:T(128)} %param.16) | copy-start | bytes 196
  17.7 11.8 %copy-start.2 = (bf16[1,2,16,64,128]{4,3,2,1,0:T(8,128)(2,1)S(1)}, bf16[1,2,16,64,128]{4,3,2,1,0:T(8,128)(2,1)}, u32[]{:S(2)}) copy-start(bf16[1,2,16,64,128]{4,3,2,1,0:T(8,128)(2,1)} %param.13) | copy-start | bytes 1572868
  17.7 8.0 %collective-permute-start = (bf16[1,16,64,128]{3,2,1,0:T(8,128)(2,1)}, bf16[1,16,64,128]{3,2,1,0:T(8,128)(2,1)S(1)}, u32[]{:S(2)}, u32[]{:S(2)}) collective-permute-start(bf16[1,16,64,128]{3,2,1,0:T(8,128)(2,1)} %get-tuple-element.92), channel_id=1, source_target_pairs={{0,1},{1,2},{2,3},{3,4},{4,5},{5,6},{6,7},{7,8},{8,9},{9,10},{10,1... | collective-permute-start | bytes 786440 | tf_op jit(solution)/shard_map/ppermute | solution.py:24
  21.1 8.4 %collective-permute-start.1 = (bf16[1,16,64,128]{3,2,1,0:T(8,128)(2,1)}, bf16[1,16,64,128]{3,2,1,0:T(8,128)(2,1)S(1)}, u32[]{:S(2)}, u32[]{:S(2)}) collective-permute-start(bf16[1,16,64,128]{3,2,1,0:T(8,128)(2,1)} %get-tuple-element.93), channel_id=1, source_target_pairs={{1,0},{2,1},{3,2},{4,3},{5,4},{6,5},{7,6},{8,7},{9,8},{10,9},{11,1... | collective-permute-start | bytes 786440 | tf_op jit(solution)/shard_map/ppermute | solution.py:27
  43.0 24.3 %copy-start.4 = (bf16[3,3,3,128,128]{4,3,2,1,0:T(8,128)(2,1)S(1)}, bf16[3,3,3,128,128]{4,3,2,1,0:T(8,128)(2,1)}, u32[]{:S(2)}) copy-start(bf16[3,3,3,128,128]{4,3,2,1,0:T(8,128)(2,1)} %param.22) | copy-start | bytes 2654212
  43.6 18.0 %all-to-all-start.1 = ((f32[16,2,128]{2,1,0:T(2,128)}), f32[16,2,128]{2,1,0:T(2,128)S(1)}, u32[]{:S(2)}, u32[]{:S(2)}) async-start(f32[16,2,128]{2,1,0:T(2,128)} %broadcast_in_dim.56), calls=%async_computation.1 | async-start | bytes 32768 | tf_op jit(solution)/shard_map/all_to_all | solution.py:46
  63.0 5.7 %collective-permute-start.2 = (bf16[1,16,64,128]{3,2,1,0:T(8,128)(2,1)S(1)}, bf16[1,16,64,128]{3,2,1,0:T(8,128)(2,1)S(1)}, u32[]{:S(2)}, u32[]{:S(2)}) collective-permute-start(bf16[1,16,64,128]{3,2,1,0:T(8,128)(2,1)S(1)} %get-tuple-element.90), channel_id=1, source_target_pairs={{0,1},{1,2},{2,3},{3,4},{4,5},{5,6},{6,7},{7,8},{8,9},{9,10},{10,1... | collective-permute-start | bytes 786440 | tf_op jit(solution)/shard_map/ppermute | solution.py:24
  65.4 7.1 %collective-permute-start.3 = (bf16[1,16,64,128]{3,2,1,0:T(8,128)(2,1)S(1)}, bf16[1,16,64,128]{3,2,1,0:T(8,128)(2,1)S(1)}, u32[]{:S(2)}, u32[]{:S(2)}) collective-permute-start(bf16[1,16,64,128]{3,2,1,0:T(8,128)(2,1)S(1)} %get-tuple-element.91), channel_id=1, source_target_pairs={{1,0},{2,1},{3,2},{4,3},{5,4},{6,5},{7,6},{8,7},{9,8},{10,9},{11,1... | collective-permute-start | bytes 786440 | tf_op jit(solution)/shard_map/ppermute | solution.py:27
  83.3 0.7 copy-start.8
  83.3 22.8 %copy-start.1 = (f32[256,256]{1,0:T(8,128)S(1)}, f32[256,256]{1,0:T(8,128)}, u32[]{:S(2)}) copy-start(f32[256,256]{1,0:T(8,128)} %param.19) | copy-start | bytes 786436
  83.9 21.5 %copy-start.7 = (f32[4,2,64]{2,1,0:T(2,128)S(1)}, f32[4,2,64]{2,1,0:T(2,128)}, u32[]{:S(2)}) copy-start(f32[4,2,64]{2,1,0:T(2,128)} %param.14) | copy-start | bytes 6148
  87.9 15.6 %all-to-all-start.2 = ((f32[16,1,512]{2,1,0:T(1,128)}), f32[16,1,512]{2,1,0:T(1,128)S(1)}, u32[]{:S(2)}, u32[]{:S(2)}) async-start(f32[16,1,512]{2,1,0:T(1,128)} %reshape.184), calls=%async_computation.2 | async-start | bytes 65536 | tf_op jit(solution)/shard_map/all_to_all | solution.py:158

commit v2 on v0

v2 whole, which is shorter than its diff:
```python
import math

import jax
import jax.numpy as jnp
from jax import lax
from jax.experimental import pallas as pl
from jax.experimental.pallas import tpu as pltpu
from jax.sharding import PartitionSpec as P

C = 128
GROUPS = 32
PER_GROUP = C // GROUPS
EMB = 256
LAT = 4
SLOTS = 8
STRIDE = 20
DEP_DEV = 2
H = 16
W = 64
HW = H * W
TERMS = 16
SHARE = HW // TERMS
SLABS = 16
CELLS = DEP_DEV * HW
MEMBERS = float(SLABS * CELLS * PER_GROUP)
TAPS = 27
F32 = jnp.float32
BF16 = jnp.bfloat16
ROWS = 2 * LAT

VMEM = pl.BlockSpec(memory_space=pltpu.VMEM)
SMEM = pl.BlockSpec(memory_space=pltpu.SMEM)
ANY = pl.BlockSpec(memory_space=pl.ANY)
PARAMS = pltpu.CompilerParams(vmem_limit_bytes=32 * 1024 * 1024)


def dot_last(left, right):
    return lax.dot_general(left, right, (((1,), (1,)), ((), ())), preferred_element_type=F32)


def silu(values):
    half = 0.5 * values
    return half + half * jnp.tanh(half)


def own_stats(values, out_ref):
    total = jnp.sum(values, axis=0, keepdims=True)
    centred = values - total * (1.0 / CELLS)
    square = jnp.sum(centred * centred, axis=0, keepdims=True)
    both = jnp.concatenate([total, square], axis=0)
    out_ref[...] = jnp.broadcast_to(both[None], (SLABS, 2, C))


def group_matrix():
    row = lax.broadcasted_iota(jnp.int32, (C, C), 0) // PER_GROUP
    column = lax.broadcasted_iota(jnp.int32, (C, C), 1) // PER_GROUP
    return (row == column).astype(F32)


def over_group(values, matrix):
    wide = jnp.broadcast_to(values, (8, C))
    return jnp.dot(wide, matrix, precision=lax.Precision.HIGHEST, preferred_element_type=F32)[:1]


def all_stats(every_ref):
    every = every_ref[...]
    totals = every[:, 0, :]
    squares = every[:, 1, :]
    matrix = group_matrix()
    average = over_group(jnp.sum(totals, axis=0, keepdims=True), matrix) / MEMBERS
    apart = totals * (1.0 / CELLS) - average
    spread = (
        over_group(jnp.sum(squares + CELLS * (apart * apart), axis=0, keepdims=True), matrix)
        / MEMBERS
    )
    return average, 1.0 / jnp.sqrt(spread + 1e-05)


def stats_kernel(features, out, low, high, held, sems):
    load = pltpu.make_async_copy(features, held, sems.at[0])
    first = pltpu.make_async_copy(features.at[0], low, sems.at[1])
    last = pltpu.make_async_copy(features.at[DEP_DEV - 1], high, sems.at[2])
    load.start()
    first.start()
    last.start()
    load.wait()
    own_stats(held[...].reshape(CELLS, C).astype(F32), out)
    first.wait()
    last.wait()


def stats_call(features):
    plane = jax.ShapeDtypeStruct((HW, C), BF16)
    return pl.pallas_call(
        stats_kernel,
        out_shape=(jax.ShapeDtypeStruct((SLABS, 2, C), F32), plane, plane),
        in_specs=[ANY],
        out_specs=(VMEM, ANY, ANY),
        scratch_shapes=[pltpu.VMEM((DEP_DEV, HW, C), BF16), pltpu.SemaphoreType.DMA((3,))],
        compiler_params=PARAMS,
        name="stats",
    )(features)


def three_parts(values):
    high = values.astype(BF16).astype(F32)
    rest = values - high
    middle = rest.astype(BF16).astype(F32)
    low = rest - middle
    zero = jnp.zeros_like(values)
    return jnp.concatenate([high, middle, low, zero], axis=0).astype(BF16)


def prep_kernel(
    codes, guides, term, sinus, table, time_weight, film, conv_two, head, features, mod, base, mix
):
    def exact(left, right):
        return jnp.dot(left, right, precision=lax.Precision.HIGHEST, preferred_element_type=F32)

    embedding = exact(jnp.broadcast_to(sinus[...], (8, EMB)), time_weight[...])[:1]
    code_part = jnp.zeros((1, EMB), F32)
    for slot in range(SLOTS):
        code_part = code_part + table[slot, pl.ds(codes[0, slot], 1), :]
    embedding = silu(embedding + code_part)
    mod[...] = exact(jnp.broadcast_to(embedding, (8, EMB)), film[...])

    others = guides[1]
    for at in range(2, TERMS):
        others = others + guides[at]
    own = jnp.where(term[0] == 0, TERMS - others, guides[term[0]])
    weight = own.astype(F32) * (1.0 / 16.0)

    head_rows = jnp.concatenate([head[...], head[...]], axis=0)
    upper = lax.broadcasted_iota(jnp.int32, (ROWS, C), 0) < LAT
    parts = three_parts(head_rows)
    composed = dot_last(parts, conv_two[...])
    composed = (
        composed[:ROWS] + (composed[ROWS : 2 * ROWS] + composed[2 * ROWS : 3 * ROWS])
    ) * weight
    nothing = jnp.zeros((ROWS, C), F32)
    for near in range(9):
        for plane in range(DEP_DEV + 2):
            at = [
                composed[:, (tap * 9 + near) * C : (tap * 9 + near + 1) * C]
                if 0 <= tap < 3
                else nothing
                for tap in (plane, plane - 1)
            ]
            mix[near * ROWS : (near + 1) * ROWS, plane * C : (plane + 1) * C] = jnp.where(
                upper, at[0], at[1]
            )

    wide = jnp.concatenate(
        [jnp.where(upper, head_rows, 0.0), jnp.where(upper, 0.0, head_rows)], axis=1
    )
    both = jnp.concatenate([features[0], features[1]], axis=1)
    direct = dot_last(three_parts(wide), both)
    base[...] = (direct[:ROWS] + (direct[ROWS : 2 * ROWS] + direct[2 * ROWS : 3 * ROWS])) * weight


def prep_call(codes, guides, term, sinus, table, time_weight, film, conv_two, head, features):
    return pl.pallas_call(
        prep_kernel,
        out_shape=(
            jax.ShapeDtypeStruct((8, 2 * C), F32),
            jax.ShapeDtypeStruct((ROWS, HW), F32),
            jax.ShapeDtypeStruct((9 * ROWS, 4 * C), F32),
        ),
        in_specs=[SMEM, SMEM, SMEM] + [VMEM] * 7,
        out_specs=(VMEM, VMEM, VMEM),
        compiler_params=PARAMS,
        cost_estimate=pl.CostEstimate(
            flops=200_000_000, bytes_accessed=3_000_000, transcendentals=512
        ),
        name="prep",
    )(codes, guides, term, sinus, table, time_weight, film, conv_two, head, features)


def conv_kernel(edges, every, low, own, high, weight, out, out_low, out_high, out_stats, held, side):
    average, scale = all_stats(every)
    shift = -average * scale
    held[0:W, :] = jnp.zeros((W, 4 * C), BF16)
    held[W + HW :, :] = jnp.zeros((W, 4 * C), BF16)
    for plane, (source, edge) in enumerate(
        [(low, 0), (own.at[0], None), (own.at[1], None), (high, 1)]
    ):
        values = silu(source[...].astype(F32) * scale + shift)
        if edge is not None:
            values = values * edges[edge]
        held[W : W + HW, plane * C : (plane + 1) * C] = values.astype(BF16)

    zero = jnp.zeros((C, C), BF16)
    column = lax.broadcasted_iota(jnp.int32, (HW, C), 0) % W

    def taps(col):
        blocks = []
        for row in range(3):
            for plane in range(4):
                pair = [
                    weight[((tap * 3 + row) * 3 + col) * C : ((tap * 3 + row) * 3 + col + 1) * C, :]
                    if 0 <= tap < 3
                    else zero
                    for tap in (plane, plane - 1)
                ]
                blocks.append(jnp.concatenate(pair, axis=1))
        return jnp.concatenate(blocks, axis=0)

    left = jnp.concatenate([held[row * W : row * W + HW, :] for row in range(3)], axis=1)
    products = [
        jnp.dot(left, taps(col), preferred_element_type=F32) for col in range(3)
    ]
    planes = []
    for plane in range(DEP_DEV):
        part = [product[:, plane * C : (plane + 1) * C] for product in products]
        side[8 : 8 + HW, :] = part[0]
        before = jnp.where(column == 0, 0.0, side[7 : 7 + HW, :])
        side[8 : 8 + HW, :] = part[2]
        after = jnp.where(column == W - 1, 0.0, side[9 : 9 + HW, :])
        values = part[1] + before + after
        out[plane] = values
        planes.append(values)
    out_low[...] = planes[0].astype(BF16)
    out_high[...] = planes[1].astype(BF16)
    own_stats(jnp.concatenate(planes, axis=0), out_stats)


def conv_call(edges, every, low, own, high, weight):
    plane = jax.ShapeDtypeStruct((HW, C), BF16)
    return pl.pallas_call(
        conv_kernel,
        out_shape=(
            jax.ShapeDtypeStruct((DEP_DEV, HW, C), F32),
            plane,
            plane,
            jax.ShapeDtypeStruct((SLABS, 2, C), F32),
        ),
        in_specs=[SMEM] + [VMEM] * 5,
        out_specs=(VMEM,) * 4,
        scratch_shapes=[
            pltpu.VMEM((HW + 2 * W, 4 * C), BF16),
            pltpu.VMEM((HW + 16, C), F32),
        ],
        compiler_params=PARAMS,
        cost_estimate=pl.CostEstimate(
            flops=2_500_000_000, bytes_accessed=4_000_000, transcendentals=500_000
        ),
        name="conv",
    )(edges, every, low, own, high, weight)


def head_kernel(edges, every, low, own, high, mod, base, mix, out, held):
    average, scale = all_stats(every)
    factor = scale * (1.0 + mod[0:1, :C])
    shift = mod[0:1, C:] - average * factor
    for plane, (source, edge) in enumerate(
        [(low, 0), (own.at[0], None), (own.at[1], None), (high, 1)]
    ):
        values = silu(source[...].astype(F32) * factor + shift)
        if edge is not None:
            values = values * edges[edge]
        held[:, plane * C : (plane + 1) * C] = values.astype(BF16)
    weights = mix[...]
    coarse = weights.astype(BF16).astype(F32)
    pair = jnp.concatenate([coarse, weights - coarse], axis=0).astype(BF16)
    product = dot_last(pair, held[...])
    product = product[: 9 * ROWS] + product[9 * ROWS :]
    at = lax.broadcasted_iota(jnp.int32, (ROWS, HW), 1)
    summed = base[...]
    for col in range(3):
        part = [product[(row * 3 + col) * ROWS : (row * 3 + col + 1) * ROWS] for row in range(3)]
        values = (
            part[1]
            + jnp.where(at < W, 0.0, pltpu.roll(part[0], W, 1))
            + jnp.where(at >= HW - W, 0.0, pltpu.roll(part[2], HW - W, 1))
        )
        if col == 0:
            values = jnp.where(at % W == 0, 0.0, pltpu.roll(values, 1, 1))
        if col == 2:
            values = jnp.where(at % W == W - 1, 0.0, pltpu.roll(values, HW - 1, 1))
        summed = summed + values
    for target in range(TERMS):
        piece = summed[:, target * SHARE : (target + 1) * SHARE]
        out[target] = jnp.concatenate([piece[:LAT], piece[LAT:]], axis=1)


def head_call(edges, every, low, own, high, mod, base, mix):
    return pl.pallas_call(
        head_kernel,
        out_shape=jax.ShapeDtypeStruct((TERMS, LAT, DEP_DEV * SHARE), F32),
        in_specs=[SMEM] + [VMEM] * 7,
        out_specs=VMEM,
        scratch_shapes=[pltpu.VMEM((HW, 4 * C), BF16)],
        compiler_params=PARAMS,
        name="head",
    )(edges, every, low, own, high, mod, base, mix)


def final_kernel(roots, pieces, latent, guided, stepped):
    total = jnp.sum(pieces[...], axis=0)
    for plane in range(DEP_DEV):
        value = total[:, plane * SHARE : (plane + 1) * SHARE]
        clean = (latent[:, plane, :] - roots[0] * value) / roots[1]
        guided[:, plane, :] = value
        stepped[:, plane, :] = roots[2] * clean + roots[3] * value


def final_call(roots, pieces, latent):
    shape = jax.ShapeDtypeStruct((LAT, DEP_DEV, SHARE), F32)
    return pl.pallas_call(
        final_kernel,
        out_shape=(shape, shape),
        in_specs=[SMEM, VMEM, VMEM],
        out_specs=(VMEM, VMEM),
        compiler_params=PARAMS,
        name="final",
    )(roots, pieces, latent)


def plan(step_value):
    frac = (step_value / 1000.0 + 0.008) / 1.008
    return jnp.cos(frac * math.pi / 2.0) ** 2


def rims(low, high):
    forward = [(i, i + 1) for i in range(SLABS - 1)]
    backward = [(i + 1, i) for i in range(SLABS - 1)]
    return lax.ppermute(high, "slab", forward), lax.ppermute(low, "slab", backward)


def per_device(
    features,
    latent,
    cond_codes,
    guide_codes,
    timestep,
    code_table,
    time_weight,
    film_weight,
    conv_one,
    conv_two,
    head_weight,
):
    planes = features.reshape(DEP_DEV, HW, C)
    slab_index = lax.axis_index("slab")
    edges = jnp.stack([slab_index > 0, slab_index < SLABS - 1]).astype(F32)
    term = lax.axis_index("cond").astype(jnp.int32).reshape(1)
    time_value = timestep[0].astype(F32)
    half_width = EMB // 2
    frequency = jnp.exp(-math.log(10000.0) * jnp.arange(half_width, dtype=F32) / half_width)
    angles = time_value * frequency
    sinus = jnp.concatenate([jnp.cos(angles), jnp.sin(angles)]).reshape(1, EMB)
    now_bar = plan(time_value)
    next_bar = plan(time_value - STRIDE)
    roots = jnp.sqrt(jnp.stack([1.0 - now_bar, now_bar, next_bar, 1.0 - next_bar]))

    stats, low, high = stats_call(planes)
    below, above = rims(low, high)
    every = lax.all_to_all(stats, "slab", 0, 0)
    mod, base, mix = prep_call(
        cond_codes,
        guide_codes,
        term,
        sinus,
        code_table,
        time_weight,
        film_weight,
        conv_two.reshape(TAPS * C, C),
        head_weight.T,
        planes,
    )
    first, low, high, stats = conv_call(
        edges, every, below, planes, above, conv_one.reshape(TAPS * C, C)
    )
    below, above = rims(low, high)
    every = lax.all_to_all(stats, "slab", 0, 0)
    pieces = head_call(edges, every, below, first, above, mod, base, mix)
    pieces = lax.all_to_all(pieces, "cond", 0, 0)
    return final_call(roots, pieces, latent)


def solution(mesh):
    placed = (
        P("cond", "slab", None, None, None),
        P(None, "slab", "cond"),
        P("cond", None),
        P(),
        P(),
        P(),
        P(),
        P(),
        P(),
        P(),
        P(),
    )
    return jax.shard_map(
        per_device,
        mesh=mesh,
        in_specs=placed,
        out_specs=(P(None, "slab", "cond"), P(None, "slab", "cond")),
        check_vma=False,
    )
```

time: 274 us -> 78.3 us (0.29)
  the two profiles are of different devices: /device:TPU:6 before, /device:TPU:1 now
where the time goes in v2:
time: 78.3 us; the launch traced here: 77.7 us
  starting transfers between devices  37.8 us (48%)
  waiting for transfers between devices  17.5 us (22%)
  Pallas kernels  12.1 us (15%)
  local copies, waits for them, and re-layouts  7.94 us (10%)
  between operations  1.62 us (2%)
    all_to_all x2, starting transfers between devices, per_device(): every = lax.all_to_all(stats, 'slab', 0, 0)  19.5 us
    all_to_all x2, waiting for transfers between devices, per_device(): every = lax.all_to_all(stats, 'slab', 0, 0)  11.8 us
    all_to_all x1, starting transfers between devices, per_device(): pieces = lax.all_to_all(pieces, 'cond', 0, 0)  9.15 us
    unnamed x36, local copies, waits for them, and re-layouts  7.94 us
    ppermute x2, starting transfers between devices, rims(): lax.ppermute(high, 'slab', forward)  6.61 us
    all_to_all x1, waiting for transfers between devices, per_device(): pieces = lax.all_to_all(pieces, 'cond', 0, 0)  5.71 us
    pallas_call x1, Pallas kernels, conv_call(): pl.pallas_call(conv_kernel, out_shape=(jax.ShapeDtypeStruct((DEP_DEV, HW,...  5.19 us
    pallas_call x1, Pallas kernels, head_call(): pl.pallas_call(head_kernel, out_shape=jax.ShapeDtypeStruct((TERMS, LAT, D...  2.78 us
  transfers between devices with their start and end apart: 7, of which 3 were waited for; matrix products, arithmetic and copies ran while one was open for 1% of the time, Pallas kernels for 2%

profile of v2, /device:TPU:1, one launch (start us, length us, event | category | flops | bytes accessed | tf_op | source)
XLA Modules:
  0.0 77.7 jit_solution(18285705582442882246)
XLA Ops:
  0.6 1.0 %copy-done = bf16[1,2,16,64,128]{4,3,2,1,0:T(8,128)(2,1)S(1)} copy-done((bf16[1,2,16,64,128]{4,3,2,1,0:T(8,128)(2,1)S(1)}, bf16[1,2,16,64,128]{4,3,2,1,0:T(8,128)(2,1)}, u32[]{:S(2)}) %copy-start) | copy-done | bytes 524312
  1.7 1.3 %stats.1 = (f32[16,2,128]{2,1,0:T(2,128)}, bf16[1024,128]{1,0:T(8,128)(2,1)S(1)}, bf16[1024,128]{1,0:T(8,128)(2,1)S(1)}) custom-call(bf16[2,1024,128]{2,1,0:T(8,128)(2,1)S(1)} %bitcast.13), custom_call_target="tpu_custom_call" | custom-call | tf_op jit(solution)/shard_map/stats/pallas_call | solution.py:94
  2.9 4.4 %collective-permute-start = (bf16[1024,128]{1,0:T(8,128)(2,1)S(1)}, bf16[1024,128]{1,0:T(8,128)(2,1)S(1)}, u32[]{:S(2)}, u32[]{:S(2)}) collective-permute-start(bf16[1024,128]{1,0:T(8,128)(2,1)S(1)} %get-tuple-element.13), channel_id=1, source_target_pairs={{0,1},{1,2},{2,3},{3,4},{4,5},{5,6},{6,7},{7,8},{8,9},{9,10},{10,1... | collective-permute-start | bytes 786440 | tf_op jit(solution)/shard_map/ppermute | solution.py:327
  7.3 1.3 %collective-permute-start.1 = (bf16[1024,128]{1,0:T(8,128)(2,1)S(1)}, bf16[1024,128]{1,0:T(8,128)(2,1)S(1)}, u32[]{:S(2)}, u32[]{:S(2)}) collective-permute-start(bf16[1024,128]{1,0:T(8,128)(2,1)S(1)} %get-tuple-element.14), channel_id=1, source_target_pairs={{1,0},{2,1},{3,2},{4,3},{5,4},{6,5},{7,6},{8,7},{9,8},{10,9},{11,1... | collective-permute-start | bytes 786440 | tf_op jit(solution)/shard_map/ppermute | solution.py:327
  8.6 12.4 %all-to-all-start = ((f32[16,2,128]{2,1,0:T(2,128)}), f32[16,2,128]{2,1,0:T(2,128)S(1)}, u32[]{:S(2)}, u32[]{:S(2)}) async-start(f32[16,2,128]{2,1,0:T(2,128)} %get-tuple-element.12), calls=%async_computation | async-start | bytes 32768 | tf_op jit(solution)/shard_map/all_to_all | solution.py:358
  21.1 0.1 add_convert_fusion.edges
  21.1 8.8 %all-to-all-done.every = f32[16,2,128]{2,1,0:T(2,128)S(1)} async-done(((f32[16,2,128]{2,1,0:T(2,128)}), f32[16,2,128]{2,1,0:T(2,128)S(1)}, u32[]{:S(2)}, u32[]{:S(2)}) %all-to-all-start) | async-done | bytes 16416 | tf_op jit(solution)/shard_map/all_to_all | solution.py:358
  29.9 0.0 copy-start.17
  29.9 1.2 %copy-done.17 = bf16[3,3,3,128,128]{4,3,2,1,0:T(8,128)(2,1)S(1)} copy-done((bf16[3,3,3,128,128]{4,3,2,1,0:T(8,128)(2,1)S(1)}, bf16[3,3,3,128,128]{4,3,2,1,0:T(8,128)(2,1)}, u32[]{:S(2)}) %copy-start.17) | copy-done | bytes 884760
  31.1 5.2 %conv.1 = (f32[2,1024,128]{2,1,0:T(8,128)S(1)}, bf16[1024,128]{1,0:T(8,128)(2,1)}, bf16[1024,128]{1,0:T(8,128)(2,1)}, f32[16,2,128]{2,1,0:T(2,128)}) custom-call(f32[2]{0:T(128)S(1)} %add_convert_fusion.edges, f32[16,2,128]{2,1,0:T(2,128)S(1)} %all-to-all-done.every, bf16[1024,128]{1,0:T(8,128)(2,1)S(1)} %collective-permute-done.low, ...), custom_call_target="tpu_custom_call" | custom-call | flops 2500000000 | bytes 4000000 | tf_op jit(solution)/shard_map/conv/pallas_call | solution.py:229
  36.3 2.2 %collective-permute-start.2 = (bf16[1024,128]{1,0:T(8,128)(2,1)}, bf16[1024,128]{1,0:T(8,128)(2,1)S(1)}, u32[]{:S(2)}, u32[]{:S(2)}) collective-permute-start(bf16[1024,128]{1,0:T(8,128)(2,1)} %get-tuple-element.16), channel_id=1, source_target_pairs={{0,1},{1,2},{2,3},{3,4},{4,5},{5,6},{6,7},{7,8},{8,9},{9,10},{10,1... | collective-permute-start | bytes 786440 | tf_op jit(solution)/shard_map/ppermute | solution.py:327
  38.5 1.3 %collective-permute-start.3 = (bf16[1024,128]{1,0:T(8,128)(2,1)}, bf16[1024,128]{1,0:T(8,128)(2,1)S(1)}, u32[]{:S(2)}, u32[]{:S(2)}) collective-permute-start(bf16[1024,128]{1,0:T(8,128)(2,1)} %get-tuple-element.18), channel_id=1, source_target_pairs={{1,0},{2,1},{3,2},{4,3},{5,4},{6,5},{7,6},{8,7},{9,8},{10,9},{11,1... | collective-permute-start | bytes 786440 | tf_op jit(solution)/shard_map/ppermute | solution.py:327
  40.5 7.1 %all-to-all-start.1 = ((f32[16,2,128]{2,1,0:T(2,128)}), f32[16,2,128]{2,1,0:T(2,128)S(1)}, u32[]{:S(2)}, u32[]{:S(2)}) async-start(f32[16,2,128]{2,1,0:T(2,128)} %get-tuple-element.15), calls=%async_computation.1 | async-start | bytes 32768 | tf_op jit(solution)/shard_map/all_to_all | solution.py:375
  47.6 0.6 pad_maximum_fusion
  48.3 0.0 copy-start.12
  48.4 0.6 copy-done.12
  49.0 0.0 copy-done.10
  49.1 0.9 %copy-done.7 = f32[8,16,256]{2,1,0:T(8,128)S(1)} copy-done((f32[8,16,256]{2,1,0:T(8,128)S(1)}, f32[8,16,256]{2,1,0:T(8,128)}, u32[]{:S(2)}) %copy-start.7) | copy-done | bytes 131096
  50.0 0.7 copy-done.14
  50.6 1.6 %prep.1 = (f32[8,256]{1,0:T(8,128)S(1)}, f32[8,1024]{1,0:T(8,128)S(1)}, f32[72,512]{1,0:T(8,128)S(1)}) custom-call(s32[1,8]{1,0:T(1,128)S(1)} %copy-done.13, s32[16]{0:T(128)S(1)} %copy-done.14, s32[1]{0:T(128)} %bitcast.9.term, f32[1,256]{1,0:T(1,128)S(1)} %bitcast.17, f32[8,16,256]{2,1,0:T(8,128)S(1)} %copy-done.7, f32[256,256]{1,0:T(8,128)S(1)} %copy-done.3, ...), custom_call_target="tpu_custom_call" | custom-call | flops 200000000 | bytes 3000000 | tf_op jit(solution)/shard_map/prep/pallas_call | solution.py:162
  52.2 0.0 copy-start.5
  52.2 0.7 copy-done.5
  52.9 0.6 copy-done.8
  53.4 3.0 %all-to-all-done.1.every = f32[16,2,128]{2,1,0:T(2,128)S(1)} async-done(((f32[16,2,128]{2,1,0:T(2,128)}), f32[16,2,128]{2,1,0:T(2,128)S(1)}, u32[]{:S(2)}, u32[]{:S(2)}) %all-to-all-start.1) | async-done | bytes 16416 | tf_op jit(solution)/shard_map/all_to_all | solution.py:375
  56.5 0.6 copy-done.16
  57.1 0.9 %copy-done.6 = f32[72,512]{1,0:T(8,128)S(1)} copy-done((f32[72,512]{1,0:T(8,128)S(1)}, f32[72,512]{1,0:T(8,128)}, u32[]{:S(2)}) %copy-start.6) | copy-done | bytes 147480
  58.0 0.7 copy-done.9
  58.7 2.8 %head.1 = f32[16,4,128]{2,1,0:T(4,128)} custom-call(f32[2]{0:T(128)S(1)} %copy-done.16, f32[16,2,128]{2,1,0:T(2,128)S(1)} %all-to-all-done.1.every, bf16[1024,128]{1,0:T(8,128)(2,1)S(1)} %collective-permute-done.2.low, f32[2,1024,128]{2,1,0:T(8,128)S(1)} %get-tuple-element.17.own, bf16[1024,128]{1,0:T(8,128)(2,1)S(1)} %collective-permute-done.3.high, ...), custom_call_target="tpu_custom_call" | custom-call | tf_op jit(solution)/shard_map/head/pallas_call | solution.py:287
  61.5 9.2 %all-to-all-start.2 = ((f32[16,4,128]{2,1,0:T(4,128)}), f32[16,4,128]{2,1,0:T(4,128)S(1)}, u32[]{:S(2)}, u32[]{:S(2)}) async-start(f32[16,4,128]{2,1,0:T(4,128)} %head.1), calls=%async_computation.2 | async-start | bytes 65536 | tf_op jit(solution)/shard_map/all_to_all | solution.py:377
  70.6 0.1 maximum_sqrt_fusion.roots
  70.7 5.7 %all-to-all-done.2.pieces = f32[16,4,128]{2,1,0:T(4,128)S(1)} async-done(((f32[16,4,128]{2,1,0:T(4,128)}), f32[16,4,128]{2,1,0:T(4,128)S(1)}, u32[]{:S(2)}, u32[]{:S(2)}) %all-to-all-start.2) | async-done | bytes 32800 | tf_op jit(solution)/shard_map/all_to_all | solution.py:377
  76.4 1.3 %final.1 = (f32[4,2,64]{2,1,0:T(2,128)}, f32[4,2,64]{2,1,0:T(2,128)}) custom-call(f32[4]{0:T(128)S(1)} %maximum_sqrt_fusion.roots, f32[16,4,128]{2,1,0:T(4,128)S(1)} %all-to-all-done.2.pieces, f32[4,2,64]{2,1,0:T(2,128)S(1)} %copy-done.11), custom_call_target="tpu_custom_call" | custom-call | tf_op jit(solution)/shard_map/final/pallas_call | solution.py:309
  (27 shorter events, 0.1 us)
Async XLA Ops:
  0.6 1.0 %copy-start = (bf16[1,2,16,64,128]{4,3,2,1,0:T(8,128)(2,1)S(1)}, bf16[1,2,16,64,128]{4,3,2,1,0:T(8,128)(2,1)}, u32[]{:S(2)}) copy-start(bf16[1,2,16,64,128]{4,3,2,1,0:T(8,128)(2,1)} %param.11) | copy-start | bytes 1572868
  1.7 28.2 %copy-start.1 = (bf16[1,2,16,64,128]{4,3,2,1,0:T(8,128)(2,1)S(1)}, bf16[1,2,16,64,128]{4,3,2,1,0:T(8,128)(2,1)}, u32[]{:S(2)}) copy-start(bf16[1,2,16,64,128]{4,3,2,1,0:T(8,128)(2,1)} %param.11) | copy-start | bytes 1572868
  2.9 27.0 %collective-permute-start = (bf16[1024,128]{1,0:T(8,128)(2,1)S(1)}, bf16[1024,128]{1,0:T(8,128)(2,1)S(1)}, u32[]{:S(2)}, u32[]{:S(2)}) collective-permute-start(bf16[1024,128]{1,0:T(8,128)(2,1)S(1)} %get-tuple-element.13), channel_id=1, source_target_pairs={{0,1},{1,2},{2,3},{3,4},{4,5},{5,6},{6,7},{7,8},{8,9},{9,10},{10,1... | collective-permute-start | bytes 786440 | tf_op jit(solution)/shard_map/ppermute | solution.py:327
  7.3 22.6 %collective-permute-start.1 = (bf16[1024,128]{1,0:T(8,128)(2,1)S(1)}, bf16[1024,128]{1,0:T(8,128)(2,1)S(1)}, u32[]{:S(2)}, u32[]{:S(2)}) collective-permute-start(bf16[1024,128]{1,0:T(8,128)(2,1)S(1)} %get-tuple-element.14), channel_id=1, source_target_pairs={{1,0},{2,1},{3,2},{4,3},{5,4},{6,5},{7,6},{8,7},{9,8},{10,9},{11,1... | collective-permute-start | bytes 786440 | tf_op jit(solution)/shard_map/ppermute | solution.py:327
  8.6 21.3 %all-to-all-start = ((f32[16,2,128]{2,1,0:T(2,128)}), f32[16,2,128]{2,1,0:T(2,128)S(1)}, u32[]{:S(2)}, u32[]{:S(2)}) async-start(f32[16,2,128]{2,1,0:T(2,128)} %get-tuple-element.12), calls=%async_computation | async-start | bytes 32768 | tf_op jit(solution)/shard_map/all_to_all | solution.py:358
  21.1 8.8 %copy-start.15 = (f32[2]{0:T(128)}, f32[2]{0:T(128)S(1)}, u32[]{:S(2)}) copy-start(f32[2]{0:T(128)S(1)} %add_convert_fusion.edges) | copy-start | bytes 28
  29.9 1.2 %copy-start.17 = (bf16[3,3,3,128,128]{4,3,2,1,0:T(8,128)(2,1)S(1)}, bf16[3,3,3,128,128]{4,3,2,1,0:T(8,128)(2,1)}, u32[]{:S(2)}) copy-start(bf16[3,3,3,128,128]{4,3,2,1,0:T(8,128)(2,1)} %param.19) | copy-start | bytes 2654212
  31.1 17.3 %copy-start.2 = (bf16[3,3,3,128,128]{4,3,2,1,0:T(8,128)(2,1)S(1)}, bf16[3,3,3,128,128]{4,3,2,1,0:T(8,128)(2,1)}, u32[]{:S(2)}) copy-start(bf16[3,3,3,128,128]{4,3,2,1,0:T(8,128)(2,1)} %param.20) | copy-start | bytes 2654212
  31.1 17.3 %copy-start.3 = (f32[256,256]{1,0:T(8,128)S(1)}, f32[256,256]{1,0:T(8,128)}, u32[]{:S(2)}) copy-start(f32[256,256]{1,0:T(8,128)} %time_weight.1) | copy-start | bytes 786436
  31.1 17.3 %copy-start.4 = (f32[256,256]{1,0:T(8,128)S(1)}, f32[256,256]{1,0:T(8,128)}, u32[]{:S(2)}) copy-start(f32[256,256]{1,0:T(8,128)} %film.1) | copy-start | bytes 786436
  36.3 20.2 %collective-permute-start.2 = (bf16[1024,128]{1,0:T(8,128)(2,1)}, bf16[1024,128]{1,0:T(8,128)(2,1)S(1)}, u32[]{:S(2)}, u32[]{:S(2)}) collective-permute-start(bf16[1024,128]{1,0:T(8,128)(2,1)} %get-tuple-element.16), channel_id=1, source_target_pairs={{0,1},{1,2},{2,3},{3,4},{4,5},{5,6},{6,7},{7,8},{8,9},{9,10},{10,1... | collective-permute-start | bytes 786440 | tf_op jit(solution)/shard_map/ppermute | solution.py:327
  38.5 17.9 %collective-permute-start.3 = (bf16[1024,128]{1,0:T(8,128)(2,1)}, bf16[1024,128]{1,0:T(8,128)(2,1)S(1)}, u32[]{:S(2)}, u32[]{:S(2)}) collective-permute-start(bf16[1024,128]{1,0:T(8,128)(2,1)} %get-tuple-element.18), channel_id=1, source_target_pairs={{1,0},{2,1},{3,2},{4,3},{5,4},{6,5},{7,6},{8,7},{9,8},{10,9},{11,1... | collective-permute-start | bytes 786440 | tf_op jit(solution)/shard_map/ppermute | solution.py:327
  40.5 15.9 %all-to-all-start.1 = ((f32[16,2,128]{2,1,0:T(2,128)}), f32[16,2,128]{2,1,0:T(2,128)S(1)}, u32[]{:S(2)}, u32[]{:S(2)}) async-start(f32[16,2,128]{2,1,0:T(2,128)} %get-tuple-element.15), calls=%async_computation.1 | async-start | bytes 32768 | tf_op jit(solution)/shard_map/all_to_all | solution.py:375
  48.3 0.7 copy-start.12
  48.3 0.7 copy-start.10
  48.4 0.7 copy-start.13
  49.1 0.9 %copy-start.7 = (f32[8,16,256]{2,1,0:T(8,128)S(1)}, f32[8,16,256]{2,1,0:T(8,128)}, u32[]{:S(2)}) copy-start(f32[8,16,256]{2,1,0:T(8,128)} %table.1) | copy-start | bytes 393220
  50.0 0.7 copy-start.14
  52.2 0.7 copy-start.5
  52.9 0.6 copy-start.8
  56.4 0.6 copy-start.16
  57.1 0.9 %copy-start.6 = (f32[72,512]{1,0:T(8,128)S(1)}, f32[72,512]{1,0:T(8,128)}, u32[]{:S(2)}) copy-start(f32[72,512]{1,0:T(8,128)} %copy-done.5) | copy-start | bytes 442372
  58.0 0.7 copy-start.9
  61.5 15.0 %all-to-all-start.2 = ((f32[16,4,128]{2,1,0:T(4,128)}), f32[16,4,128]{2,1,0:T(4,128)S(1)}, u32[]{:S(2)}, u32[]{:S(2)}) async-start(f32[16,4,128]{2,1,0:T(4,128)} %head.1), calls=%async_computation.2 | async-start | bytes 65536 | tf_op jit(solution)/shard_map/all_to_all | solution.py:377
  70.6 5.8 %copy-start.11 = (f32[4,2,64]{2,1,0:T(2,128)S(1)}, f32[4,2,64]{2,1,0:T(2,128)}, u32[]{:S(2)}) copy-start(f32[4,2,64]{2,1,0:T(2,128)} %latent.1) | copy-start | bytes 6148

commit v3 on v2

v3 whole, which is shorter than its diff:
```python
import math

import jax
import jax.numpy as jnp
from jax import lax
from jax.experimental import pallas as pl
from jax.experimental.pallas import tpu as pltpu
from jax.sharding import PartitionSpec as P

C = 128
GROUPS = 32
PER_GROUP = C // GROUPS
EMB = 256
LAT = 4
SLOTS = 8
STRIDE = 20
DEP_DEV = 2
H = 16
W = 64
HW = H * W
TERMS = 16
SHARE = HW // TERMS
SLABS = 16
CELLS = DEP_DEV * HW
MEMBERS = float(SLABS * CELLS * PER_GROUP)
TAPS = 27
F32 = jnp.float32
BF16 = jnp.bfloat16
ROWS = 2 * LAT

VMEM = pl.BlockSpec(memory_space=pltpu.VMEM)
SMEM = pl.BlockSpec(memory_space=pltpu.SMEM)
ANY = pl.BlockSpec(memory_space=pl.ANY)
HBM = pl.BlockSpec(memory_space=pltpu.HBM)


def params(mebibytes):
    return pltpu.CompilerParams(vmem_limit_bytes=mebibytes * 1024 * 1024)


def dot_last(left, right):
    return lax.dot_general(left, right, (((1,), (1,)), ((), ())), preferred_element_type=F32)


def silu(values):
    half = 0.5 * values
    return half + half * jnp.tanh(half)


def own_stats(values, out_ref):
    total = jnp.sum(values, axis=0, keepdims=True)
    centred = values - total * (1.0 / CELLS)
    square = jnp.sum(centred * centred, axis=0, keepdims=True)
    both = jnp.concatenate([total, square], axis=0)
    out_ref[...] = jnp.broadcast_to(both[None], (SLABS, 2, C))


def group_matrix():
    row = lax.broadcasted_iota(jnp.int32, (C, C), 0) // PER_GROUP
    column = lax.broadcasted_iota(jnp.int32, (C, C), 1) // PER_GROUP
    return (row == column).astype(BF16)


def three_parts(values):
    high = values.astype(BF16).astype(F32)
    rest = values - high
    middle = rest.astype(BF16).astype(F32)
    low = rest - middle
    zero = jnp.zeros_like(values)
    return jnp.concatenate([high, middle, low, zero], axis=0).astype(BF16)


def over_group(values, matrix):
    wide = three_parts(jnp.broadcast_to(values, (8, C)))
    folded = jnp.dot(wide, matrix, preferred_element_type=F32)
    return folded[:1] + (folded[8:9] + folded[16:17])


def all_stats(every_ref):
    every = every_ref[...]
    totals = every[:, 0, :]
    squares = every[:, 1, :]
    matrix = group_matrix()
    average = over_group(jnp.sum(totals, axis=0, keepdims=True), matrix) / MEMBERS
    apart = totals * (1.0 / CELLS) - average
    spread = (
        over_group(jnp.sum(squares + CELLS * (apart * apart), axis=0, keepdims=True), matrix)
        / MEMBERS
    )
    return average, 1.0 / jnp.sqrt(spread + 1e-05)


def stats_kernel(features, out):
    own_stats(features[...].reshape(CELLS, C).astype(F32), out)


def stats_call(features):
    return pl.pallas_call(
        stats_kernel,
        out_shape=jax.ShapeDtypeStruct((SLABS, 2, C), F32),
        in_specs=[VMEM],
        out_specs=VMEM,
        compiler_params=params(4),
        name="stats",
    )(features)


def rims_kernel(planes, odd, even):
    parity = lax.axis_index("slab") % 2
    odd[...] = planes[parity]
    even[...] = planes[DEP_DEV - 1 - parity]


def rims_call(planes):
    plane = jax.ShapeDtypeStruct((HW, C), BF16)
    return pl.pallas_call(
        rims_kernel,
        out_shape=(plane, plane),
        in_specs=[VMEM],
        out_specs=(VMEM, VMEM),
        compiler_params=params(4),
        name="rims",
    )(planes)


def prep_kernel(
    codes,
    guides,
    sinus,
    roots,
    table,
    time_weight,
    film,
    conv_two,
    head,
    features,
    mod,
    base,
    mix,
    held_roots,
):
    held_roots[...] = jnp.broadcast_to(roots[...], (8, C))

    def exact(left, right):
        return jnp.dot(left, right, precision=lax.Precision.HIGHEST, preferred_element_type=F32)

    embedding = exact(jnp.broadcast_to(sinus[...], (8, EMB)), time_weight[...])[:1]
    code_part = jnp.zeros((1, EMB), F32)
    for slot in range(SLOTS):
        code_part = code_part + table[slot, pl.ds(codes[0, slot], 1), :]
    embedding = silu(embedding + code_part)
    mod[...] = exact(jnp.broadcast_to(embedding, (8, EMB)), film[...])

    others = guides[1]
    for at in range(2, TERMS):
        others = others + guides[at]
    term = lax.axis_index("cond")
    own = jnp.where(term == 0, TERMS - others, guides[term])
    weight = own.astype(F32) * (1.0 / 16.0)

    head_rows = jnp.concatenate([head[...], head[...]], axis=0)
    upper = lax.broadcasted_iota(jnp.int32, (ROWS, C), 0) < LAT
    parts = three_parts(head_rows)
    composed = dot_last(parts, conv_two[...])
    composed = (
        composed[:ROWS] + (composed[ROWS : 2 * ROWS] + composed[2 * ROWS : 3 * ROWS])
    ) * weight
    nothing = jnp.zeros((ROWS, C), F32)
    for near in range(9):
        for plane in range(DEP_DEV + 2):
            at = [
                composed[:, (tap * 9 + near) * C : (tap * 9 + near + 1) * C]
                if 0 <= tap < 3
                else nothing
                for tap in (plane, plane - 1)
            ]
            mix[near * ROWS : (near + 1) * ROWS, plane * C : (plane + 1) * C] = jnp.where(
                upper, at[0], at[1]
            )

    wide = jnp.concatenate(
        [jnp.where(upper, head_rows, 0.0), jnp.where(upper, 0.0, head_rows)], axis=1
    )
    both = jnp.concatenate([features[0], features[1]], axis=1)
    direct = dot_last(three_parts(wide), both)
    base[...] = (direct[:ROWS] + (direct[ROWS : 2 * ROWS] + direct[2 * ROWS : 3 * ROWS])) * weight


def prep_call(codes, guides, sinus, roots, table, time_weight, film, conv_two, head, features):
    return pl.pallas_call(
        prep_kernel,
        out_shape=(
            jax.ShapeDtypeStruct((8, 2 * C), F32),
            jax.ShapeDtypeStruct((ROWS, HW), F32),
            jax.ShapeDtypeStruct((9 * ROWS, 4 * C), F32),
            jax.ShapeDtypeStruct((8, C), F32),
        ),
        in_specs=[SMEM, SMEM] + [VMEM] * 8,
        out_specs=(VMEM,) * 4,
        compiler_params=params(8),
        cost_estimate=pl.CostEstimate(
            flops=200_000_000, bytes_accessed=3_000_000, transcendentals=512
        ),
        name="prep",
    )(codes, guides, sinus, roots, table, time_weight, film, conv_two, head, features)


def conv_part(planes, taps_of, weight, held, side):
    held[0:W, :] = jnp.zeros((W, 2 * C), BF16)
    held[W + HW :, :] = jnp.zeros((W, 2 * C), BF16)
    for at, values in enumerate(planes):
        held[W : W + HW, at * C : (at + 1) * C] = values.astype(BF16)
    zero = jnp.zeros((C, C), BF16)
    left = jnp.concatenate([held[row * W : row * W + HW, :] for row in range(3)], axis=1)

    def block(tap, row, col):
        at = ((tap * 3 + row) * 3 + col) * C
        return weight[at : at + C, :]

    products = []
    for col in range(3):
        right = jnp.concatenate(
            [
                jnp.concatenate(
                    [zero if tap is None else block(tap, row, col) for tap in taps], axis=1
                )
                for row in range(3)
                for taps in taps_of
            ],
            axis=0,
        )
        products.append(jnp.dot(left, right, preferred_element_type=F32))
    column = lax.broadcasted_iota(jnp.int32, (HW, C), 0) % W
    sums = []
    for plane in range(DEP_DEV):
        part = [product[:, plane * C : (plane + 1) * C] for product in products]
        side[8 : 8 + HW, :] = part[0]
        before = jnp.where(column == 0, 0.0, side[7 : 7 + HW, :])
        side[8 : 8 + HW, :] = part[2]
        after = jnp.where(column == W - 1, 0.0, side[9 : 9 + HW, :])
        sums.append(part[1] + before + after)
    return sums


def conv_scratch():
    return [pltpu.VMEM((HW + 2 * W, 2 * C), BF16), pltpu.VMEM((HW + 16, C), F32)]


def inner_kernel(every, own, weight, odd, out, norm, held, side):
    del odd
    average, scale = all_stats(every)
    shift = -average * scale
    norm[0:1, :] = scale
    norm[1:2, :] = shift
    planes = [silu(own[at].astype(F32) * scale + shift) for at in range(DEP_DEV)]
    sums = conv_part(planes, [(1, 0), (2, 1)], weight, held, side)
    for at in range(DEP_DEV):
        out[at] = sums[at]


def inner_call(every, own, weight, odd):
    return pl.pallas_call(
        inner_kernel,
        out_shape=(
            jax.ShapeDtypeStruct((DEP_DEV, HW, C), F32),
            jax.ShapeDtypeStruct((8, C), F32),
        ),
        in_specs=[VMEM] * 4,
        out_specs=(VMEM, VMEM),
        scratch_shapes=conv_scratch(),
        compiler_params=params(12),
        cost_estimate=pl.CostEstimate(
            flops=2_500_000_000, bytes_accessed=4_000_000, transcendentals=500_000
        ),
        name="inner",
    )(every, own, weight, odd)


def rim_planes(swapped):
    slab = lax.axis_index("slab")
    first = slab % 2 == 0
    low = jnp.where(first, swapped[1], swapped[0])
    high = jnp.where(first, swapped[0], swapped[1])
    return [jnp.where(slab > 0, low, 0.0), jnp.where(slab < SLABS - 1, high, 0.0)]


def outer_kernel(norm, odd, even, inner, weight, out, out_stats, out_odd, out_even, held, side):
    scale = norm[0:1, :]
    shift = norm[1:2, :]
    planes = rim_planes([silu(source[...].astype(F32) * scale + shift) for source in (even, odd)])
    sums = conv_part(planes, [(0, None), (None, 2)], weight, held, side)
    for at in range(DEP_DEV):
        out[at] = inner[at] + sums[at]
    own_stats(out[...].reshape(CELLS, C), out_stats)
    parity = lax.axis_index("slab") % 2
    out_odd[...] = out[parity].astype(BF16)
    out_even[...] = out[DEP_DEV - 1 - parity].astype(BF16)


def outer_call(norm, odd, even, inner, weight):
    return pl.pallas_call(
        outer_kernel,
        out_shape=(
            jax.ShapeDtypeStruct((DEP_DEV, HW, C), F32),
            jax.ShapeDtypeStruct((SLABS, 2, C), F32),
            jax.ShapeDtypeStruct((HW, C), BF16),
            jax.ShapeDtypeStruct((HW, C), BF16),
        ),
        in_specs=[VMEM] * 5,
        out_specs=(VMEM,) * 4,
        scratch_shapes=conv_scratch(),
        compiler_params=params(12),
        cost_estimate=pl.CostEstimate(
            flops=2_500_000_000, bytes_accessed=4_000_000, transcendentals=500_000
        ),
        name="outer",
    )(norm, odd, even, inner, weight)


def mixed(planes, weights, held):
    for at, values in enumerate(planes):
        held[:, at * C : (at + 1) * C] = values.astype(BF16)
    coarse = weights.astype(BF16).astype(F32)
    pair = jnp.concatenate([coarse, weights - coarse], axis=0).astype(BF16)
    product = dot_last(pair, held[...])
    return product[: 9 * ROWS] + product[9 * ROWS :]


def near_kernel(every, own, mod, mix, odd, out, norm, held):
    del odd
    average, scale = all_stats(every)
    factor = scale * (1.0 + mod[0:1, :C])
    shift = mod[0:1, C:] - average * factor
    norm[0:1, :] = factor
    norm[1:2, :] = shift
    planes = [silu(own[at] * factor + shift) for at in range(DEP_DEV)]
    out[...] = mixed(planes, mix[:, C : 3 * C], held)


def near_call(every, own, mod, mix, odd):
    return pl.pallas_call(
        near_kernel,
        out_shape=(
            jax.ShapeDtypeStruct((9 * ROWS, HW), F32),
            jax.ShapeDtypeStruct((8, C), F32),
        ),
        in_specs=[VMEM] * 5,
        out_specs=(VMEM, VMEM),
        scratch_shapes=[pltpu.VMEM((HW, 2 * C), BF16)],
        compiler_params=params(6),
        cost_estimate=pl.CostEstimate(
            flops=2_500_000_000, bytes_accessed=4_000_000, transcendentals=500_000
        ),
        name="near",
    )(every, own, mod, mix, odd)


def head_kernel(norm, odd, even, near, base, mix, out, held):
    factor = norm[0:1, :]
    shift = norm[1:2, :]
    planes = rim_planes([silu(source[...].astype(F32) * factor + shift) for source in (even, odd)])
    weights = jnp.concatenate([mix[:, :C], mix[:, 3 * C :]], axis=1)
    product = near[...] + mixed(planes, weights, held)
    at = lax.broadcasted_iota(jnp.int32, (ROWS, HW), 1)
    summed = base[...]
    for col in range(3):
        part = [product[(row * 3 + col) * ROWS : (row * 3 + col + 1) * ROWS] for row in range(3)]
        values = (
            part[1]
            + jnp.where(at < W, 0.0, pltpu.roll(part[0], W, 1))
            + jnp.where(at >= HW - W, 0.0, pltpu.roll(part[2], HW - W, 1))
        )
        if col == 0:
            values = jnp.where(at % W == 0, 0.0, pltpu.roll(values, 1, 1))
        if col == 2:
            values = jnp.where(at % W == W - 1, 0.0, pltpu.roll(values, HW - 1, 1))
        summed = summed + values
    for target in range(TERMS):
        piece = summed[:, target * SHARE : (target + 1) * SHARE]
        out[target] = jnp.concatenate([piece[:LAT], piece[LAT:]], axis=1)


def head_call(norm, odd, even, near, base, mix):
    return pl.pallas_call(
        head_kernel,
        out_shape=jax.ShapeDtypeStruct((TERMS, LAT, DEP_DEV * SHARE), F32),
        in_specs=[VMEM] * 6,
        out_specs=VMEM,
        scratch_shapes=[pltpu.VMEM((HW, 2 * C), BF16)],
        compiler_params=params(6),
        name="head",
    )(norm, odd, even, near, base, mix)


def final_kernel(roots, pieces, latent, guided, stepped):
    total = jnp.sum(pieces[...], axis=0)
    noise_now, root_now, root_next, noise_next = [roots[0, at * 32] for at in range(4)]
    for plane in range(DEP_DEV):
        value = total[:, plane * SHARE : (plane + 1) * SHARE]
        clean = (latent[:, plane, :] - noise_now * value) / root_now
        guided[:, plane, :] = value
        stepped[:, plane, :] = root_next * clean + noise_next * value


def final_call(roots, pieces, latent):
    shape = jax.ShapeDtypeStruct((LAT, DEP_DEV, SHARE), F32)
    return pl.pallas_call(
        final_kernel,
        out_shape=(shape, shape),
        in_specs=[VMEM, VMEM, VMEM],
        out_specs=(VMEM, VMEM),
        compiler_params=params(2),
        name="final",
    )(roots, pieces, latent)


def plan(step_value):
    frac = (step_value / 1000.0 + 0.008) / 1.008
    return jnp.cos(frac * math.pi / 2.0) ** 2


EVEN_PAIRS = [(at, at ^ 1) for at in range(SLABS)]
ODD_PAIRS = [(at, ((at + 1) ^ 1) - 1) for at in range(1, SLABS - 1)]


def per_device(
    features,
    latent,
    cond_codes,
    guide_codes,
    timestep,
    code_table,
    time_weight,
    film_weight,
    conv_one,
    conv_two,
    head_weight,
):
    planes = features.reshape(DEP_DEV, HW, C)
    time_value = timestep[0].astype(F32)
    half_width = EMB // 2
    frequency = jnp.exp(-math.log(10000.0) * jnp.arange(half_width, dtype=F32) / half_width)
    angles = time_value * frequency
    sinus = jnp.concatenate([jnp.cos(angles), jnp.sin(angles)]).reshape(1, EMB)
    now_bar = plan(time_value)
    next_bar = plan(time_value - STRIDE)
    roots = jnp.sqrt(jnp.stack([1.0 - now_bar, now_bar, next_bar, 1.0 - next_bar]))
    roots = jnp.repeat(roots, C // 4).reshape(1, C)

    odd, even = rims_call(planes)
    odd = lax.ppermute(odd, "slab", ODD_PAIRS)
    stats = stats_call(planes)
    every = lax.all_to_all(stats, "slab", 0, 0)
    even = lax.ppermute(even, "slab", EVEN_PAIRS)
    mod, base, mix, roots = prep_call(
        cond_codes,
        guide_codes,
        sinus,
        roots,
        code_table,
        time_weight,
        film_weight,
        conv_two.reshape(TAPS * C, C),
        head_weight.T,
        planes,
    )
    weight = conv_one.reshape(TAPS * C, C)
    inner, norm = inner_call(every, planes, weight, odd)
    first, stats, odd, even = outer_call(norm, odd, even, inner, weight)
    odd = lax.ppermute(odd, "slab", ODD_PAIRS)
    every = lax.all_to_all(stats, "slab", 0, 0)
    even = lax.ppermute(even, "slab", EVEN_PAIRS)
    near, norm = near_call(every, first, mod, mix, odd)
    pieces = head_call(norm, odd, even, near, base, mix)
    pieces = lax.all_to_all(pieces, "cond", 0, 0)
    return final_call(roots, pieces, latent)


def solution(mesh):
    placed = (
        P("cond", "slab", None, None, None),
        P(None, "slab", "cond"),
        P("cond", None),
        P(),
        P(),
        P(),
        P(),
        P(),
        P(),
        P(),
        P(),
    )
    return jax.shard_map(
        per_device,
        mesh=mesh,
        in_specs=placed,
        out_specs=(P(None, "slab", "cond"), P(None, "slab", "cond")),
        check_vma=False,
    )
```

time: 78.3 us -> 66.7 us (0.85)
  starting transfers between devices: 37.8 us -> 23.2 us
  blocking collectives: 0 us -> 14.2 us
  waiting for transfers between devices: 17.5 us -> 11.8 us
  local copies, waits for them, and re-layouts: 7.94 us -> 5.28 us
  Pallas kernels: 12.1 us -> 9.98 us
    all_to_all x0 -> x1, blocking collectives: none -> 14.2 us  [per_device(): pieces = lax.all_to_all(pieces, 'cond', 0, 0)]
    all_to_all x1 -> x0, starting transfers between devices: 9.15 us -> none  [per_device(): pieces = lax.all_to_all(pieces, 'cond', 0, 0)]
    all_to_all x1 -> x0, waiting for transfers between devices: 5.71 us -> none  [per_device(): pieces = lax.all_to_all(pieces, 'cond', 0, 0)]
    ppermute x4, starting transfers between devices: 9.19 us -> 4.21 us  [the longest x2 2.73 us: per_device(): even = lax.ppermute(even, 'slab', EVEN_PAIRS)]
    unnamed x36 -> x26, local copies, waits for them, and re-layouts: 7.94 us -> 5.13 us
    pallas_call x1, Pallas kernels: 2.78 us -> 0.84 us  [head_call(): pl.pallas_call(head_kernel, out_shape=jax.ShapeDtypeStruct((TERMS, LAT, D...]
    pallas_call x3 -> x6, Pallas kernels: 7.73 us -> 7.58 us  [the longest x1 2.93 us: outer_call(): pl.pallas_call(outer_kernel, out_shape=(jax.ShapeDtypeStruct((DEP_DEV, HW...]
  transfers between devices with their start and end apart: 7 -> 6, of which waited for: 3 -> 2; matrix products, arithmetic and copies ran while one was open for 1% -> 0% of each run, Pallas kernels for 2% -> 8%
where the time goes in v3:
time: 66.7 us; the launch traced here: 66.3 us
  starting transfers between devices  23.2 us (35%)
  blocking collectives  14.2 us (21%)
  waiting for transfers between devices  11.8 us (18%)
  Pallas kernels  9.98 us (15%)
  local copies, waits for them, and re-layouts  5.28 us (8%)
  between operations  1.63 us (2%)
    all_to_all x2, starting transfers between devices, per_device(): every = lax.all_to_all(stats, 'slab', 0, 0)  19 us
    all_to_all x1, blocking collectives, per_device(): pieces = lax.all_to_all(pieces, 'cond', 0, 0)  14.2 us
    all_to_all x2, waiting for transfers between devices, per_device(): every = lax.all_to_all(stats, 'slab', 0, 0)  11.8 us
    unnamed x26, local copies, waits for them, and re-layouts  5.13 us
    pallas_call x1, Pallas kernels, outer_call(): pl.pallas_call(outer_kernel, out_shape=(jax.ShapeDtypeStruct((DEP_DEV, HW...  2.93 us
    ppermute x2, starting transfers between devices, per_device(): even = lax.ppermute(even, 'slab', EVEN_PAIRS)  2.73 us
    pallas_call x1, Pallas kernels, inner_call(): pl.pallas_call(inner_kernel, out_shape=(jax.ShapeDtypeStruct((DEP_DEV, HW...  1.85 us
    pallas_call x1, Pallas kernels, prep_call(): pl.pallas_call(prep_kernel, out_shape=(jax.ShapeDtypeStruct((8, 2 * C), F...  1.55 us
  transfers between devices with their start and end apart: 6, of which 2 were waited for; matrix products, arithmetic and copies ran while one was open for 0% of the time, Pallas kernels for 8%

profile of v3, /device:TPU:1, one launch (start us, length us, event | category | flops | bytes accessed | tf_op | source)
XLA Modules:
  0.0 66.3 jit_solution(8181222699751268253)
XLA Ops:
  0.6 1.0 %copy-done = bf16[1,2,16,64,128]{4,3,2,1,0:T(8,128)(2,1)S(1)} copy-done((bf16[1,2,16,64,128]{4,3,2,1,0:T(8,128)(2,1)S(1)}, bf16[1,2,16,64,128]{4,3,2,1,0:T(8,128)(2,1)}, u32[]{:S(2)}) %copy-start) | copy-done | bytes 524312
  1.7 0.8 %collective-permute-start = (bf16[1024,128]{1,0:T(8,128)(2,1)S(1)}, bf16[1024,128]{1,0:T(8,128)(2,1)S(1)}, u32[]{:S(2)}, u32[]{:S(2)}) collective-permute-start(bf16[1024,128]{1,0:T(8,128)(2,1)S(1)} %get-tuple-element.17), channel_id=1, source_target_pairs={{1,2},{2,1},{3,4},{4,3},{5,6},{6,5},{7,8},{8,7},{9,10},{10,9},{11,... | collective-permute-start | bytes 786440 | tf_op jit(solution)/shard_map/ppermute | solution.py:451
  2.5 1.2 %stats.1 = f32[16,2,128]{2,1,0:T(2,128)} custom-call(bf16[2,1024,128]{2,1,0:T(8,128)(2,1)S(1)} %bitcast.11), custom_call_target="tpu_custom_call" | custom-call | tf_op jit(solution)/shard_map/stats/pallas_call | solution.py:98
  3.7 13.1 %all-to-all-start = ((f32[16,2,128]{2,1,0:T(2,128)}), f32[16,2,128]{2,1,0:T(2,128)S(1)}, u32[]{:S(2)}, u32[]{:S(2)}) async-start(f32[16,2,128]{2,1,0:T(2,128)} %stats.1), calls=%async_computation | async-start | bytes 32768 | tf_op jit(solution)/shard_map/all_to_all | solution.py:453
  16.8 1.4 %collective-permute-start.1 = (bf16[1024,128]{1,0:T(8,128)(2,1)S(1)}, bf16[1024,128]{1,0:T(8,128)(2,1)S(1)}, u32[]{:S(2)}, u32[]{:S(2)}) collective-permute-start(bf16[1024,128]{1,0:T(8,128)(2,1)S(1)} %get-tuple-element.19), channel_id=1, source_target_pairs={{0,1},{1,0},{2,3},{3,2},{4,5},{5,4},{6,7},{7,6},{8,9},{9,8},{10,11... | collective-permute-start | bytes 786440 | tf_op jit(solution)/shard_map/ppermute | solution.py:454
  18.8 6.8 %all-to-all-done.every = f32[16,2,128]{2,1,0:T(2,128)S(1)} async-done(((f32[16,2,128]{2,1,0:T(2,128)}), f32[16,2,128]{2,1,0:T(2,128)S(1)}, u32[]{:S(2)}, u32[]{:S(2)}) %all-to-all-start) | async-done | bytes 16416 | tf_op jit(solution)/shard_map/all_to_all | solution.py:453
  25.6 0.0 collective-permute-done.odd
  25.6 1.2 %copy-done.10 = bf16[3,3,3,128,128]{4,3,2,1,0:T(8,128)(2,1)S(1)} copy-done((bf16[3,3,3,128,128]{4,3,2,1,0:T(8,128)(2,1)S(1)}, bf16[3,3,3,128,128]{4,3,2,1,0:T(8,128)(2,1)}, u32[]{:S(2)}) %copy-start.10) | copy-done | bytes 884760
  26.8 1.8 %inner.1 = (f32[2,1024,128]{2,1,0:T(8,128)S(1)}, f32[8,128]{1,0:T(8,128)S(1)}) custom-call(f32[16,2,128]{2,1,0:T(2,128)S(1)} %all-to-all-done.every, bf16[2,1024,128]{2,1,0:T(8,128)(2,1)S(1)} %bitcast.12, bf16[3456,128]{1,0:T(8,128)(2,1)S(1)} %bitcast.17, bf16[1024,128]{1,0:T(8,128)(2,1)S(1)} %collective-permute-done.odd), custom_call_target="tpu_custom_call" | custom-call | flops 2500000000 | bytes 4000000 | tf_op jit(solution)/shard_map/inner/pallas_call | solution.py:262
  28.7 0.0 collective-permute-done.1.even
  28.7 0.0 copy-start.2
  28.7 0.0 copy-start.3
  28.7 0.0 copy-start.4
  28.7 0.0 copy-start.5
  28.7 2.9 %outer.1 = (f32[2,1024,128]{2,1,0:T(8,128)S(1)}, f32[16,2,128]{2,1,0:T(2,128)}, bf16[1024,128]{1,0:T(8,128)(2,1)S(1)}, bf16[1024,128]{1,0:T(8,128)(2,1)S(1)}) custom-call(f32[8,128]{1,0:T(8,128)S(1)} %get-tuple-element.18.norm, bf16[1024,128]{1,0:T(8,128)(2,1)S(1)} %collective-permute-done.odd, bf16[1024,128]{1,0:T(8,128)(2,1)S(1)} %collective-permute-done.1.even, ...), custom_call_target="tpu_custom_call" | custom-call | flops 2500000000 | bytes 4000000 | tf_op jit(solution)/shard_map/outer/pallas_call | solution.py:301
  31.7 1.0 %copy-done.11 = f32[2,1024,128]{2,1,0:T(8,128)} copy-done((f32[2,1024,128]{2,1,0:T(8,128)}, f32[2,1024,128]{2,1,0:T(8,128)S(1)}, u32[]{:S(2)}) %copy-start.11) | copy-done | bytes 1048600
  32.7 0.7 %collective-permute-start.2 = (bf16[1024,128]{1,0:T(8,128)(2,1)S(1)}, bf16[1024,128]{1,0:T(8,128)(2,1)S(1)}, u32[]{:S(2)}, u32[]{:S(2)}) collective-permute-start(bf16[1024,128]{1,0:T(8,128)(2,1)S(1)} %get-tuple-element.25), channel_id=1, source_target_pairs={{1,2},{2,1},{3,4},{4,3},{5,6},{6,5},{7,8},{8,7},{9,10},{10,9},{11,... | collective-permute-start | bytes 786440 | tf_op jit(solution)/shard_map/ppermute | solution.py:470
  33.6 5.9 %all-to-all-start.1 = ((f32[16,2,128]{2,1,0:T(2,128)}), f32[16,2,128]{2,1,0:T(2,128)S(1)}, u32[]{:S(2)}, u32[]{:S(2)}) async-start(f32[16,2,128]{2,1,0:T(2,128)} %get-tuple-element.21), calls=%async_computation.1 | async-start | bytes 32768 | tf_op jit(solution)/shard_map/all_to_all | solution.py:471
  39.5 1.4 %collective-permute-start.3 = (bf16[1024,128]{1,0:T(8,128)(2,1)S(1)}, bf16[1024,128]{1,0:T(8,128)(2,1)S(1)}, u32[]{:S(2)}, u32[]{:S(2)}) collective-permute-start(bf16[1024,128]{1,0:T(8,128)(2,1)S(1)} %get-tuple-element.27), channel_id=1, source_target_pairs={{0,1},{1,0},{2,3},{3,2},{4,5},{5,4},{6,7},{7,6},{8,9},{9,8},{10,11... | collective-permute-start | bytes 786440 | tf_op jit(solution)/shard_map/ppermute | solution.py:472
  40.9 0.1 maximum_sqrt_fusion
  41.0 0.1 broadcast_in_dim.3
  41.1 0.1 reshape_reshape.3.roots
  41.2 0.6 copy-done.7
  41.8 1.6 %prep.1 = (f32[8,256]{1,0:T(8,128)S(1)}, f32[8,1024]{1,0:T(8,128)S(1)}, f32[72,512]{1,0:T(8,128)S(1)}, f32[8,128]{1,0:T(8,128)S(1)}) custom-call(s32[1,8]{1,0:T(1,128)S(1)} %copy-done.8, s32[16]{0:T(128)S(1)} %copy-done.9, f32[1,256]{1,0:T(1,128)S(1)} %bitcast.15, f32[1,128]{1,0:T(1,128)S(1)} %reshape_reshape.3.roots, f32[8,16,256]{2,1,0:T(8,128)S(1)} %copy-done.5, ...), custom_call_target="tpu_custom_call" | custom-call | flops 200000000 | bytes 3000000 | tf_op jit(solution)/shard_map/prep/pallas_call | solution.py:190
  43.4 5.0 %all-to-all-done.1.every = f32[16,2,128]{2,1,0:T(2,128)S(1)} async-done(((f32[16,2,128]{2,1,0:T(2,128)}), f32[16,2,128]{2,1,0:T(2,128)S(1)}, u32[]{:S(2)}, u32[]{:S(2)}) %all-to-all-start.1) | async-done | bytes 16416 | tf_op jit(solution)/shard_map/all_to_all | solution.py:471
  48.4 1.2 %copy-done.12 = f32[2,1024,128]{2,1,0:T(8,128)S(1)} copy-done((f32[2,1024,128]{2,1,0:T(8,128)S(1)}, f32[2,1024,128]{2,1,0:T(8,128)}, u32[]{:S(2)}) %copy-start.12) | copy-done | bytes 1048600
  49.6 0.8 %near.1 = (f32[72,1024]{1,0:T(8,128)S(1)}, f32[8,128]{1,0:T(8,128)S(1)}) custom-call(f32[16,2,128]{2,1,0:T(2,128)S(1)} %all-to-all-done.1.every, f32[2,1024,128]{2,1,0:T(8,128)S(1)} %copy-done.12, f32[8,256]{1,0:T(8,128)S(1)} %get-tuple-element.23.mod, f32[72,512]{1,0:T(8,128)S(1)} %get-tuple-element.24.mix, bf16[1024,128]{1,0:T(8,128)(2,1)S(1)} %collective-permute-done.2.odd), custom_call_target="tpu_custom_call" | custom-call | flops 2500000000 | bytes 4000000 | tf_op jit(solution)/shard_map/near/pallas_call | solution.py:341
  50.4 0.0 collective-permute-done.3.even
  50.4 0.0 copy-start.6
  50.5 0.8 %head.1 = f32[16,4,128]{2,1,0:T(4,128)S(1)} custom-call(f32[8,128]{1,0:T(8,128)S(1)} %get-tuple-element.26.norm, bf16[1024,128]{1,0:T(8,128)(2,1)S(1)} %collective-permute-done.2.odd, bf16[1024,128]{1,0:T(8,128)(2,1)S(1)} %collective-permute-done.3.even, f32[72,1024]{1,0:T(8,128)S(1)} %get-tuple-element.28.near, f32[8,1024]{1,0:T(8,128)S(1)} %get-tuple-element.29.base, ...), custom_call_target="tpu_custom_call" | custom-call | tf_op jit(solution)/shard_map/head/pallas_call | solution.py:384
  51.3 14.2 %all_to_all.15.pieces = f32[16,4,128]{2,1,0:T(4,128)S(1)} all-to-all(f32[16,4,128]{2,1,0:T(4,128)S(1)} %head.1), channel_id=1, replica_groups=mesh['cond'=16,'slab'=16] {'cond'}, dimensions={0} | all-to-all | bytes 65536 | tf_op jit(solution)/shard_map/all_to_all | solution.py:475
  65.5 0.8 %final.1 = (f32[4,2,64]{2,1,0:T(2,128)}, f32[4,2,64]{2,1,0:T(2,128)}) custom-call(f32[8,128]{1,0:T(8,128)S(1)} %get-tuple-element.16.roots, f32[16,4,128]{2,1,0:T(4,128)S(1)} %all_to_all.15.pieces, f32[4,2,64]{2,1,0:T(2,128)S(1)} %copy-done.6), custom_call_target="tpu_custom_call" | custom-call | tf_op jit(solution)/shard_map/final/pallas_call | solution.py:407
  (20 shorter events, 0.1 us)
Async XLA Ops:
  0.6 1.0 %copy-start = (bf16[1,2,16,64,128]{4,3,2,1,0:T(8,128)(2,1)S(1)}, bf16[1,2,16,64,128]{4,3,2,1,0:T(8,128)(2,1)}, u32[]{:S(2)}) copy-start(bf16[1,2,16,64,128]{4,3,2,1,0:T(8,128)(2,1)} %param.11) | copy-start | bytes 1572868
  1.7 24.0 %copy-start.1 = (bf16[1,2,16,64,128]{4,3,2,1,0:T(8,128)(2,1)S(1)}, bf16[1,2,16,64,128]{4,3,2,1,0:T(8,128)(2,1)}, u32[]{:S(2)}) copy-start(bf16[1,2,16,64,128]{4,3,2,1,0:T(8,128)(2,1)} %param.11) | copy-start | bytes 1572868
  1.7 23.9 %collective-permute-start = (bf16[1024,128]{1,0:T(8,128)(2,1)S(1)}, bf16[1024,128]{1,0:T(8,128)(2,1)S(1)}, u32[]{:S(2)}, u32[]{:S(2)}) collective-permute-start(bf16[1024,128]{1,0:T(8,128)(2,1)S(1)} %get-tuple-element.17), channel_id=1, source_target_pairs={{1,2},{2,1},{3,4},{4,3},{5,6},{6,5},{7,8},{8,7},{9,10},{10,9},{11,... | collective-permute-start | bytes 786440 | tf_op jit(solution)/shard_map/ppermute | solution.py:451
  3.7 22.0 %all-to-all-start = ((f32[16,2,128]{2,1,0:T(2,128)}), f32[16,2,128]{2,1,0:T(2,128)S(1)}, u32[]{:S(2)}, u32[]{:S(2)}) async-start(f32[16,2,128]{2,1,0:T(2,128)} %stats.1), calls=%async_computation | async-start | bytes 32768 | tf_op jit(solution)/shard_map/all_to_all | solution.py:453
  16.8 11.9 %collective-permute-start.1 = (bf16[1024,128]{1,0:T(8,128)(2,1)S(1)}, bf16[1024,128]{1,0:T(8,128)(2,1)S(1)}, u32[]{:S(2)}, u32[]{:S(2)}) collective-permute-start(bf16[1024,128]{1,0:T(8,128)(2,1)S(1)} %get-tuple-element.19), channel_id=1, source_target_pairs={{0,1},{1,0},{2,3},{3,2},{4,5},{5,4},{6,7},{7,6},{8,9},{9,8},{10,11... | collective-permute-start | bytes 786440 | tf_op jit(solution)/shard_map/ppermute | solution.py:454
  25.6 1.2 %copy-start.10 = (bf16[3,3,3,128,128]{4,3,2,1,0:T(8,128)(2,1)S(1)}, bf16[3,3,3,128,128]{4,3,2,1,0:T(8,128)(2,1)}, u32[]{:S(2)}) copy-start(bf16[3,3,3,128,128]{4,3,2,1,0:T(8,128)(2,1)} %param.19) | copy-start | bytes 2654212
  28.7 12.5 %copy-start.2 = (bf16[3,3,3,128,128]{4,3,2,1,0:T(8,128)(2,1)S(1)}, bf16[3,3,3,128,128]{4,3,2,1,0:T(8,128)(2,1)}, u32[]{:S(2)}) copy-start(bf16[3,3,3,128,128]{4,3,2,1,0:T(8,128)(2,1)} %param.20) | copy-start | bytes 2654212
  28.7 12.5 %copy-start.3 = (f32[256,256]{1,0:T(8,128)S(1)}, f32[256,256]{1,0:T(8,128)}, u32[]{:S(2)}) copy-start(f32[256,256]{1,0:T(8,128)} %time_weight.1) | copy-start | bytes 786436
  28.7 12.5 %copy-start.4 = (f32[256,256]{1,0:T(8,128)S(1)}, f32[256,256]{1,0:T(8,128)}, u32[]{:S(2)}) copy-start(f32[256,256]{1,0:T(8,128)} %film.1) | copy-start | bytes 786436
  28.7 12.5 %copy-start.5 = (f32[8,16,256]{2,1,0:T(8,128)S(1)}, f32[8,16,256]{2,1,0:T(8,128)}, u32[]{:S(2)}) copy-start(f32[8,16,256]{2,1,0:T(8,128)} %table.1) | copy-start | bytes 393220
  31.7 1.0 %copy-start.11 = (f32[2,1024,128]{2,1,0:T(8,128)}, f32[2,1024,128]{2,1,0:T(8,128)S(1)}, u32[]{:S(2)}) copy-start(f32[2,1024,128]{2,1,0:T(8,128)S(1)} %get-tuple-element.22.own) | copy-start | bytes 3145732
  32.7 15.7 %collective-permute-start.2 = (bf16[1024,128]{1,0:T(8,128)(2,1)S(1)}, bf16[1024,128]{1,0:T(8,128)(2,1)S(1)}, u32[]{:S(2)}, u32[]{:S(2)}) collective-permute-start(bf16[1024,128]{1,0:T(8,128)(2,1)S(1)} %get-tuple-element.25), channel_id=1, source_target_pairs={{1,2},{2,1},{3,4},{4,3},{5,6},{6,5},{7,8},{8,7},{9,10},{10,9},{11,... | collective-permute-start | bytes 786440 | tf_op jit(solution)/shard_map/ppermute | solution.py:470
  33.6 14.8 %all-to-all-start.1 = ((f32[16,2,128]{2,1,0:T(2,128)}), f32[16,2,128]{2,1,0:T(2,128)S(1)}, u32[]{:S(2)}, u32[]{:S(2)}) async-start(f32[16,2,128]{2,1,0:T(2,128)} %get-tuple-element.21), calls=%async_computation.1 | async-start | bytes 32768 | tf_op jit(solution)/shard_map/all_to_all | solution.py:471
  39.5 10.9 %collective-permute-start.3 = (bf16[1024,128]{1,0:T(8,128)(2,1)S(1)}, bf16[1024,128]{1,0:T(8,128)(2,1)S(1)}, u32[]{:S(2)}, u32[]{:S(2)}) collective-permute-start(bf16[1024,128]{1,0:T(8,128)(2,1)S(1)} %get-tuple-element.27), channel_id=1, source_target_pairs={{0,1},{1,0},{2,3},{3,2},{4,5},{5,4},{6,7},{7,6},{8,9},{9,8},{10,11... | collective-permute-start | bytes 786440 | tf_op jit(solution)/shard_map/ppermute | solution.py:472
  41.1 0.7 %copy-start.7 = (f32[128,4]{0,1:T(4,128)S(1)}, f32[128,4]{0,1:T(4,128)}, u32[]{:S(2)}) copy-start(f32[128,4]{0,1:T(4,128)} %param.21) | copy-start | bytes 6148
  41.1 0.7 %copy-start.8 = (s32[1,8]{1,0:T(1,128)S(1)}, s32[1,8]{1,0:T(1,128)}, u32[]{:S(2)}) copy-start(s32[1,8]{1,0:T(1,128)} %codes.1) | copy-start | bytes 100
  41.1 0.7 %copy-start.9 = (s32[16]{0:T(128)S(1)}, s32[16]{0:T(128)}, u32[]{:S(2)}) copy-start(s32[16]{0:T(128)} %guides.1) | copy-start | bytes 196
  48.4 1.2 %copy-start.12 = (f32[2,1024,128]{2,1,0:T(8,128)S(1)}, f32[2,1024,128]{2,1,0:T(8,128)}, u32[]{:S(2)}) copy-start(f32[2,1024,128]{2,1,0:T(8,128)} %copy-done.11) | copy-start | bytes 3145732
  50.4 15.0 %copy-start.6 = (f32[4,2,64]{2,1,0:T(2,128)S(1)}, f32[4,2,64]{2,1,0:T(2,128)}, u32[]{:S(2)}) copy-start(f32[4,2,64]{2,1,0:T(2,128)} %latent.1) | copy-start | bytes 6148

commit v4 on v3

v4 whole, which is shorter than its diff:
```python
import math

import jax
import jax.numpy as jnp
from jax import lax
from jax.experimental import pallas as pl
from jax.experimental.pallas import tpu as pltpu
from jax.sharding import PartitionSpec as P

C = 128
GROUPS = 32
PER_GROUP = C // GROUPS
EMB = 256
LAT = 4
SLOTS = 8
CODES = 16
STRIDE = 20
DEP_DEV = 2
H = 16
W = 64
HW = H * W
TERMS = 16
SHARE = HW // TERMS
SLABS = 16
CELLS = DEP_DEV * HW
MEMBERS = float(SLABS * CELLS * PER_GROUP)
TAPS = 27
F32 = jnp.float32
BF16 = jnp.bfloat16
ROWS = 2 * LAT

VMEM = pl.BlockSpec(memory_space=pltpu.VMEM)


def params(mebibytes):
    return pltpu.CompilerParams(vmem_limit_bytes=mebibytes * 1024 * 1024)


def cost(gigaflops, mebibytes):
    return pl.CostEstimate(
        flops=gigaflops * 10**9, bytes_accessed=mebibytes * 2**20, transcendentals=0
    )


def dot_last(left, right):
    return lax.dot_general(left, right, (((1,), (1,)), ((), ())), preferred_element_type=F32)


def silu(values):
    half = 0.5 * values
    return half + half * jnp.tanh(half)


def column_sum(values):
    partial = jnp.sum(values.reshape(-1, W, C), axis=0)
    return jnp.sum(partial, axis=0, keepdims=True)


def own_stats(values, out_ref):
    pivot = jnp.sum(values[:W], axis=0, keepdims=True) * (1.0 / W)
    apart = values - pivot
    total = column_sum(apart)
    square = column_sum(apart * apart) - total * total * (1.0 / CELLS)
    both = jnp.concatenate([total + CELLS * pivot, square], axis=0)
    out_ref[...] = jnp.broadcast_to(both[None], (SLABS, 2, C))


def over_group(values):
    lane = lax.broadcasted_iota(jnp.int32, values.shape, 1)
    for step in (1, 2):
        other = jnp.where(
            lane // step % 2 == 0, pltpu.roll(values, C - step, 1), pltpu.roll(values, step, 1)
        )
        values = values + other
    return values


def three_parts(values):
    high = values.astype(BF16).astype(F32)
    rest = values - high
    middle = rest.astype(BF16).astype(F32)
    low = rest - middle
    zero = jnp.zeros_like(values)
    return jnp.concatenate([high, middle, low, zero], axis=0).astype(BF16)


def all_stats(every_ref):
    every = every_ref[...]
    totals = every[:, 0, :]
    squares = every[:, 1, :]
    average = over_group(jnp.sum(totals, axis=0, keepdims=True)) / MEMBERS
    apart = totals * (1.0 / CELLS) - average
    spread = (
        over_group(jnp.sum(squares + CELLS * (apart * apart), axis=0, keepdims=True))
        / MEMBERS
    )
    return average, 1.0 / jnp.sqrt(spread + 1e-05)


def stats_kernel(features, out):
    own_stats(features[...].reshape(CELLS, C).astype(F32), out)


def stats_call(features):
    return pl.pallas_call(
        stats_kernel,
        out_shape=jax.ShapeDtypeStruct((SLABS, 2, C), F32),
        in_specs=[VMEM],
        out_specs=VMEM,
        compiler_params=params(4),
        cost_estimate=cost(2, 1),
        name="stats",
    )(features)


def rims_kernel(planes, step, even, odd, time):
    time[...] = jnp.broadcast_to(step[...].astype(F32).reshape(1, 1), (8, C))
    parity = lax.axis_index("slab") % 2
    even[...] = planes[DEP_DEV - 1 - parity]
    odd[...] = planes[parity]


def rims_call(planes, step):
    plane = jax.ShapeDtypeStruct((HW, C), BF16)
    return pl.pallas_call(
        rims_kernel,
        out_shape=(plane, plane, jax.ShapeDtypeStruct((8, C), F32)),
        in_specs=[VMEM, VMEM],
        out_specs=(VMEM, VMEM, VMEM),
        compiler_params=params(4),
        cost_estimate=cost(2, 1),
        name="rims",
    )(planes, step)


def exact(left, right):
    parts = three_parts(left)
    coarse = right.astype(BF16)
    fine = (right - coarse.astype(F32)).astype(BF16)
    product = jnp.dot(parts, coarse, preferred_element_type=F32) + jnp.dot(
        parts, fine, preferred_element_type=F32
    )
    return three_sum(product)


def plan(step_value):
    frac = (step_value / 1000.0 + 0.008) / 1.008
    return jnp.cos(frac * (math.pi / 2.0)) ** 2


def sampler_roots(time_value):
    now_bar = plan(time_value)
    next_bar = plan(time_value - STRIDE)
    return jnp.sqrt(
        jnp.concatenate([1.0 - now_bar, now_bar, next_bar, 1.0 - next_bar], axis=0)
    )


def modulate(time_value, codes, table, time_weight, film):
    lane = lax.broadcasted_iota(jnp.int32, (1, EMB // 2), 1)
    angles = time_value * jnp.exp(
        -math.log(10000.0) * lane.astype(F32) / (EMB // 2)
    )
    sinus = jnp.concatenate([jnp.cos(angles), jnp.sin(angles)], axis=1)
    wanted = jnp.zeros((1, SLOTS * CODES), jnp.int32)
    for slot in range(SLOTS):
        wanted = jnp.where(lane // CODES == slot, codes[0:1, slot : slot + 1], wanted)
    one_hot = (lane % CODES == wanted).astype(F32)
    rows = jnp.broadcast_to(jnp.concatenate([sinus, one_hot], axis=1), (8, EMB + SLOTS * CODES))
    tables = jnp.concatenate([time_weight[...], table[...]], axis=0)
    embedding = silu(exact(rows, tables))
    return exact(embedding, film[...])[:1]


def own_weight(guides):
    term = lax.axis_index("cond")
    lane = lax.broadcasted_iota(jnp.int32, (1, TERMS), 1)
    values = guides[...].astype(F32)
    others = jnp.sum(jnp.where(lane == 0, 0.0, values), axis=1, keepdims=True)
    mine = jnp.sum(jnp.where(lane == term, values, 0.0), axis=1, keepdims=True)
    return jnp.where(term == 0, TERMS - others, mine) * (1.0 / 16.0)


def three_sum(product):
    return product[:ROWS] + (product[ROWS : 2 * ROWS] + product[2 * ROWS : 3 * ROWS])


def compose(conv_two, head, weight):
    head_rows = jnp.concatenate([head[...], head[...]], axis=0)
    upper = lax.broadcasted_iota(jnp.int32, (ROWS, C), 0) < LAT
    composed = three_sum(dot_last(three_parts(head_rows), conv_two[...])) * weight
    nothing = jnp.zeros((ROWS, C), F32)
    rows = []
    for near in range(9):
        blocks = []
        for plane in range(DEP_DEV + 2):
            at = [
                composed[:, (tap * 9 + near) * C : (tap * 9 + near + 1) * C]
                if 0 <= tap < 3
                else nothing
                for tap in (plane, plane - 1)
            ]
            blocks.append(jnp.where(upper, at[0], at[1]))
        rows.append(jnp.concatenate(blocks, axis=1))
    return jnp.concatenate(rows, axis=0)


def direct(features, head, weight):
    head_rows = jnp.concatenate([head[...], head[...]], axis=0)
    upper = lax.broadcasted_iota(jnp.int32, (ROWS, C), 0) < LAT
    wide = jnp.concatenate(
        [jnp.where(upper, head_rows, 0.0), jnp.where(upper, 0.0, head_rows)], axis=1
    )
    both = jnp.concatenate([features[0], features[1]], axis=1)
    return three_sum(dot_last(three_parts(wide), both)) * weight


def conv_part(planes, taps_of, weight, held, side):
    held[0:W, :] = jnp.zeros((W, len(planes) * C), BF16)
    held[W + HW :, :] = jnp.zeros((W, len(planes) * C), BF16)
    for at, values in enumerate(planes):
        held[W : W + HW, at * C : (at + 1) * C] = values.astype(BF16)
    zero = jnp.zeros((C, C), BF16)
    depth = len(planes) * C

    def block(tap, row, col):
        at = ((tap * 3 + row) * 3 + col) * C
        return weight[at : at + C, :]

    products = []
    for col in range(3):
        right = jnp.concatenate(
            [
                jnp.concatenate(
                    [zero if tap is None else block(tap, row, col) for tap in taps], axis=1
                )
                for row in range(3)
                for taps in taps_of
            ],
            axis=0,
        )
        products.append(
            sum(
                jnp.dot(
                    held[row * W : row * W + HW, :],
                    right[row * depth : (row + 1) * depth],
                    preferred_element_type=F32,
                )
                for row in range(3)
            )
        )
    column = lax.broadcasted_iota(jnp.int32, (HW, C), 0) % W
    sums = []
    for plane in range(DEP_DEV):
        part = [product[:, plane * C : (plane + 1) * C] for product in products]
        side[8 : 8 + HW, :] = part[0]
        before = jnp.where(column == 0, 0.0, side[7 : 7 + HW, :])
        side[8 : 8 + HW, :] = part[2]
        after = jnp.where(column == W - 1, 0.0, side[9 : 9 + HW, :])
        sums.append(part[1] + before + after)
    return sums


def conv_scratch():
    return [pltpu.VMEM((HW + 2 * W, 4 * C), BF16), pltpu.VMEM((HW + 16, C), F32)]


def rim_planes(swapped):
    slab = lax.axis_index("slab")
    first = slab % 2 == 0
    low = jnp.where(first, swapped[1], swapped[0])
    high = jnp.where(first, swapped[0], swapped[1])
    return [jnp.where(slab > 0, low, 0.0), jnp.where(slab < SLABS - 1, high, 0.0)]


def conv_kernel(every, even, odd, own, weight, out, out_stats, out_even, out_odd, held, side):
    average, scale = all_stats(every)
    shift = -average * scale

    def act(values):
        return silu(values.astype(F32) * scale + shift)

    low, high = rim_planes([act(even[...]), act(odd[...])])
    planes = [low, act(own[0]), act(own[1]), high]
    sums = conv_part(planes, [(0, None), (1, 0), (2, 1), (None, 2)], weight, held, side)
    for at in range(DEP_DEV):
        out[at] = sums[at]
    own_stats(out[...].reshape(CELLS, C), out_stats)
    parity = lax.axis_index("slab") % 2
    out_even[...] = out[DEP_DEV - 1 - parity].astype(BF16)
    out_odd[...] = out[parity].astype(BF16)


def conv_call(every, even, odd, own, weight):
    plane = jax.ShapeDtypeStruct((HW, C), BF16)
    return pl.pallas_call(
        conv_kernel,
        out_shape=(
            jax.ShapeDtypeStruct((DEP_DEV, HW, C), F32),
            jax.ShapeDtypeStruct((SLABS, 2, C), F32),
            plane,
            plane,
        ),
        in_specs=[VMEM] * 5,
        out_specs=(VMEM,) * 4,
        scratch_shapes=conv_scratch(),
        compiler_params=params(16),
        cost_estimate=cost(2, 32),
        name="conv",
    )(every, even, odd, own, weight)


def mixed(planes, weights, held):
    for at, values in enumerate(planes):
        held[:, at * C : (at + 1) * C] = values.astype(BF16)
    coarse = weights.astype(BF16).astype(F32)
    pair = jnp.concatenate([coarse, weights - coarse], axis=0).astype(BF16)
    product = dot_last(pair, held[...])
    return product[: 9 * ROWS] + product[9 * ROWS :]


def head_kernel(
    every,
    even,
    odd,
    own,
    features,
    time,
    codes,
    guides,
    table,
    time_weight,
    film,
    conv_two,
    head,
    out,
    roots,
    held,
):
    time_value = time[0:1, :]
    roots[...] = sampler_roots(time_value)
    mod = modulate(time_value, codes, table, time_weight, film)
    weight = own_weight(guides)
    mix = compose(conv_two, head, weight)
    base = direct(features, head, weight)
    average, scale = all_stats(every)
    factor = scale * (1.0 + mod[:, :C])
    shift = mod[:, C:] - average * factor

    def act(values):
        return silu(values.astype(F32) * factor + shift)

    low, high = rim_planes([act(even[...]), act(odd[...])])
    product = mixed([low, act(own[0]), act(own[1]), high], mix, held)
    at = lax.broadcasted_iota(jnp.int32, (ROWS, HW), 1)
    summed = base
    for col in range(3):
        part = [product[(row * 3 + col) * ROWS : (row * 3 + col + 1) * ROWS] for row in range(3)]
        values = (
            part[1]
            + jnp.where(at < W, 0.0, pltpu.roll(part[0], W, 1))
            + jnp.where(at >= HW - W, 0.0, pltpu.roll(part[2], HW - W, 1))
        )
        if col == 0:
            values = jnp.where(at % W == 0, 0.0, pltpu.roll(values, 1, 1))
        if col == 2:
            values = jnp.where(at % W == W - 1, 0.0, pltpu.roll(values, HW - 1, 1))
        summed = summed + values
    for target in range(TERMS):
        piece = summed[:, target * SHARE : (target + 1) * SHARE]
        out[target] = jnp.concatenate([piece[:LAT], piece[LAT:]], axis=1)


def head_call(*operands):
    return pl.pallas_call(
        head_kernel,
        out_shape=(
            jax.ShapeDtypeStruct((TERMS, LAT, DEP_DEV * SHARE), F32),
            jax.ShapeDtypeStruct((4, C), F32),
        ),
        in_specs=[VMEM] * len(operands),
        out_specs=(VMEM, VMEM),
        scratch_shapes=[pltpu.VMEM((HW, 4 * C), BF16)],
        compiler_params=params(12),
        cost_estimate=cost(1, 32),
        name="head",
    )(*operands)


def final_kernel(roots, pieces, latent, guided, stepped):
    total = jnp.sum(pieces[...], axis=0)
    noise_now, root_now, root_next, noise_next = [roots[at : at + 1, :SHARE] for at in range(4)]
    for plane in range(DEP_DEV):
        value = total[:, plane * SHARE : (plane + 1) * SHARE]
        clean = (latent[:, plane, :] - noise_now * value) / root_now
        guided[:, plane, :] = value
        stepped[:, plane, :] = root_next * clean + noise_next * value


def final_call(roots, pieces, latent):
    shape = jax.ShapeDtypeStruct((LAT, DEP_DEV, SHARE), F32)
    return pl.pallas_call(
        final_kernel,
        out_shape=(shape, shape),
        in_specs=[VMEM, VMEM, VMEM],
        out_specs=(VMEM, VMEM),
        compiler_params=params(2),
        name="final",
    )(roots, pieces, latent)


EVEN_PAIRS = [(at, at ^ 1) for at in range(SLABS)]
ODD_PAIRS = [(at, ((at + 1) ^ 1) - 1) for at in range(1, SLABS - 1)]


def per_device(
    features,
    latent,
    cond_codes,
    guide_codes,
    timestep,
    code_table,
    time_weight,
    film_weight,
    conv_one,
    conv_two,
    head_weight,
):
    planes = features.reshape(DEP_DEV, HW, C)
    even, odd, time = rims_call(planes, timestep)
    even = lax.ppermute(even, "slab", EVEN_PAIRS)
    odd = lax.ppermute(odd, "slab", ODD_PAIRS)
    every = lax.all_to_all(stats_call(planes), "slab", 0, 0)
    first, stats, even, odd = conv_call(
        every, even, odd, planes, conv_one.reshape(TAPS * C, C)
    )
    even = lax.ppermute(even, "slab", EVEN_PAIRS)
    odd = lax.ppermute(odd, "slab", ODD_PAIRS)
    every = lax.all_to_all(stats, "slab", 0, 0)
    pieces, roots = head_call(
        every,
        even,
        odd,
        first,
        planes,
        time,
        cond_codes,
        guide_codes.reshape(1, TERMS),
        code_table.reshape(SLOTS * CODES, EMB),
        time_weight,
        film_weight,
        conv_two.reshape(TAPS * C, C),
        head_weight.T,
    )
    pieces = lax.all_to_all(pieces, "cond", 0, 0)
    return final_call(roots, pieces, latent)


def solution(mesh):
    placed = (
        P("cond", "slab", None, None, None),
        P(None, "slab", "cond"),
        P("cond", None),
        P(),
        P(),
        P(),
        P(),
        P(),
        P(),
        P(),
        P(),
    )
    return jax.shard_map(
        per_device,
        mesh=mesh,
        in_specs=placed,
        out_specs=(P(None, "slab", "cond"), P(None, "slab", "cond")),
        check_vma=False,
    )
```

time: 66.7 us -> 64.1 us (0.961)
  blocking collectives: 14.2 us -> 49.7 us
  starting transfers between devices: 23.2 us -> 4.4 us
  waiting for transfers between devices: 11.8 us -> 0.01 us
  local copies, waits for them, and re-layouts: 5.28 us -> 1.7 us
  Pallas kernels: 9.98 us -> 6.56 us
    all_to_all x0 -> x2, blocking collectives: none -> 35.1 us  [the longest x1 20 us: per_device(): every = lax.all_to_all(stats_call(planes), 'slab', 0, 0)]
    all_to_all x2 -> x0, starting transfers between devices: 19 us -> none  [per_device(): every = lax.all_to_all(stats, 'slab', 0, 0)]
    all_to_all x2 -> x0, waiting for transfers between devices: 11.8 us -> none  [per_device(): every = lax.all_to_all(stats, 'slab', 0, 0)]
    unnamed x26 -> x22, local copies, waits for them, and re-layouts: 5.13 us -> 1.7 us
    pallas_call x6 -> x3, Pallas kernels: 8.04 us -> 5.57 us  [the longest x1 3.79 us: conv_call(): pl.pallas_call(conv_kernel, out_shape=(jax.ShapeDtypeStruct((DEP_DEV, HW,...]
    pallas_call x1, Pallas kernels: 1.16 us -> 0.3 us  [stats_call(): pl.pallas_call(stats_kernel, out_shape=jax.ShapeDtypeStruct((SLABS, 2, C)...]
  transfers between devices with their start and end apart: 6 -> 4, of which waited for: 2 -> 0; matrix products, arithmetic and copies ran while one was open for 0% -> 0% of each run, Pallas kernels for 8% -> 0%
where the time goes in v4:
time: 64.1 us; the launch traced here: 63.8 us
  blocking collectives  49.7 us (78%)
  Pallas kernels  6.56 us (10%)
  starting transfers between devices  4.4 us (7%)
  local copies, waits for them, and re-layouts  1.7 us (3%)
  between operations  1.42 us (2%)
    all_to_all x1, blocking collectives, per_device(): every = lax.all_to_all(stats_call(planes), 'slab', 0, 0)  20 us
    all_to_all x1, blocking collectives, per_device(): every = lax.all_to_all(stats, 'slab', 0, 0)  15.1 us
    all_to_all x1, blocking collectives, per_device(): pieces = lax.all_to_all(pieces, 'cond', 0, 0)  14.6 us
    pallas_call x1, Pallas kernels, conv_call(): pl.pallas_call(conv_kernel, out_shape=(jax.ShapeDtypeStruct((DEP_DEV, HW,...  3.79 us
    ppermute x2, starting transfers between devices, per_device(): even = lax.ppermute(even, 'slab', EVEN_PAIRS)  2.93 us
    pallas_call x1, Pallas kernels, head_call(): pl.pallas_call(head_kernel, out_shape=(jax.ShapeDtypeStruct((TERMS, LAT,...  1.71 us
    unnamed x22, local copies, waits for them, and re-layouts  1.7 us
    ppermute x2, starting transfers between devices, per_device(): odd = lax.ppermute(odd, 'slab', ODD_PAIRS)  1.46 us
  transfers between devices with their start and end apart: 4, of which 0 were waited for; matrix products, arithmetic and copies ran while one was open for 0% of the time, Pallas kernels for 0%

profile of v4, /device:TPU:1, one launch (start us, length us, event | category | flops | bytes accessed | tf_op | source)
XLA Modules:
  0.0 63.8 jit_solution(6184516826727060509)
XLA Ops:
  1.3 0.0 copy-start.3
  1.3 1.0 %copy-done.3 = bf16[1,2,16,64,128]{4,3,2,1,0:T(8,128)(2,1)S(1)} copy-done((bf16[1,2,16,64,128]{4,3,2,1,0:T(8,128)(2,1)S(1)}, bf16[1,2,16,64,128]{4,3,2,1,0:T(8,128)(2,1)}, u32[]{:S(2)}) %copy-start.3) | copy-done | bytes 524312
  2.3 0.1 rims.1
  2.4 2.5 %collective-permute-start = (bf16[1024,128]{1,0:T(8,128)(2,1)S(1)}, bf16[1024,128]{1,0:T(8,128)(2,1)S(1)}, u32[]{:S(2)}, u32[]{:S(2)}) collective-permute-start(bf16[1024,128]{1,0:T(8,128)(2,1)S(1)} %get-tuple-element.11), channel_id=1, source_target_pairs={{0,1},{1,0},{2,3},{3,2},{4,5},{5,4},{6,7},{7,6},{8,9},{9,8},{10,11... | collective-permute-start | bytes 786440 | tf_op jit(solution)/shard_map/ppermute | solution.py:431
  4.9 0.8 %collective-permute-start.1 = (bf16[1024,128]{1,0:T(8,128)(2,1)S(1)}, bf16[1024,128]{1,0:T(8,128)(2,1)S(1)}, u32[]{:S(2)}, u32[]{:S(2)}) collective-permute-start(bf16[1024,128]{1,0:T(8,128)(2,1)S(1)} %get-tuple-element.12), channel_id=1, source_target_pairs={{1,2},{2,1},{3,4},{4,3},{5,6},{6,5},{7,8},{8,7},{9,10},{10,9},{11,... | collective-permute-start | bytes 786440 | tf_op jit(solution)/shard_map/ppermute | solution.py:432
  5.7 0.3 stats.1
  6.0 20.0 %all_to_all.15.every = f32[16,2,128]{2,1,0:T(2,128)S(1)} all-to-all(f32[16,2,128]{2,1,0:T(2,128)S(1)} %stats.1), channel_id=1, replica_groups=mesh['cond'=16,'slab'=16] {'slab'}, dimensions={0} | all-to-all | bytes 32768 | tf_op jit(solution)/shard_map/all_to_all | solution.py:433
  26.0 0.0 collective-permute-done.even
  26.0 0.0 collective-permute-done.1.odd
  26.1 0.0 copy-done.1
  26.1 0.0 copy-done.4
  26.1 0.0 copy-start.2
  26.1 0.0 copy-start.5
  26.1 0.0 copy-start.6
  26.1 0.0 copy-start.7
  26.1 3.8 %conv.1 = (f32[2,1024,128]{2,1,0:T(8,128)S(1)}, f32[16,2,128]{2,1,0:T(2,128)S(1)}, bf16[1024,128]{1,0:T(8,128)(2,1)S(1)}, bf16[1024,128]{1,0:T(8,128)(2,1)S(1)}) custom-call(f32[16,2,128]{2,1,0:T(2,128)S(1)} %all_to_all.15.every, bf16[1024,128]{1,0:T(8,128)(2,1)S(1)} %collective-permute-done.even, bf16[1024,128]{1,0:T(8,128)(2,1)S(1)} %collective-permute-done.1.odd, ...), custom_call_target="tpu_custom_call" | custom-call | flops 2000000000 | bytes 33554432 | tf_op jit(solution)/shard_map/conv/pallas_call | solution.py:296
  29.9 0.4 collective-permute-start.2
  30.3 0.7 %collective-permute-start.3 = (bf16[1024,128]{1,0:T(8,128)(2,1)S(1)}, bf16[1024,128]{1,0:T(8,128)(2,1)S(1)}, u32[]{:S(2)}, u32[]{:S(2)}) collective-permute-start(bf16[1024,128]{1,0:T(8,128)(2,1)S(1)} %get-tuple-element.15), channel_id=1, source_target_pairs={{1,2},{2,1},{3,4},{4,3},{5,6},{6,5},{7,8},{8,7},{9,10},{10,9},{11,... | collective-permute-start | bytes 786440 | tf_op jit(solution)/shard_map/ppermute | solution.py:438
  31.0 15.1 %all_to_all.16.every = f32[16,2,128]{2,1,0:T(2,128)S(1)} all-to-all(f32[16,2,128]{2,1,0:T(2,128)S(1)} %get-tuple-element.13), channel_id=1, replica_groups=mesh['cond'=16,'slab'=16] {'slab'}, dimensions={0} | all-to-all | bytes 32768 | tf_op jit(solution)/shard_map/all_to_all | solution.py:439
  46.1 0.0 collective-permute-done.2.even
  46.1 0.0 collective-permute-done.3.odd
  46.1 0.0 copy-start.9
  46.1 0.0 copy-start.10
  46.1 0.0 copy-done.2
  46.2 0.0 copy-done.5
  46.2 0.0 copy-done.6
  46.2 0.6 copy-done.8
  46.8 0.0 copy-done.9
  46.8 1.7 %head.1 = (f32[16,4,128]{2,1,0:T(4,128)S(1)}, f32[4,128]{1,0:T(4,128)S(1)}) custom-call(f32[16,2,128]{2,1,0:T(2,128)S(1)} %all_to_all.16.every, bf16[1024,128]{1,0:T(8,128)(2,1)S(1)} %collective-permute-done.2.even, bf16[1024,128]{1,0:T(8,128)(2,1)S(1)} %collective-permute-done.3.odd, f32[2,1024,128]{2,1,0:T(8,128)S(1)} %get-tuple-element.16.own, ...), custom_call_target="tpu_custom_call" | custom-call | flops 1000000000 | bytes 33554432 | tf_op jit(solution)/shard_map/head/pallas_call | solution.py:375
  48.5 14.6 %all_to_all.17.pieces = f32[16,4,128]{2,1,0:T(4,128)S(1)} all-to-all(f32[16,4,128]{2,1,0:T(4,128)S(1)} %get-tuple-element.19), channel_id=1, replica_groups=mesh['cond'=16,'slab'=16] {'cond'}, dimensions={0} | all-to-all | bytes 65536 | tf_op jit(solution)/shard_map/all_to_all | solution.py:455
  63.1 0.0 copy-done
  63.1 0.7 %final.1 = (f32[4,2,64]{2,1,0:T(2,128)}, f32[4,2,64]{2,1,0:T(2,128)}) custom-call(f32[4,128]{1,0:T(4,128)S(1)} %get-tuple-element.18.roots, f32[16,4,128]{2,1,0:T(4,128)S(1)} %all_to_all.17.pieces, f32[4,2,64]{2,1,0:T(2,128)S(1)} %copy-done), custom_call_target="tpu_custom_call" | custom-call | tf_op jit(solution)/shard_map/final/pallas_call | solution.py:402
  (6 shorter events, 0.0 us)
Async XLA Ops:
  1.3 1.0 %copy-start.3 = (bf16[1,2,16,64,128]{4,3,2,1,0:T(8,128)(2,1)S(1)}, bf16[1,2,16,64,128]{4,3,2,1,0:T(8,128)(2,1)}, u32[]{:S(2)}) copy-start(bf16[1,2,16,64,128]{4,3,2,1,0:T(8,128)(2,1)} %param.11) | copy-start | bytes 1572868
  2.4 23.7 %collective-permute-start = (bf16[1024,128]{1,0:T(8,128)(2,1)S(1)}, bf16[1024,128]{1,0:T(8,128)(2,1)S(1)}, u32[]{:S(2)}, u32[]{:S(2)}) collective-permute-start(bf16[1024,128]{1,0:T(8,128)(2,1)S(1)} %get-tuple-element.11), channel_id=1, source_target_pairs={{0,1},{1,0},{2,3},{3,2},{4,5},{5,4},{6,7},{7,6},{8,9},{9,8},{10,11... | collective-permute-start | bytes 786440 | tf_op jit(solution)/shard_map/ppermute | solution.py:431
  4.9 21.1 %copy-start.1 = (bf16[3,3,3,128,128]{4,3,2,1,0:T(8,128)(2,1)S(1)}, bf16[3,3,3,128,128]{4,3,2,1,0:T(8,128)(2,1)}, u32[]{:S(2)}) copy-start(bf16[3,3,3,128,128]{4,3,2,1,0:T(8,128)(2,1)} %param.19) | copy-start | bytes 2654212
  4.9 21.1 %copy-start.4 = (bf16[1,2,16,64,128]{4,3,2,1,0:T(8,128)(2,1)S(1)}, bf16[1,2,16,64,128]{4,3,2,1,0:T(8,128)(2,1)}, u32[]{:S(2)}) copy-start(bf16[1,2,16,64,128]{4,3,2,1,0:T(8,128)(2,1)} %param.11) | copy-start | bytes 1572868
  4.9 21.1 %collective-permute-start.1 = (bf16[1024,128]{1,0:T(8,128)(2,1)S(1)}, bf16[1024,128]{1,0:T(8,128)(2,1)S(1)}, u32[]{:S(2)}, u32[]{:S(2)}) collective-permute-start(bf16[1024,128]{1,0:T(8,128)(2,1)S(1)} %get-tuple-element.12), channel_id=1, source_target_pairs={{1,2},{2,1},{3,4},{4,3},{5,6},{6,5},{7,8},{8,7},{9,10},{10,9},{11,... | collective-permute-start | bytes 786440 | tf_op jit(solution)/shard_map/ppermute | solution.py:432
  26.1 20.1 %copy-start.2 = (bf16[3,3,3,128,128]{4,3,2,1,0:T(8,128)(2,1)S(1)}, bf16[3,3,3,128,128]{4,3,2,1,0:T(8,128)(2,1)}, u32[]{:S(2)}) copy-start(bf16[3,3,3,128,128]{4,3,2,1,0:T(8,128)(2,1)} %param.20) | copy-start | bytes 2654212
  26.1 20.1 %copy-start.5 = (f32[256,256]{1,0:T(8,128)S(1)}, f32[256,256]{1,0:T(8,128)}, u32[]{:S(2)}) copy-start(f32[256,256]{1,0:T(8,128)} %time_weight.1) | copy-start | bytes 786436
  26.1 20.1 %copy-start.6 = (f32[256,256]{1,0:T(8,128)S(1)}, f32[256,256]{1,0:T(8,128)}, u32[]{:S(2)}) copy-start(f32[256,256]{1,0:T(8,128)} %film.1) | copy-start | bytes 786436
  26.1 20.1 %copy-start.7 = (f32[8,16,256]{2,1,0:T(8,128)S(1)}, f32[8,16,256]{2,1,0:T(8,128)}, u32[]{:S(2)}) copy-start(f32[8,16,256]{2,1,0:T(8,128)} %param.16) | copy-start | bytes 393220
  29.9 16.2 %collective-permute-start.2 = (bf16[1024,128]{1,0:T(8,128)(2,1)S(1)}, bf16[1024,128]{1,0:T(8,128)(2,1)S(1)}, u32[]{:S(2)}, u32[]{:S(2)}) collective-permute-start(bf16[1024,128]{1,0:T(8,128)(2,1)S(1)} %get-tuple-element.14), channel_id=1, source_target_pairs={{0,1},{1,0},{2,3},{3,2},{4,5},{5,4},{6,7},{7,6},{8,9},{9,8},{10,11... | collective-permute-start | bytes 786440 | tf_op jit(solution)/shard_map/ppermute | solution.py:437
  30.3 15.8 %collective-permute-start.3 = (bf16[1024,128]{1,0:T(8,128)(2,1)S(1)}, bf16[1024,128]{1,0:T(8,128)(2,1)S(1)}, u32[]{:S(2)}, u32[]{:S(2)}) collective-permute-start(bf16[1024,128]{1,0:T(8,128)(2,1)S(1)} %get-tuple-element.15), channel_id=1, source_target_pairs={{1,2},{2,1},{3,4},{4,3},{5,6},{6,5},{7,8},{8,7},{9,10},{10,9},{11,... | collective-permute-start | bytes 786440 | tf_op jit(solution)/shard_map/ppermute | solution.py:438
  46.1 0.7 %copy-start.8 = (f32[128,4]{0,1:T(4,128)S(1)}, f32[128,4]{0,1:T(4,128)}, u32[]{:S(2)}) copy-start(f32[128,4]{0,1:T(4,128)} %param.21) | copy-start | bytes 6148
  46.1 0.7 %copy-start.9 = (s32[1,8]{1,0:T(1,128)S(1)}, s32[1,8]{1,0:T(1,128)}, u32[]{:S(2)}) copy-start(s32[1,8]{1,0:T(1,128)} %codes.1) | copy-start | bytes 100
  46.1 0.7 %copy-start.10 = (s32[16]{0:T(128)S(1)}, s32[16]{0:T(128)}, u32[]{:S(2)}) copy-start(s32[16]{0:T(128)} %param.14) | copy-start | bytes 196
  46.8 16.3 %copy-start = (f32[4,2,64]{2,1,0:T(2,128)S(1)}, f32[4,2,64]{2,1,0:T(2,128)}, u32[]{:S(2)}) copy-start(f32[4,2,64]{2,1,0:T(2,128)} %latent.1) | copy-start | bytes 6148

commit v5 on v4

--- a/solution.py
+++ b/solution.py
@@ -97,40 +97,24 @@
     return average, 1.0 / jnp.sqrt(spread + 1e-05)
 
 
-def stats_kernel(features, out):
+def stats_kernel(features, step, out, time):
+    time[...] = jnp.broadcast_to(step[...].astype(F32).reshape(1, 1), (8, C))
     own_stats(features[...].reshape(CELLS, C).astype(F32), out)
 
 
-def stats_call(features):
+def stats_call(features, step):
     return pl.pallas_call(
         stats_kernel,
-        out_shape=jax.ShapeDtypeStruct((SLABS, 2, C), F32),
-        in_specs=[VMEM],
-        out_specs=VMEM,
+        out_shape=(
+            jax.ShapeDtypeStruct((SLABS, 2, C), F32),
+            jax.ShapeDtypeStruct((8, C), F32),
+        ),
+        in_specs=[VMEM, VMEM],
+        out_specs=(VMEM, VMEM),
         compiler_params=params(4),
-        cost_estimate=cost(2, 1),
+        cost_estimate=cost(4, 1),
         name="stats",
-    )(features)
-
-
-def rims_kernel(planes, step, even, odd, time):
-    time[...] = jnp.broadcast_to(step[...].astype(F32).reshape(1, 1), (8, C))
-    parity = lax.axis_index("slab") % 2
-    even[...] = planes[DEP_DEV - 1 - parity]
-    odd[...] = planes[parity]
-
-
-def rims_call(planes, step):
-    plane = jax.ShapeDtypeStruct((HW, C), BF16)
-    return pl.pallas_call(
-        rims_kernel,
-        out_shape=(plane, plane, jax.ShapeDtypeStruct((8, C), F32)),
-        in_specs=[VMEM, VMEM],
-        out_specs=(VMEM, VMEM, VMEM),
-        compiler_params=params(4),
-        cost_estimate=cost(2, 1),
-        name="rims",
-    )(planes, step)
+    )(features, step)
 
 
 def exact(left, right):
@@ -175,7 +159,7 @@
 def own_weight(guides):
     term = lax.axis_index("cond")
     lane = lax.broadcasted_iota(jnp.int32, (1, TERMS), 1)
-    values = guides[...].astype(F32)
+    values = guides
     others = jnp.sum(jnp.where(lane == 0, 0.0, values), axis=1, keepdims=True)
     mine = jnp.sum(jnp.where(lane == term, values, 0.0), axis=1, keepdims=True)
     return jnp.where(term == 0, TERMS - others, mine) * (1.0 / 16.0)
@@ -186,7 +170,7 @@
 
 
 def compose(conv_two, head, weight):
-    head_rows = jnp.concatenate([head[...], head[...]], axis=0)
+    head_rows = jnp.concatenate([head, head], axis=0)
     upper = lax.broadcasted_iota(jnp.int32, (ROWS, C), 0) < LAT
     composed = three_sum(dot_last(three_parts(head_rows), conv_two[...])) * weight
     nothing = jnp.zeros((ROWS, C), F32)
@@ -206,63 +190,13 @@
 
 
 def direct(features, head, weight):
-    head_rows = jnp.concatenate([head[...], head[...]], axis=0)
+    head_rows = jnp.concatenate([head, head], axis=0)
     upper = lax.broadcasted_iota(jnp.int32, (ROWS, C), 0) < LAT
     wide = jnp.concatenate(
         [jnp.where(upper, head_rows, 0.0), jnp.where(upper, 0.0, head_rows)], axis=1
     )
     both = jnp.concatenate([features[0], features[1]], axis=1)
     return three_sum(dot_last(three_parts(wide), both)) * weight
-
-
-def conv_part(planes, taps_of, weight, held, side):
-    held[0:W, :] = jnp.zeros((W, len(planes) * C), BF16)
-    held[W + HW :, :] = jnp.zeros((W, len(planes) * C), BF16)
-    for at, values in enumerate(planes):
-        held[W : W + HW, at * C : (at + 1) * C] = values.astype(BF16)
-    zero = jnp.zeros((C, C), BF16)
-    depth = len(planes) * C
-
-    def block(tap, row, col):
-        at = ((tap * 3 + row) * 3 + col) * C
-        return weight[at : at + C, :]
-
-    products = []
-    for col in range(3):
-        right = jnp.concatenate(
-            [
-                jnp.concatenate(
-                    [zero if tap is None else block(tap, row, col) for tap in taps], axis=1
-                )
-                for row in range(3)
-                for taps in taps_of
-            ],
-            axis=0,
-        )
-        products.append(
-            sum(
-                jnp.dot(
-                    held[row * W : row * W + HW, :],
-                    right[row * depth : (row + 1) * depth],
-                    preferred_element_type=F32,
-                )
-                for row in range(3)
-            )
-        )
-    column = lax.broadcasted_iota(jnp.int32, (HW, C), 0) % W
-    sums = []
-    for plane in range(DEP_DEV):
-        part = [product[:, plane * C : (plane + 1) * C] for product in products]
-        side[8 : 8 + HW, :] = part[0]
-        before = jnp.where(column == 0, 0.0, side[7 : 7 + HW, :])
-        side[8 : 8 + HW, :] = part[2]
-        after = jnp.where(column == W - 1, 0.0, side[9 : 9 + HW, :])
-        sums.append(part[1] + before + after)
-    return sums
-
-
-def conv_scratch():
-    return [pltpu.VMEM((HW + 2 * W, 4 * C), BF16), pltpu.VMEM((HW + 16, C), F32)]
 
 
 def rim_planes(swapped):
@@ -273,41 +207,114 @@
     return [jnp.where(slab > 0, low, 0.0), jnp.where(slab < SLABS - 1, high, 0.0)]
 
 
-def conv_kernel(every, even, odd, own, weight, out, out_stats, out_even, out_odd, held, side):
+def store_planes(held, planes):
+    held[0:W, :] = jnp.zeros((W, held.shape[1]), BF16)
+    held[W + HW :, :] = jnp.zeros((W, held.shape[1]), BF16)
+    for at, values in enumerate(planes):
+        held[W : W + HW, at * C : (at + 1) * C] = values.astype(BF16)
+
+
+def block(weight, tap, row, col):
+    at = ((tap * 3 + row) * 3 + col) * C
+    return weight[at : at + C, :]
+
+
+def shifted_sum(part, side):
+    column = lax.broadcasted_iota(jnp.int32, (HW, C), 0) % W
+    side[8 : 8 + HW, :] = part[0]
+    before = jnp.where(column == 0, 0.0, side[7 : 7 + HW, :])
+    side[8 : 8 + HW, :] = part[2]
+    after = jnp.where(column == W - 1, 0.0, side[9 : 9 + HW, :])
+    return part[1] + before + after
+
+
+def conv_kernel(every, even, odd, own, weight, out, out_stats, held, norm, side):
     average, scale = all_stats(every)
     shift = -average * scale
+    norm[0:1, :] = scale
+    norm[1:2, :] = shift
 
     def act(values):
         return silu(values.astype(F32) * scale + shift)
 
-    low, high = rim_planes([act(even[...]), act(odd[...])])
-    planes = [low, act(own[0]), act(own[1]), high]
-    sums = conv_part(planes, [(0, None), (1, 0), (2, 1), (None, 2)], weight, held, side)
-    for at in range(DEP_DEV):
-        out[at] = sums[at]
+    parity = lax.axis_index("slab") % 2
+    low, high = rim_planes([act(even[parity]), act(odd[1 - parity])])
+    store_planes(held, [low, act(own[0]), act(own[1]), high])
+    zero = jnp.zeros((C, C), BF16)
+    products = []
+    for col in range(3):
+        product = None
+        for row in range(3):
+            right = jnp.concatenate(
+                [
+                    jnp.concatenate(
+                        [
+                            zero if tap is None else block(weight, tap, row, col)
+                            for tap in taps
+                        ],
+                        axis=1,
+                    )
+                    for taps in [(0, None), (1, 0), (2, 1), (None, 2)]
+                ],
+                axis=0,
+            )
+            term = jnp.dot(
+                held[row * W : row * W + HW, :], right, preferred_element_type=F32
+            )
+            product = term if product is None else product + term
+        products.append(product)
+    for plane in range(DEP_DEV):
+        out[plane] = shifted_sum(
+            [product[:, plane * C : (plane + 1) * C] for product in products], side
+        )
     own_stats(out[...].reshape(CELLS, C), out_stats)
-    parity = lax.axis_index("slab") % 2
-    out_even[...] = out[DEP_DEV - 1 - parity].astype(BF16)
-    out_odd[...] = out[parity].astype(BF16)
-
-
-def conv_call(every, even, odd, own, weight):
-    plane = jax.ShapeDtypeStruct((HW, C), BF16)
+
+
+def conv_call(*operands):
     return pl.pallas_call(
         conv_kernel,
         out_shape=(
             jax.ShapeDtypeStruct((DEP_DEV, HW, C), F32),
             jax.ShapeDtypeStruct((SLABS, 2, C), F32),
-            plane,
-            plane,
+            jax.ShapeDtypeStruct((HW + 2 * W, 4 * C), BF16),
+            jax.ShapeDtypeStruct((8, C), F32),
         ),
-        in_specs=[VMEM] * 5,
+        in_specs=[VMEM] * len(operands),
         out_specs=(VMEM,) * 4,
-        scratch_shapes=conv_scratch(),
+        scratch_shapes=[pltpu.VMEM((HW + 16, C), F32)],
         compiler_params=params(16),
         cost_estimate=cost(2, 32),
         name="conv",
-    )(every, even, odd, own, weight)
+    )(*operands)
+
+
+def far_planes(norm, even, odd, near, weight, held, side):
+    def act(values):
+        return silu(values.astype(F32) * norm[0:1, :] + norm[1:2, :])
+
+    parity = lax.axis_index("slab") % 2
+    store_planes(held, rim_planes([act(even[1 - parity]), act(odd[parity])]))
+    planes = []
+    for plane in range(2):
+        left = []
+        for row in range(3):
+            rows = pl.ds(row * W, HW)
+            if plane == 0:
+                left += [held[rows, :C], near[rows, : 2 * C]]
+            else:
+                left += [near[rows, 2 * C :], held[rows, C:]]
+        left = jnp.concatenate(left, axis=1)
+
+        def right(col):
+            return jnp.concatenate(
+                [block(weight, tap, row, col) for row in range(3) for tap in range(3)], axis=0
+            )
+
+        pair = jnp.concatenate([right(0), right(1)], axis=1)
+        wide = jnp.dot(left, pair, preferred_element_type=F32)
+        narrow = jnp.dot(left, right(2), preferred_element_type=F32)
+        planes.append(shifted_sum([wide[:, :C], wide[:, C:], narrow], side))
+    return planes
 
 
 def mixed(planes, weights, held):
@@ -321,10 +328,13 @@
 
 def head_kernel(
     every,
+    first,
+    norm,
     even,
     odd,
+    near,
+    weight,
     own,
-    features,
     time,
     codes,
     guides,
@@ -335,23 +345,28 @@
     head,
     out,
     roots,
+    rim,
+    side,
     held,
 ):
+    far = far_planes(norm, even, odd, near, weight, rim, side)
     time_value = time[0:1, :]
     roots[...] = sampler_roots(time_value)
     mod = modulate(time_value, codes, table, time_weight, film)
-    weight = own_weight(guides)
-    mix = compose(conv_two, head, weight)
-    base = direct(features, head, weight)
+    share = own_weight(guides[...].astype(F32))
+    mix = compose(conv_two, head[...], share)
+    base = direct(own, head[...], share)
     average, scale = all_stats(every)
     factor = scale * (1.0 + mod[:, :C])
     shift = mod[:, C:] - average * factor
 
     def act(values):
-        return silu(values.astype(F32) * factor + shift)
-
-    low, high = rim_planes([act(even[...]), act(odd[...])])
-    product = mixed([low, act(own[0]), act(own[1]), high], mix, held)
+        return silu(values * factor + shift)
+
+    slab = lax.axis_index("slab")
+    low = jnp.where(slab > 0, act(far[0]), 0.0)
+    high = jnp.where(slab < SLABS - 1, act(far[1]), 0.0)
+    product = mixed([low, act(first[0]), act(first[1]), high], mix, held)
     at = lax.broadcasted_iota(jnp.int32, (ROWS, HW), 1)
     summed = base
     for col in range(3):
@@ -380,8 +395,12 @@
         ),
         in_specs=[VMEM] * len(operands),
         out_specs=(VMEM, VMEM),
-        scratch_shapes=[pltpu.VMEM((HW, 4 * C), BF16)],
-        compiler_params=params(12),
+        scratch_shapes=[
+            pltpu.VMEM((HW + 2 * W, 2 * C), BF16),
+            pltpu.VMEM((HW + 16, C), F32),
+            pltpu.VMEM((HW, 4 * C), BF16),
+        ],
+        compiler_params=params(20),
         cost_estimate=cost(1, 32),
         name="head",
     )(*operands)
@@ -427,21 +446,21 @@
     head_weight,
 ):
     planes = features.reshape(DEP_DEV, HW, C)
-    even, odd, time = rims_call(planes, timestep)
-    even = lax.ppermute(even, "slab", EVEN_PAIRS)
-    odd = lax.ppermute(odd, "slab", ODD_PAIRS)
-    every = lax.all_to_all(stats_call(planes), "slab", 0, 0)
-    first, stats, even, odd = conv_call(
-        every, even, odd, planes, conv_one.reshape(TAPS * C, C)
-    )
-    even = lax.ppermute(even, "slab", EVEN_PAIRS)
-    odd = lax.ppermute(odd, "slab", ODD_PAIRS)
+    even = lax.ppermute(planes, "slab", EVEN_PAIRS)
+    odd = lax.ppermute(planes, "slab", ODD_PAIRS)
+    stats, time = stats_call(planes, timestep)
+    every = lax.all_to_all(stats, "slab", 0, 0)
+    weight = conv_one.reshape(TAPS * C, C)
+    first, stats, near, norm = conv_call(every, even, odd, planes, weight)
     every = lax.all_to_all(stats, "slab", 0, 0)
     pieces, roots = head_call(
         every,
+        first,
+        norm,
         even,
         odd,
-        first,
+        near,
+        weight,
         planes,
         time,
         cond_codes,

time: 64.1 us -> 62.3 us (0.972)
  blocking collectives: 49.7 us -> 44.2 us
  Pallas kernels: 6.56 us -> 9.19 us
  starting transfers between devices: 4.4 us -> 6.1 us
    all_to_all x1 -> x0, blocking collectives: 20 us -> none  [per_device(): every = lax.all_to_all(stats_call(planes), 'slab', 0, 0)]
    all_to_all x1 -> x2, blocking collectives: 15.1 us -> 29.7 us  [per_device(): every = lax.all_to_all(stats, 'slab', 0, 0)]
    pallas_call x1, Pallas kernels: 1.71 us -> 4.6 us  [head_call(): pl.pallas_call(head_kernel, out_shape=(jax.ShapeDtypeStruct((TERMS, LAT,...]
    ppermute x4 -> x2, starting transfers between devices: 4.4 us -> 6.1 us  [the longest x1 5.4 us: per_device(): even = lax.ppermute(planes, 'slab', EVEN_PAIRS)]
  transfers between devices with their start and end apart: 4 -> 2, of which waited for: 0 -> 0; matrix products, arithmetic and copies ran while one was open for 0% -> 0% of each run, Pallas kernels for 0% -> 0%
where the time goes in v5:
time: 62.3 us; the launch traced here: 62 us
  blocking collectives  44.2 us (71%)
  Pallas kernels  9.19 us (15%)
  starting transfers between devices  6.1 us (10%)
  between operations  1.43 us (2%)
  local copies, waits for them, and re-layouts  1.09 us (2%)
    all_to_all x2, blocking collectives, per_device(): every = lax.all_to_all(stats, 'slab', 0, 0)  29.7 us
    all_to_all x1, blocking collectives, per_device(): pieces = lax.all_to_all(pieces, 'cond', 0, 0)  14.5 us
    ppermute x1, starting transfers between devices, per_device(): even = lax.ppermute(planes, 'slab', EVEN_PAIRS)  5.4 us
    pallas_call x1, Pallas kernels, head_call(): pl.pallas_call(head_kernel, out_shape=(jax.ShapeDtypeStruct((TERMS, LAT,...  4.6 us
    pallas_call x1, Pallas kernels, conv_call(): pl.pallas_call(conv_kernel, out_shape=(jax.ShapeDtypeStruct((DEP_DEV, HW,...  3.61 us
  transfers between devices with their start and end apart: 2, of which 0 were waited for; matrix products, arithmetic and copies ran while one was open for 0% of the time, Pallas kernels for 0%

profile of v5, /device:TPU:1, one launch (start us, length us, event | category | flops | bytes accessed | tf_op | source)
XLA Modules:
  0.0 62.0 jit_solution(17928628698607341580)
XLA Ops:
  0.6 0.7 %collective-permute-start.1 = (bf16[2,1024,128]{2,1,0:T(8,128)(2,1)}, bf16[2,1024,128]{2,1,0:T(8,128)(2,1)S(1)}, u32[]{:S(2)}, u32[]{:S(2)}) collective-permute-start(bf16[2,1024,128]{2,1,0:T(8,128)(2,1)} %bitcast.9), channel_id=1, source_target_pairs={{1,2},{2,1},{3,4},{4,3},{5,6},{6,5},{7,8},{8,7},{9,10},{10,9},{11,... | collective-permute-start | bytes 1572872 | tf_op jit(solution)/shard_map/ppermute | solution.py:450
  1.3 5.4 %collective-permute-start = (bf16[2,1024,128]{2,1,0:T(8,128)(2,1)}, bf16[2,1024,128]{2,1,0:T(8,128)(2,1)S(1)}, u32[]{:S(2)}, u32[]{:S(2)}) collective-permute-start(bf16[2,1024,128]{2,1,0:T(8,128)(2,1)} %bitcast.10), channel_id=1, source_target_pairs={{0,1},{1,0},{2,3},{3,2},{4,5},{5,4},{6,7},{7,6},{8,9},{9,8},{10,11... | collective-permute-start | bytes 1572872 | tf_op jit(solution)/shard_map/ppermute | solution.py:449
  7.4 0.0 copy-start.2
  7.4 1.0 %copy-done.2 = bf16[1,2,16,64,128]{4,3,2,1,0:T(8,128)(2,1)S(1)} copy-done((bf16[1,2,16,64,128]{4,3,2,1,0:T(8,128)(2,1)S(1)}, bf16[1,2,16,64,128]{4,3,2,1,0:T(8,128)(2,1)}, u32[]{:S(2)}) %copy-start.2) | copy-done | bytes 524312
  8.4 0.0 copy-start
  8.4 0.3 stats.1
  8.7 17.8 %all_to_all.15.every = f32[16,2,128]{2,1,0:T(2,128)S(1)} all-to-all(f32[16,2,128]{2,1,0:T(2,128)S(1)} %get-tuple-element.10), channel_id=1, replica_groups=mesh['cond'=16,'slab'=16] {'slab'}, dimensions={0} | all-to-all | bytes 32768 | tf_op jit(solution)/shard_map/all_to_all | solution.py:452
  26.5 0.0 collective-permute-done.1.odd
  26.5 0.0 collective-permute-done.even
  26.5 0.0 copy-done
  26.5 0.0 copy-done.3
  26.6 0.0 copy-start.1
  26.6 0.0 copy-start.4
  26.6 0.0 copy-start.5
  26.6 0.0 copy-start.6
  26.6 0.0 copy-start.8
  26.6 0.0 copy-start.9
  26.6 0.0 copy-start.10
  26.6 3.6 %conv.1 = (f32[2,1024,128]{2,1,0:T(8,128)S(1)}, f32[16,2,128]{2,1,0:T(2,128)S(1)}, bf16[1152,512]{1,0:T(8,128)(2,1)S(1)}, f32[8,128]{1,0:T(8,128)S(1)}) custom-call(f32[16,2,128]{2,1,0:T(2,128)S(1)} %all_to_all.15.every, bf16[2,1024,128]{2,1,0:T(8,128)(2,1)S(1)} %collective-permute-done.even, bf16[2,1024,128]{2,1,0:T(8,128)(2,1)S(1)} %collective-permute-done.1.odd, ...), custom_call_target="tpu_custom_call" | custom-call | flops 2000000000 | bytes 33554432 | tf_op jit(solution)/shard_map/conv/pallas_call | solution.py:274
  30.3 11.9 %all_to_all.16.every = f32[16,2,128]{2,1,0:T(2,128)S(1)} all-to-all(f32[16,2,128]{2,1,0:T(2,128)S(1)} %get-tuple-element.11), channel_id=1, replica_groups=mesh['cond'=16,'slab'=16] {'slab'}, dimensions={0} | all-to-all | bytes 32768 | tf_op jit(solution)/shard_map/all_to_all | solution.py:455
  42.1 0.0 copy-done.1
  42.1 0.0 copy-done.4
  42.1 0.0 copy-done.5
  42.1 0.0 copy-done.6
  42.1 0.0 copy-done.8
  42.1 0.0 copy-done.9
  42.2 0.0 copy-done.10
  42.2 0.0 copy-start.7
  42.2 4.6 %head.1 = (f32[16,4,128]{2,1,0:T(4,128)S(1)}, f32[4,128]{1,0:T(4,128)S(1)}) custom-call(f32[16,2,128]{2,1,0:T(2,128)S(1)} %all_to_all.16.every, f32[2,1024,128]{2,1,0:T(8,128)S(1)} %get-tuple-element.12.first, f32[8,128]{1,0:T(8,128)S(1)} %get-tuple-element.13.norm, bf16[2,1024,128]{2,1,0:T(8,128)(2,1)S(1)} %collective-permute-done.even, ...), custom_call_target="tpu_custom_call" | custom-call | flops 1000000000 | bytes 33554432 | tf_op jit(solution)/shard_map/head/pallas_call | solution.py:390
  46.8 14.5 %all_to_all.17.pieces = f32[16,4,128]{2,1,0:T(4,128)S(1)} all-to-all(f32[16,4,128]{2,1,0:T(4,128)S(1)} %get-tuple-element.17), channel_id=1, replica_groups=mesh['cond'=16,'slab'=16] {'cond'}, dimensions={0} | all-to-all | bytes 65536 | tf_op jit(solution)/shard_map/all_to_all | solution.py:474
  61.3 0.0 copy-done.7
  61.3 0.7 %final.1 = (f32[4,2,64]{2,1,0:T(2,128)}, f32[4,2,64]{2,1,0:T(2,128)}) custom-call(f32[4,128]{1,0:T(4,128)S(1)} %get-tuple-element.16.roots, f32[16,4,128]{2,1,0:T(4,128)S(1)} %all_to_all.17.pieces, f32[4,2,64]{2,1,0:T(2,128)S(1)} %copy-done.7), custom_call_target="tpu_custom_call" | custom-call | tf_op jit(solution)/shard_map/final/pallas_call | solution.py:421
  (1 shorter events, 0.0 us)
Async XLA Ops:
  0.6 25.9 %collective-permute-start.1 = (bf16[2,1024,128]{2,1,0:T(8,128)(2,1)}, bf16[2,1024,128]{2,1,0:T(8,128)(2,1)S(1)}, u32[]{:S(2)}, u32[]{:S(2)}) collective-permute-start(bf16[2,1024,128]{2,1,0:T(8,128)(2,1)} %bitcast.9), channel_id=1, source_target_pairs={{1,2},{2,1},{3,4},{4,3},{5,6},{6,5},{7,8},{8,7},{9,10},{10,9},{11,... | collective-permute-start | bytes 1572872 | tf_op jit(solution)/shard_map/ppermute | solution.py:450
  1.3 25.2 %collective-permute-start = (bf16[2,1024,128]{2,1,0:T(8,128)(2,1)}, bf16[2,1024,128]{2,1,0:T(8,128)(2,1)S(1)}, u32[]{:S(2)}, u32[]{:S(2)}) collective-permute-start(bf16[2,1024,128]{2,1,0:T(8,128)(2,1)} %bitcast.10), channel_id=1, source_target_pairs={{0,1},{1,0},{2,3},{3,2},{4,5},{5,4},{6,7},{7,6},{8,9},{9,8},{10,11... | collective-permute-start | bytes 1572872 | tf_op jit(solution)/shard_map/ppermute | solution.py:449
  7.4 1.0 %copy-start.2 = (bf16[1,2,16,64,128]{4,3,2,1,0:T(8,128)(2,1)S(1)}, bf16[1,2,16,64,128]{4,3,2,1,0:T(8,128)(2,1)}, u32[]{:S(2)}) copy-start(bf16[1,2,16,64,128]{4,3,2,1,0:T(8,128)(2,1)} %param.11) | copy-start | bytes 1572868
  8.4 18.1 %copy-start = (bf16[3,3,3,128,128]{4,3,2,1,0:T(8,128)(2,1)S(1)}, bf16[3,3,3,128,128]{4,3,2,1,0:T(8,128)(2,1)}, u32[]{:S(2)}) copy-start(bf16[3,3,3,128,128]{4,3,2,1,0:T(8,128)(2,1)} %param.19) | copy-start | bytes 2654212
  8.4 18.1 %copy-start.3 = (bf16[1,2,16,64,128]{4,3,2,1,0:T(8,128)(2,1)S(1)}, bf16[1,2,16,64,128]{4,3,2,1,0:T(8,128)(2,1)}, u32[]{:S(2)}) copy-start(bf16[1,2,16,64,128]{4,3,2,1,0:T(8,128)(2,1)} %param.11) | copy-start | bytes 1572868
  26.6 15.6 %copy-start.1 = (bf16[3,3,3,128,128]{4,3,2,1,0:T(8,128)(2,1)S(1)}, bf16[3,3,3,128,128]{4,3,2,1,0:T(8,128)(2,1)}, u32[]{:S(2)}) copy-start(bf16[3,3,3,128,128]{4,3,2,1,0:T(8,128)(2,1)} %param.20) | copy-start | bytes 2654212
  26.6 15.6 %copy-start.4 = (f32[256,256]{1,0:T(8,128)S(1)}, f32[256,256]{1,0:T(8,128)}, u32[]{:S(2)}) copy-start(f32[256,256]{1,0:T(8,128)} %time_weight.1) | copy-start | bytes 786436
  26.6 15.5 %copy-start.5 = (f32[256,256]{1,0:T(8,128)S(1)}, f32[256,256]{1,0:T(8,128)}, u32[]{:S(2)}) copy-start(f32[256,256]{1,0:T(8,128)} %film.1) | copy-start | bytes 786436
  26.6 15.5 %copy-start.6 = (f32[8,16,256]{2,1,0:T(8,128)S(1)}, f32[8,16,256]{2,1,0:T(8,128)}, u32[]{:S(2)}) copy-start(f32[8,16,256]{2,1,0:T(8,128)} %param.16) | copy-start | bytes 393220
  26.6 15.5 %copy-start.8 = (f32[128,4]{0,1:T(4,128)S(1)}, f32[128,4]{0,1:T(4,128)}, u32[]{:S(2)}) copy-start(f32[128,4]{0,1:T(4,128)} %param.21) | copy-start | bytes 6148
  26.6 15.5 %copy-start.9 = (s32[1,8]{1,0:T(1,128)S(1)}, s32[1,8]{1,0:T(1,128)}, u32[]{:S(2)}) copy-start(s32[1,8]{1,0:T(1,128)} %codes.1) | copy-start | bytes 100
  26.6 15.5 %copy-start.10 = (s32[16]{0:T(128)S(1)}, s32[16]{0:T(128)}, u32[]{:S(2)}) copy-start(s32[16]{0:T(128)} %param.14) | copy-start | bytes 196
  42.2 19.2 %copy-start.7 = (f32[4,2,64]{2,1,0:T(2,128)S(1)}, f32[4,2,64]{2,1,0:T(2,128)}, u32[]{:S(2)}) copy-start(f32[4,2,64]{2,1,0:T(2,128)} %latent.1) | copy-start | bytes 6148

commit v6 on v5

--- a/solution.py
+++ b/solution.py
@@ -97,24 +97,60 @@
     return average, 1.0 / jnp.sqrt(spread + 1e-05)
 
 
-def stats_kernel(features, step, out, time):
-    time[...] = jnp.broadcast_to(step[...].astype(F32).reshape(1, 1), (8, C))
+def stats_kernel(features, out):
     own_stats(features[...].reshape(CELLS, C).astype(F32), out)
 
 
-def stats_call(features, step):
+def stats_call(features):
     return pl.pallas_call(
         stats_kernel,
-        out_shape=(
-            jax.ShapeDtypeStruct((SLABS, 2, C), F32),
-            jax.ShapeDtypeStruct((8, C), F32),
-        ),
-        in_specs=[VMEM, VMEM],
-        out_specs=(VMEM, VMEM),
+        out_shape=jax.ShapeDtypeStruct((SLABS, 2, C), F32),
+        in_specs=[VMEM],
+        out_specs=VMEM,
         compiler_params=params(4),
         cost_estimate=cost(4, 1),
         name="stats",
-    )(features, step)
+    )(features)
+
+
+def prep_kernel(
+    features,
+    step,
+    codes,
+    guides,
+    table,
+    time_weight,
+    film,
+    conv_two,
+    head,
+    mod,
+    mix,
+    base,
+    roots,
+):
+    time_value = jnp.broadcast_to(step[...].astype(F32).reshape(1, 1), (1, C))
+    roots[...] = sampler_roots(time_value)
+    mod[0:1, :] = modulate(time_value, codes, table, time_weight, film)
+    share = own_weight(guides[...].astype(F32))
+    mix[...] = compose(conv_two, head[...], share)
+    base[...] = direct(features, head[...], share)
+
+
+def prep_call(*operands):
+    return pl.pallas_call(
+        prep_kernel,
+        out_shape=(
+            jax.ShapeDtypeStruct((8, 2 * C), F32),
+            jax.ShapeDtypeStruct((9 * ROWS, 4 * C), F32),
+            jax.ShapeDtypeStruct((ROWS, HW), F32),
+            jax.ShapeDtypeStruct((4, C), F32),
+        ),
+        in_specs=[VMEM] * len(operands),
+        out_specs=(VMEM,) * 4,
+        compiler_params=params(60),
+        cost_estimate=cost(1, 4),
+        name="prep",
+    )(*operands)
 
 
 def exact(left, right):
@@ -228,7 +264,8 @@
     return part[1] + before + after
 
 
-def conv_kernel(every, even, odd, own, weight, out, out_stats, held, norm, side):
+def conv_kernel(every, odd, even, own, weight, mod, out, out_stats, held, norm, side):
+    del mod
     average, scale = all_stats(every)
     shift = -average * scale
     norm[0:1, :] = scale
@@ -330,35 +367,22 @@
     every,
     first,
     norm,
+    odd,
     even,
-    odd,
     near,
     weight,
-    own,
-    time,
-    codes,
-    guides,
-    table,
-    time_weight,
-    film,
-    conv_two,
-    head,
+    mod,
+    mix,
+    base,
     out,
-    roots,
     rim,
     side,
     held,
 ):
     far = far_planes(norm, even, odd, near, weight, rim, side)
-    time_value = time[0:1, :]
-    roots[...] = sampler_roots(time_value)
-    mod = modulate(time_value, codes, table, time_weight, film)
-    share = own_weight(guides[...].astype(F32))
-    mix = compose(conv_two, head[...], share)
-    base = direct(own, head[...], share)
     average, scale = all_stats(every)
-    factor = scale * (1.0 + mod[:, :C])
-    shift = mod[:, C:] - average * factor
+    factor = scale * (1.0 + mod[0:1, :C])
+    shift = mod[0:1, C:] - average * factor
 
     def act(values):
         return silu(values * factor + shift)
@@ -366,9 +390,9 @@
     slab = lax.axis_index("slab")
     low = jnp.where(slab > 0, act(far[0]), 0.0)
     high = jnp.where(slab < SLABS - 1, act(far[1]), 0.0)
-    product = mixed([low, act(first[0]), act(first[1]), high], mix, held)
+    product = mixed([low, act(first[0]), act(first[1]), high], mix[...], held)
     at = lax.broadcasted_iota(jnp.int32, (ROWS, HW), 1)
-    summed = base
+    summed = base[...]
     for col in range(3):
         part = [product[(row * 3 + col) * ROWS : (row * 3 + col + 1) * ROWS] for row in range(3)]
         values = (
@@ -389,12 +413,9 @@
 def head_call(*operands):
     return pl.pallas_call(
         head_kernel,
-        out_shape=(
-            jax.ShapeDtypeStruct((TERMS, LAT, DEP_DEV * SHARE), F32),
-            jax.ShapeDtypeStruct((4, C), F32),
-        ),
+        out_shape=jax.ShapeDtypeStruct((TERMS, LAT, DEP_DEV * SHARE), F32),
         in_specs=[VMEM] * len(operands),
-        out_specs=(VMEM, VMEM),
+        out_specs=VMEM,
         scratch_shapes=[
             pltpu.VMEM((HW + 2 * W, 2 * C), BF16),
             pltpu.VMEM((HW + 16, C), F32),
@@ -448,21 +469,10 @@
     planes = features.reshape(DEP_DEV, HW, C)
     even = lax.ppermute(planes, "slab", EVEN_PAIRS)
     odd = lax.ppermute(planes, "slab", ODD_PAIRS)
-    stats, time = stats_call(planes, timestep)
-    every = lax.all_to_all(stats, "slab", 0, 0)
-    weight = conv_one.reshape(TAPS * C, C)
-    first, stats, near, norm = conv_call(every, even, odd, planes, weight)
-    every = lax.all_to_all(stats, "slab", 0, 0)
-    pieces, roots = head_call(
-        every,
-        first,
-        norm,
-        even,
-        odd,
-        near,
-        weight,
+    stats = stats_call(planes)
+    mod, mix, base, roots = prep_call(
         planes,
-        time,
+        timestep,
         cond_codes,
         guide_codes.reshape(1, TERMS),
         code_table.reshape(SLOTS * CODES, EMB),
@@ -471,6 +481,11 @@
         conv_two.reshape(TAPS * C, C),
         head_weight.T,
     )
+    every = lax.all_to_all(stats, "slab", 0, 0)
+    weight = conv_one.reshape(TAPS * C, C)
+    first, stats, near, norm = conv_call(every, odd, even, planes, weight, mod)
+    every = lax.all_to_all(stats, "slab", 0, 0)
+    pieces = head_call(every, first, norm, odd, even, near, weight, mod, mix, base)
     pieces = lax.all_to_all(pieces, "cond", 0, 0)
     return final_call(roots, pieces, latent)
 

time: 62.3 us -> 61.5 us (0.987)
  blocking collectives: 44.2 us -> 26.5 us
  starting transfers between devices: 6.1 us -> 14.6 us
  waiting for transfers between devices: 0.01 us -> 4.99 us
  Pallas kernels: 9.19 us -> 12 us
  local copies, waits for them, and re-layouts: 1.09 us -> 1.76 us
    all_to_all x2 -> x1, blocking collectives: 29.7 us -> 12.7 us  [per_device(): every = lax.all_to_all(stats, 'slab', 0, 0)]
    all_to_all x0 -> x1, starting transfers between devices: none -> 11.4 us  [per_device(): every = lax.all_to_all(stats, 'slab', 0, 0)]
    all_to_all x0 -> x1, waiting for transfers between devices: none -> 4.98 us  [per_device(): every = lax.all_to_all(stats, 'slab', 0, 0)]
    ppermute x1, starting transfers between devices: 5.4 us -> 2.55 us  [per_device(): even = lax.ppermute(planes, 'slab', EVEN_PAIRS)]
    pallas_call x2 -> x3, Pallas kernels: 4.9 us -> 7.74 us  [the longest x1 3.65 us: head_call(): pl.pallas_call(head_kernel, out_shape=jax.ShapeDtypeStruct((TERMS, LAT, D...]
    all_to_all x1, blocking collectives: 14.5 us -> 13.7 us  [per_device(): pieces = lax.all_to_all(pieces, 'cond', 0, 0)]
    unnamed x22 -> x18, local copies, waits for them, and re-layouts: 1.09 us -> 1.76 us
  transfers between devices with their start and end apart: 2 -> 3, of which waited for: 0 -> 1; matrix products, arithmetic and copies ran while one was open for 0% -> 0% of each run, Pallas kernels for 0% -> 7%
where the time goes in v6:
time: 61.5 us; the launch traced here: 61.2 us
  blocking collectives  26.5 us (43%)
  starting transfers between devices  14.6 us (24%)
  Pallas kernels  12 us (20%)
  waiting for transfers between devices  4.99 us (8%)
  local copies, waits for them, and re-layouts  1.76 us (3%)
  between operations  1.38 us (2%)
    all_to_all x1, blocking collectives, per_device(): pieces = lax.all_to_all(pieces, 'cond', 0, 0)  13.7 us
    all_to_all x1, blocking collectives, per_device(): every = lax.all_to_all(stats, 'slab', 0, 0)  12.7 us
    all_to_all x1, starting transfers between devices, per_device(): every = lax.all_to_all(stats, 'slab', 0, 0)  11.4 us
    all_to_all x1, waiting for transfers between devices, per_device(): every = lax.all_to_all(stats, 'slab', 0, 0)  4.98 us
    pallas_call x1, Pallas kernels, head_call(): pl.pallas_call(head_kernel, out_shape=jax.ShapeDtypeStruct((TERMS, LAT, D...  3.65 us
    pallas_call x1, Pallas kernels, conv_call(): pl.pallas_call(conv_kernel, out_shape=(jax.ShapeDtypeStruct((DEP_DEV, HW,...  3.59 us
    pallas_call x1, Pallas kernels, prep_call(): pl.pallas_call(prep_kernel, out_shape=(jax.ShapeDtypeStruct((8, 2 * C), F...  3.19 us
    ppermute x1, starting transfers between devices, per_device(): even = lax.ppermute(planes, 'slab', EVEN_PAIRS)  2.55 us
  transfers between devices with their start and end apart: 3, of which 1 were waited for; matrix products, arithmetic and copies ran while one was open for 0% of the time, Pallas kernels for 7%

profile of v6, /device:TPU:1, one launch (start us, length us, event | category | flops | bytes accessed | tf_op | source)
XLA Modules:
  0.0 61.2 jit_solution(10706217064370509583)
XLA Ops:
  0.6 2.6 %collective-permute-start.1 = (bf16[2,1024,128]{2,1,0:T(8,128)(2,1)}, bf16[2,1024,128]{2,1,0:T(8,128)(2,1)S(1)}, u32[]{:S(2)}, u32[]{:S(2)}) collective-permute-start(bf16[2,1024,128]{2,1,0:T(8,128)(2,1)} %bitcast.8), channel_id=1, source_target_pairs={{0,1},{1,0},{2,3},{3,2},{4,5},{5,4},{6,7},{7,6},{8,9},{9,8},{10,11... | collective-permute-start | bytes 1572872 | tf_op jit(solution)/shard_map/ppermute | solution.py:470
  3.2 0.7 %collective-permute-start = (bf16[2,1024,128]{2,1,0:T(8,128)(2,1)}, bf16[2,1024,128]{2,1,0:T(8,128)(2,1)S(1)}, u32[]{:S(2)}, u32[]{:S(2)}) collective-permute-start(bf16[2,1024,128]{2,1,0:T(8,128)(2,1)} %bitcast.9), channel_id=1, source_target_pairs={{1,2},{2,1},{3,4},{4,3},{5,6},{6,5},{7,8},{8,7},{9,10},{10,9},{11,... | collective-permute-start | bytes 1572872 | tf_op jit(solution)/shard_map/ppermute | solution.py:471
  3.9 0.0 copy-start.7
  3.9 1.0 %copy-done.7 = bf16[1,2,16,64,128]{4,3,2,1,0:T(8,128)(2,1)S(1)} copy-done((bf16[1,2,16,64,128]{4,3,2,1,0:T(8,128)(2,1)S(1)}, bf16[1,2,16,64,128]{4,3,2,1,0:T(8,128)(2,1)}, u32[]{:S(2)}) %copy-start.7) | copy-done | bytes 524312
  4.9 0.9 %stats.1 = f32[16,2,128]{2,1,0:T(2,128)} custom-call(bf16[2,1024,128]{2,1,0:T(8,128)(2,1)S(1)} %bitcast.11), custom_call_target="tpu_custom_call" | custom-call | flops 4000000000 | bytes 1048576 | tf_op jit(solution)/shard_map/stats/pallas_call | solution.py:105
  5.8 11.4 %all-to-all-start = ((f32[16,2,128]{2,1,0:T(2,128)}), f32[16,2,128]{2,1,0:T(2,128)S(1)}, u32[]{:S(2)}, u32[]{:S(2)}) async-start(f32[16,2,128]{2,1,0:T(2,128)} %stats.1), calls=%async_computation | async-start | bytes 32768 | tf_op jit(solution)/shard_map/all_to_all | solution.py:484
  17.8 0.0 copy-start
  17.9 0.0 copy-start.8
  17.9 3.2 %prep.1 = (f32[8,256]{1,0:T(8,128)}, f32[72,512]{1,0:T(8,128)}, f32[8,1024]{1,0:T(8,128)}, f32[4,128]{1,0:T(4,128)}) custom-call(bf16[2,1024,128]{2,1,0:T(8,128)(2,1)} %bitcast.10, s32[1]{0:T(128)S(6)} %copy.13.step, s32[1,8]{1,0:T(1,128)} %codes.1, s32[1,16]{1,0:T(1,128)} %bitcast.16, f32[128,256]{1,0:T(8,128)} %bitcast.14, f32[256,256]{1,0:T(8,128)} %time_weight.1, ...), custom_call_target="tpu_custom_call" | custom-call | flops 1000000000 | bytes 4194304 | tf_op jit(solution)/shard_map/prep/pallas_call | solution.py:140
  21.1 5.0 %all-to-all-done.every = f32[16,2,128]{2,1,0:T(2,128)S(1)} async-done(((f32[16,2,128]{2,1,0:T(2,128)}), f32[16,2,128]{2,1,0:T(2,128)S(1)}, u32[]{:S(2)}, u32[]{:S(2)}) %all-to-all-start) | async-done | bytes 16416 | tf_op jit(solution)/shard_map/all_to_all | solution.py:484
  26.0 0.0 collective-permute-done.1.even
  26.0 0.0 collective-permute-done.odd
  26.0 0.0 copy-done
  26.0 0.0 copy-done.8
  26.1 0.0 copy-start.3
  26.1 0.7 %copy-done.3 = f32[8,256]{1,0:T(8,128)S(1)} copy-done((f32[8,256]{1,0:T(8,128)S(1)}, f32[8,256]{1,0:T(8,128)}, u32[]{:S(2)}) %copy-start.3) | copy-done | bytes 8216
  26.8 0.0 copy-start.1
  26.8 0.0 copy-start.2
  26.8 0.0 copy-start.4
  26.8 3.6 %conv.1 = (f32[2,1024,128]{2,1,0:T(8,128)S(1)}, f32[16,2,128]{2,1,0:T(2,128)S(1)}, bf16[1152,512]{1,0:T(8,128)(2,1)S(1)}, f32[8,128]{1,0:T(8,128)S(1)}) custom-call(f32[16,2,128]{2,1,0:T(2,128)S(1)} %all-to-all-done.every, bf16[2,1024,128]{2,1,0:T(8,128)(2,1)S(1)} %collective-permute-done.odd, bf16[2,1024,128]{2,1,0:T(8,128)(2,1)S(1)} %collective-permute-done.1.even, ...), custom_call_target="tpu_custom_call" | custom-call | flops 2000000000 | bytes 33554432 | tf_op jit(solution)/shard_map/conv/pallas_call | solution.py:311
  30.4 12.7 %all_to_all.15.every = f32[16,2,128]{2,1,0:T(2,128)S(1)} all-to-all(f32[16,2,128]{2,1,0:T(2,128)S(1)} %get-tuple-element.12), channel_id=1, replica_groups=mesh['cond'=16,'slab'=16] {'slab'}, dimensions={0} | all-to-all | bytes 32768 | tf_op jit(solution)/shard_map/all_to_all | solution.py:487
  43.1 0.0 copy-done.1
  43.1 0.0 copy-done.2
  43.1 0.0 copy-done.4
  43.1 0.0 copy-start.5
  43.1 0.0 copy-start.6
  43.1 3.7 %head.1 = f32[16,4,128]{2,1,0:T(4,128)S(1)} custom-call(f32[16,2,128]{2,1,0:T(2,128)S(1)} %all_to_all.15.every, f32[2,1024,128]{2,1,0:T(8,128)S(1)} %get-tuple-element.13.first, f32[8,128]{1,0:T(8,128)S(1)} %get-tuple-element.14.norm, bf16[2,1024,128]{2,1,0:T(8,128)(2,1)S(1)} %collective-permute-done.odd, ...), custom_call_target="tpu_custom_call" | custom-call | flops 1000000000 | bytes 33554432 | tf_op jit(solution)/shard_map/head/pallas_call | solution.py:414
  46.8 13.7 %all_to_all.16.pieces = f32[16,4,128]{2,1,0:T(4,128)S(1)} all-to-all(f32[16,4,128]{2,1,0:T(4,128)S(1)} %head.1), channel_id=1, replica_groups=mesh['cond'=16,'slab'=16] {'cond'}, dimensions={0} | all-to-all | bytes 65536 | tf_op jit(solution)/shard_map/all_to_all | solution.py:489
  60.5 0.0 copy-done.5
  60.5 0.0 copy-done.6
  60.5 0.7 %final.1 = (f32[4,2,64]{2,1,0:T(2,128)}, f32[4,2,64]{2,1,0:T(2,128)}) custom-call(f32[4,128]{1,0:T(4,128)S(1)} %copy-done.6, f32[16,4,128]{2,1,0:T(4,128)S(1)} %all_to_all.16.pieces, f32[4,2,64]{2,1,0:T(2,128)S(1)} %copy-done.5), custom_call_target="tpu_custom_call" | custom-call | tf_op jit(solution)/shard_map/final/pallas_call | solution.py:442
Async XLA Ops:
  0.6 25.4 %collective-permute-start.1 = (bf16[2,1024,128]{2,1,0:T(8,128)(2,1)}, bf16[2,1024,128]{2,1,0:T(8,128)(2,1)S(1)}, u32[]{:S(2)}, u32[]{:S(2)}) collective-permute-start(bf16[2,1024,128]{2,1,0:T(8,128)(2,1)} %bitcast.8), channel_id=1, source_target_pairs={{0,1},{1,0},{2,3},{3,2},{4,5},{5,4},{6,7},{7,6},{8,9},{9,8},{10,11... | collective-permute-start | bytes 1572872 | tf_op jit(solution)/shard_map/ppermute | solution.py:470
  3.2 22.9 %collective-permute-start = (bf16[2,1024,128]{2,1,0:T(8,128)(2,1)}, bf16[2,1024,128]{2,1,0:T(8,128)(2,1)S(1)}, u32[]{:S(2)}, u32[]{:S(2)}) collective-permute-start(bf16[2,1024,128]{2,1,0:T(8,128)(2,1)} %bitcast.9), channel_id=1, source_target_pairs={{1,2},{2,1},{3,4},{4,3},{5,6},{6,5},{7,8},{8,7},{9,10},{10,9},{11,... | collective-permute-start | bytes 1572872 | tf_op jit(solution)/shard_map/ppermute | solution.py:471
  3.9 1.0 %copy-start.7 = (bf16[1,2,16,64,128]{4,3,2,1,0:T(8,128)(2,1)S(1)}, bf16[1,2,16,64,128]{4,3,2,1,0:T(8,128)(2,1)}, u32[]{:S(2)}) copy-start(bf16[1,2,16,64,128]{4,3,2,1,0:T(8,128)(2,1)} %param.11) | copy-start | bytes 1572868
  5.8 20.2 %all-to-all-start = ((f32[16,2,128]{2,1,0:T(2,128)}), f32[16,2,128]{2,1,0:T(2,128)S(1)}, u32[]{:S(2)}, u32[]{:S(2)}) async-start(f32[16,2,128]{2,1,0:T(2,128)} %stats.1), calls=%async_computation | async-start | bytes 32768 | tf_op jit(solution)/shard_map/all_to_all | solution.py:484
  17.8 8.2 %copy-start = (bf16[3,3,3,128,128]{4,3,2,1,0:T(8,128)(2,1)S(1)}, bf16[3,3,3,128,128]{4,3,2,1,0:T(8,128)(2,1)}, u32[]{:S(2)}) copy-start(bf16[3,3,3,128,128]{4,3,2,1,0:T(8,128)(2,1)} %param.19) | copy-start | bytes 2654212
  17.9 8.2 %copy-start.8 = (bf16[1,2,16,64,128]{4,3,2,1,0:T(8,128)(2,1)S(1)}, bf16[1,2,16,64,128]{4,3,2,1,0:T(8,128)(2,1)}, u32[]{:S(2)}) copy-start(bf16[1,2,16,64,128]{4,3,2,1,0:T(8,128)(2,1)} %param.11) | copy-start | bytes 1572868
  26.1 0.7 %copy-start.3 = (f32[8,256]{1,0:T(8,128)S(1)}, f32[8,256]{1,0:T(8,128)}, u32[]{:S(2)}) copy-start(f32[8,256]{1,0:T(8,128)} %get-tuple-element.11.mod) | copy-start | bytes 24580
  26.8 16.4 %copy-start.1 = (f32[72,512]{1,0:T(8,128)S(1)}, f32[72,512]{1,0:T(8,128)}, u32[]{:S(2)}) copy-start(f32[72,512]{1,0:T(8,128)} %get-tuple-element.16.mix) | copy-start | bytes 442372
  26.8 16.4 %copy-start.2 = (f32[8,1024]{1,0:T(8,128)S(1)}, f32[8,1024]{1,0:T(8,128)}, u32[]{:S(2)}) copy-start(f32[8,1024]{1,0:T(8,128)} %get-tuple-element.17.base) | copy-start | bytes 98308
  26.8 16.4 %copy-start.4 = (f32[8,256]{1,0:T(8,128)S(1)}, f32[8,256]{1,0:T(8,128)}, u32[]{:S(2)}) copy-start(f32[8,256]{1,0:T(8,128)} %get-tuple-element.11.mod) | copy-start | bytes 24580
  43.1 17.4 %copy-start.5 = (f32[4,2,64]{2,1,0:T(2,128)S(1)}, f32[4,2,64]{2,1,0:T(2,128)}, u32[]{:S(2)}) copy-start(f32[4,2,64]{2,1,0:T(2,128)} %latent.1) | copy-start | bytes 6148
  43.1 17.4 %copy-start.6 = (f32[4,128]{1,0:T(4,128)S(1)}, f32[4,128]{1,0:T(4,128)}, u32[]{:S(2)}) copy-start(f32[4,128]{1,0:T(4,128)} %get-tuple-element.10.roots) | copy-start | bytes 6148

commit v7 on v6

--- a/solution.py
+++ b/solution.py
@@ -151,6 +151,22 @@
         cost_estimate=cost(1, 4),
         name="prep",
     )(*operands)
+
+
+def carry_kernel(mod, out):
+    out[...] = mod[...]
+
+
+def carry_call(mod):
+    return pl.pallas_call(
+        carry_kernel,
+        out_shape=jax.ShapeDtypeStruct(mod.shape, F32),
+        in_specs=[VMEM],
+        out_specs=VMEM,
+        compiler_params=params(2),
+        cost_estimate=cost(1, 1),
+        name="carry",
+    )(mod)
 
 
 def exact(left, right):
@@ -483,6 +499,7 @@
     )
     every = lax.all_to_all(stats, "slab", 0, 0)
     weight = conv_one.reshape(TAPS * C, C)
+    mod = carry_call(mod)
     first, stats, near, norm = conv_call(every, odd, even, planes, weight, mod)
     every = lax.all_to_all(stats, "slab", 0, 0)
     pieces = head_call(every, first, norm, odd, even, near, weight, mod, mix, base)

time: 61.5 us -> 62.3 us (1.013)
  blocking collectives: 26.5 us -> 27.8 us
    all_to_all x1, blocking collectives: 12.7 us -> 14.5 us  [per_device(): every = lax.all_to_all(stats, 'slab', 0, 0)]
    unnamed x18 -> x16, local copies, waits for them, and re-layouts: 1.76 us -> 1.76 us
  transfers between devices with their start and end apart: 3 -> 3, of which waited for: 1 -> 1; matrix products, arithmetic and copies ran while one was open for 0% -> 0% of each run, Pallas kernels for 7% -> 6%
where the time goes in v7:
time: 62.3 us; the launch traced here: 61.9 us
  blocking collectives  27.8 us (45%)
  starting transfers between devices  14.6 us (23%)
  Pallas kernels  11.9 us (19%)
  waiting for transfers between devices  4.5 us (7%)
  local copies, waits for them, and re-layouts  1.76 us (3%)
  between operations  1.36 us (2%)
    all_to_all x1, blocking collectives, per_device(): every = lax.all_to_all(stats, 'slab', 0, 0)  14.5 us
    all_to_all x1, blocking collectives, per_device(): pieces = lax.all_to_all(pieces, 'cond', 0, 0)  13.3 us
    all_to_all x1, starting transfers between devices, per_device(): every = lax.all_to_all(stats, 'slab', 0, 0)  11.4 us
    all_to_all x1, waiting for transfers between devices, per_device(): every = lax.all_to_all(stats, 'slab', 0, 0)  4.49 us
    pallas_call x1, Pallas kernels, head_call(): pl.pallas_call(head_kernel, out_shape=jax.ShapeDtypeStruct((TERMS, LAT, D...  3.64 us
    pallas_call x1, Pallas kernels, conv_call(): pl.pallas_call(conv_kernel, out_shape=(jax.ShapeDtypeStruct((DEP_DEV, HW,...  3.6 us
    pallas_call x1, Pallas kernels, prep_call(): pl.pallas_call(prep_kernel, out_shape=(jax.ShapeDtypeStruct((8, 2 * C), F...  3.1 us
    ppermute x1, starting transfers between devices, per_device(): even = lax.ppermute(planes, 'slab', EVEN_PAIRS)  2.55 us
  transfers between devices with their start and end apart: 3, of which 1 were waited for; matrix products, arithmetic and copies ran while one was open for 0% of the time, Pallas kernels for 6%

profile of v7, /device:TPU:1, one launch (start us, length us, event | category | flops | bytes accessed | tf_op | source)
XLA Modules:
  0.0 61.9 jit_solution(12971308912644327335)
XLA Ops:
  0.6 2.6 %collective-permute-start.1 = (bf16[2,1024,128]{2,1,0:T(8,128)(2,1)}, bf16[2,1024,128]{2,1,0:T(8,128)(2,1)S(1)}, u32[]{:S(2)}, u32[]{:S(2)}) collective-permute-start(bf16[2,1024,128]{2,1,0:T(8,128)(2,1)} %bitcast.8), channel_id=1, source_target_pairs={{0,1},{1,0},{2,3},{3,2},{4,5},{5,4},{6,7},{7,6},{8,9},{9,8},{10,11... | collective-permute-start | bytes 1572872 | tf_op jit(solution)/shard_map/ppermute | solution.py:486
  3.2 0.7 %collective-permute-start = (bf16[2,1024,128]{2,1,0:T(8,128)(2,1)}, bf16[2,1024,128]{2,1,0:T(8,128)(2,1)S(1)}, u32[]{:S(2)}, u32[]{:S(2)}) collective-permute-start(bf16[2,1024,128]{2,1,0:T(8,128)(2,1)} %bitcast.9), channel_id=1, source_target_pairs={{1,2},{2,1},{3,4},{4,3},{5,6},{6,5},{7,8},{8,7},{9,10},{10,9},{11,... | collective-permute-start | bytes 1572872 | tf_op jit(solution)/shard_map/ppermute | solution.py:487
  3.9 0.0 copy-start.5
  3.9 1.0 %copy-done.5 = bf16[1,2,16,64,128]{4,3,2,1,0:T(8,128)(2,1)S(1)} copy-done((bf16[1,2,16,64,128]{4,3,2,1,0:T(8,128)(2,1)S(1)}, bf16[1,2,16,64,128]{4,3,2,1,0:T(8,128)(2,1)}, u32[]{:S(2)}) %copy-start.5) | copy-done | bytes 524312
  4.9 0.9 %stats.1 = f32[16,2,128]{2,1,0:T(2,128)} custom-call(bf16[2,1024,128]{2,1,0:T(8,128)(2,1)S(1)} %bitcast.11), custom_call_target="tpu_custom_call" | custom-call | flops 4000000000 | bytes 1048576 | tf_op jit(solution)/shard_map/stats/pallas_call | solution.py:105
  5.8 11.4 %all-to-all-start = ((f32[16,2,128]{2,1,0:T(2,128)}), f32[16,2,128]{2,1,0:T(2,128)S(1)}, u32[]{:S(2)}, u32[]{:S(2)}) async-start(f32[16,2,128]{2,1,0:T(2,128)} %stats.1), calls=%async_computation | async-start | bytes 32768 | tf_op jit(solution)/shard_map/all_to_all | solution.py:500
  17.8 3.1 %prep.1 = (f32[8,256]{1,0:T(8,128)}, f32[72,512]{1,0:T(8,128)}, f32[8,1024]{1,0:T(8,128)}, f32[4,128]{1,0:T(4,128)}) custom-call(bf16[2,1024,128]{2,1,0:T(8,128)(2,1)} %bitcast.10, s32[1]{0:T(128)S(6)} %copy.13.step, s32[1,8]{1,0:T(1,128)} %codes.1, s32[1,16]{1,0:T(1,128)} %bitcast.16, f32[128,256]{1,0:T(8,128)} %bitcast.14, f32[256,256]{1,0:T(8,128)} %time_weight.1, ...), custom_call_target="tpu_custom_call" | custom-call | flops 1000000000 | bytes 4194304 | tf_op jit(solution)/shard_map/prep/pallas_call | solution.py:140
  20.9 0.0 copy-start.7
  20.9 0.7 %copy-done.7 = f32[8,256]{1,0:T(8,128)S(1)} copy-done((f32[8,256]{1,0:T(8,128)S(1)}, f32[8,256]{1,0:T(8,128)}, u32[]{:S(2)}) %copy-start.7) | copy-done | bytes 8216
  21.6 0.0 copy-start
  21.6 0.0 copy-start.6
  21.6 4.5 %all-to-all-done.every = f32[16,2,128]{2,1,0:T(2,128)S(1)} async-done(((f32[16,2,128]{2,1,0:T(2,128)}), f32[16,2,128]{2,1,0:T(2,128)S(1)}, u32[]{:S(2)}, u32[]{:S(2)}) %all-to-all-start) | async-done | bytes 16416 | tf_op jit(solution)/shard_map/all_to_all | solution.py:500
  26.1 0.0 collective-permute-done.1.even
  26.1 0.0 collective-permute-done.odd
  26.1 0.0 copy-done
  26.1 0.0 copy-done.6
  26.2 0.0 copy-start.1
  26.2 0.0 copy-start.2
  26.2 3.6 %conv.1 = (f32[2,1024,128]{2,1,0:T(8,128)S(1)}, f32[16,2,128]{2,1,0:T(2,128)S(1)}, bf16[1152,512]{1,0:T(8,128)(2,1)S(1)}, f32[8,128]{1,0:T(8,128)S(1)}) custom-call(f32[16,2,128]{2,1,0:T(2,128)S(1)} %all-to-all-done.every, bf16[2,1024,128]{2,1,0:T(8,128)(2,1)S(1)} %collective-permute-done.odd, bf16[2,1024,128]{2,1,0:T(8,128)(2,1)S(1)} %collective-permute-done.1.even, ...), custom_call_target="tpu_custom_call" | custom-call | flops 2000000000 | bytes 33554432 | tf_op jit(solution)/shard_map/conv/pallas_call | solution.py:327
  29.8 14.5 %all_to_all.15.every = f32[16,2,128]{2,1,0:T(2,128)S(1)} all-to-all(f32[16,2,128]{2,1,0:T(2,128)S(1)} %get-tuple-element.12), channel_id=1, replica_groups=mesh['cond'=16,'slab'=16] {'slab'}, dimensions={0} | all-to-all | bytes 32768 | tf_op jit(solution)/shard_map/all_to_all | solution.py:504
  44.3 0.0 copy-done.1
  44.3 0.0 copy-done.2
  44.3 0.0 copy-start.3
  44.3 0.0 copy-start.4
  44.3 3.6 %head.1 = f32[16,4,128]{2,1,0:T(4,128)S(1)} custom-call(f32[16,2,128]{2,1,0:T(2,128)S(1)} %all_to_all.15.every, f32[2,1024,128]{2,1,0:T(8,128)S(1)} %get-tuple-element.13.first, f32[8,128]{1,0:T(8,128)S(1)} %get-tuple-element.14.norm, bf16[2,1024,128]{2,1,0:T(8,128)(2,1)S(1)} %collective-permute-done.odd, ...), custom_call_target="tpu_custom_call" | custom-call | flops 1000000000 | bytes 33554432 | tf_op jit(solution)/shard_map/head/pallas_call | solution.py:430
  47.9 13.3 %all_to_all.16.pieces = f32[16,4,128]{2,1,0:T(4,128)S(1)} all-to-all(f32[16,4,128]{2,1,0:T(4,128)S(1)} %head.1), channel_id=1, replica_groups=mesh['cond'=16,'slab'=16] {'cond'}, dimensions={0} | all-to-all | bytes 65536 | tf_op jit(solution)/shard_map/all_to_all | solution.py:506
  61.2 0.0 copy-done.3
  61.3 0.0 copy-done.4
  61.3 0.7 %final.1 = (f32[4,2,64]{2,1,0:T(2,128)}, f32[4,2,64]{2,1,0:T(2,128)}) custom-call(f32[4,128]{1,0:T(4,128)S(1)} %copy-done.4, f32[16,4,128]{2,1,0:T(4,128)S(1)} %all_to_all.16.pieces, f32[4,2,64]{2,1,0:T(2,128)S(1)} %copy-done.3), custom_call_target="tpu_custom_call" | custom-call | tf_op jit(solution)/shard_map/final/pallas_call | solution.py:458
  (1 shorter events, 0.0 us)
Async XLA Ops:
  0.6 25.5 %collective-permute-start.1 = (bf16[2,1024,128]{2,1,0:T(8,128)(2,1)}, bf16[2,1024,128]{2,1,0:T(8,128)(2,1)S(1)}, u32[]{:S(2)}, u32[]{:S(2)}) collective-permute-start(bf16[2,1024,128]{2,1,0:T(8,128)(2,1)} %bitcast.8), channel_id=1, source_target_pairs={{0,1},{1,0},{2,3},{3,2},{4,5},{5,4},{6,7},{7,6},{8,9},{9,8},{10,11... | collective-permute-start | bytes 1572872 | tf_op jit(solution)/shard_map/ppermute | solution.py:486
  3.2 23.0 %collective-permute-start = (bf16[2,1024,128]{2,1,0:T(8,128)(2,1)}, bf16[2,1024,128]{2,1,0:T(8,128)(2,1)S(1)}, u32[]{:S(2)}, u32[]{:S(2)}) collective-permute-start(bf16[2,1024,128]{2,1,0:T(8,128)(2,1)} %bitcast.9), channel_id=1, source_target_pairs={{1,2},{2,1},{3,4},{4,3},{5,6},{6,5},{7,8},{8,7},{9,10},{10,9},{11,... | collective-permute-start | bytes 1572872 | tf_op jit(solution)/shard_map/ppermute | solution.py:487
  3.9 1.0 %copy-start.5 = (bf16[1,2,16,64,128]{4,3,2,1,0:T(8,128)(2,1)S(1)}, bf16[1,2,16,64,128]{4,3,2,1,0:T(8,128)(2,1)}, u32[]{:S(2)}) copy-start(bf16[1,2,16,64,128]{4,3,2,1,0:T(8,128)(2,1)} %param.11) | copy-start | bytes 1572868
  5.8 20.3 %all-to-all-start = ((f32[16,2,128]{2,1,0:T(2,128)}), f32[16,2,128]{2,1,0:T(2,128)S(1)}, u32[]{:S(2)}, u32[]{:S(2)}) async-start(f32[16,2,128]{2,1,0:T(2,128)} %stats.1), calls=%async_computation | async-start | bytes 32768 | tf_op jit(solution)/shard_map/all_to_all | solution.py:500
  20.9 0.7 %copy-start.7 = (f32[8,256]{1,0:T(8,128)S(1)}, f32[8,256]{1,0:T(8,128)}, u32[]{:S(2)}) copy-start(f32[8,256]{1,0:T(8,128)} %get-tuple-element.11.mod) | copy-start | bytes 24580
  21.6 4.5 %copy-start = (bf16[3,3,3,128,128]{4,3,2,1,0:T(8,128)(2,1)S(1)}, bf16[3,3,3,128,128]{4,3,2,1,0:T(8,128)(2,1)}, u32[]{:S(2)}) copy-start(bf16[3,3,3,128,128]{4,3,2,1,0:T(8,128)(2,1)} %param.19) | copy-start | bytes 2654212
  21.6 4.5 %copy-start.6 = (bf16[1,2,16,64,128]{4,3,2,1,0:T(8,128)(2,1)S(1)}, bf16[1,2,16,64,128]{4,3,2,1,0:T(8,128)(2,1)}, u32[]{:S(2)}) copy-start(bf16[1,2,16,64,128]{4,3,2,1,0:T(8,128)(2,1)} %param.11) | copy-start | bytes 1572868
  26.2 18.1 %copy-start.1 = (f32[72,512]{1,0:T(8,128)S(1)}, f32[72,512]{1,0:T(8,128)}, u32[]{:S(2)}) copy-start(f32[72,512]{1,0:T(8,128)} %get-tuple-element.16.mix) | copy-start | bytes 442372
  26.2 18.1 %copy-start.2 = (f32[8,1024]{1,0:T(8,128)S(1)}, f32[8,1024]{1,0:T(8,128)}, u32[]{:S(2)}) copy-start(f32[8,1024]{1,0:T(8,128)} %get-tuple-element.17.base) | copy-start | bytes 98308
  44.3 17.0 %copy-start.3 = (f32[4,2,64]{2,1,0:T(2,128)S(1)}, f32[4,2,64]{2,1,0:T(2,128)}, u32[]{:S(2)}) copy-start(f32[4,2,64]{2,1,0:T(2,128)} %latent.1) | copy-start | bytes 6148
  44.3 17.0 %copy-start.4 = (f32[4,128]{1,0:T(4,128)S(1)}, f32[4,128]{1,0:T(4,128)}, u32[]{:S(2)}) copy-start(f32[4,128]{1,0:T(4,128)} %get-tuple-element.10.roots) | copy-start | bytes 6148
